TPU v7x, 32 devices: a whole 2x2x4 slice. The times are simulated.
32 devices in a mesh: ctx: 8 (over z, x), head: 4 (over y, core).
Axes of the slice: x: 2, y: 2, z: 4, core: 2. Of those that a mesh axis runs over, the one named last changes fastest.
Arguments:
- queries: bfloat16 [1536, 768], P(('ctx', 'head')), may hold values from -2.5 to 2.5
- keys: bfloat16 [1536, 768], P(('ctx', 'head')), may hold values from -2.5 to 2.5
- values: bfloat16 [1536, 768], P(('ctx', 'head')), may hold values from -6 to 6
- attended: bfloat16 [1536, 768], P(('ctx', 'head')), may hold values from -6 to 6
- grad_out: bfloat16 [1536, 768], P(('ctx', 'head')), may hold values from -6 to 6
- logsumexp: float32 [1536, 12], P('ctx', 'head'), may hold values from 5 to 8
Outputs:
- grad_queries: bfloat16 [1536, 768], P(('ctx', 'head'))
- grad_keys: bfloat16 [1536, 768], P(('ctx', 'head'))
- grad_values: bfloat16 [1536, 768], P(('ctx', 'head'))
All inputs are finite; a program needn't handle non-finite values.
Results may differ from a plain program's by a relative error of at most 0.0051.
Values may be sent and summed in bfloat16 or wider, within the bound.
No kernel may reach another device: no remote copies, remote signals or barrier semaphores. Data moves between devices by JAX's collectives and lax.ppermute only.
A program may use at most 128 MiB of HBM per device.

v0:
```python
import jax
import jax.numpy as jnp
from jax import lax
from jax.sharding import PartitionSpec as P


def block_rows(length):
    for candidate in (2048, 1024, 512):
        if length > candidate and length % candidate == 0:
            return candidate
    return length


def over_blocks(advance, totals, tensors):
    length = tensors[0].shape[0]
    block_size = block_rows(length)
    stacked = tuple(
        (
            matrix.reshape((length // block_size, block_size) + matrix.shape[1:])
            for matrix in tensors
        )
    )

    def single(current, blocks):
        return (advance(current, blocks), None)

    return lax.scan(single, totals, stacked)[0]


def attend(query_part, grad_part, norm_part, delta_part, key_part, value_part, scaling):
    scores = (
        jnp.einsum("ahd,bhd->hab", query_part, key_part, preferred_element_type=jnp.float32)
        * scaling
    )
    weights = jnp.exp(scores - jnp.transpose(norm_part)[:, :, None])
    weights_low = weights.astype(jnp.bfloat16)
    dweights = jnp.einsum("ahd,bhd->hab", grad_part, value_part, preferred_element_type=jnp.float32)
    dscores = (weights * (dweights - jnp.transpose(delta_part)[:, :, None])).astype(jnp.bfloat16)
    return (weights_low, dscores)


def query_term(dscores, key_part, scaling):
    return (
        jnp.einsum("hab,bhd->ahd", dscores, key_part, preferred_element_type=jnp.float32) * scaling
    )


def key_terms(weights_low, dscores, query_part, grad_part, scaling):
    grad_key = (
        jnp.einsum("hab,ahd->bhd", dscores, query_part, preferred_element_type=jnp.float32)
        * scaling
    )
    grad_value = jnp.einsum(
        "hab,ahd->bhd", weights_low, grad_part, preferred_element_type=jnp.float32
    )
    return (grad_key, grad_value)


def local(queries, keys, values, attended, grad_out, logsumexp):
    heads_local = logsumexp.shape[1]
    group_size = lax.axis_size("head")
    width_local = queries.shape[1] // group_size
    head_width = width_local // heads_local
    scaling = head_width ** (-0.5)
    moved = (
        lax.all_to_all(queries, "head", split_axis=1, concat_axis=0, tiled=True),
        lax.all_to_all(keys, "head", split_axis=1, concat_axis=0, tiled=True),
        lax.all_to_all(values, "head", split_axis=1, concat_axis=0, tiled=True),
        lax.all_to_all(grad_out, "head", split_axis=1, concat_axis=0, tiled=True),
        lax.all_to_all(attended, "head", split_axis=1, concat_axis=0, tiled=True),
    )
    length = moved[0].shape[0]

    def split(piece):
        return piece.reshape(piece.shape[0], heads_local, head_width)

    local_q, local_k, local_v, local_g, local_o = [split(matrix) for matrix in moved]
    deltas = jnp.sum(local_g.astype(jnp.float32) * local_o.astype(jnp.float32), axis=2)
    zeros = jnp.zeros((length, heads_local, head_width), jnp.float32)

    def keys_step(grad_query, blocks):
        key_part, value_part = blocks
        dscores = attend(local_q, local_g, logsumexp, deltas, key_part, value_part, scaling)[1]
        return grad_query + query_term(dscores, key_part, scaling)

    def queries_step(totals, blocks):
        query_part, grad_part, norm_part, delta_part = blocks
        weights_low, dscores = attend(
            query_part, grad_part, norm_part, delta_part, local_k, local_v, scaling
        )
        grad_key, grad_value = key_terms(weights_low, dscores, query_part, grad_part, scaling)
        return (totals[0] + grad_key, totals[1] + grad_value)

    all_norms, all_deltas = (
        lax.all_gather(logsumexp, "ctx", axis=0, tiled=True),
        lax.all_gather(deltas, "ctx", axis=0, tiled=True),
    )
    pieces = (
        lax.all_gather(moved[1], "ctx", axis=0, tiled=True),
        lax.all_gather(moved[2], "ctx", axis=0, tiled=True),
    )
    key_piece, value_piece = [split(piece) for piece in pieces]
    grad_query = over_blocks(keys_step, zeros, (key_piece, value_piece))
    pieces = (
        lax.all_gather(moved[0], "ctx", axis=0, tiled=True),
        lax.all_gather(moved[3], "ctx", axis=0, tiled=True),
    )
    query_piece, grad_piece = [split(piece) for piece in pieces]
    grad_key, grad_value = over_blocks(
        queries_step, (zeros, zeros), (query_piece, grad_piece, all_norms, all_deltas)
    )
    query_low = grad_query.reshape(length, width_local).astype(jnp.bfloat16)
    key_low = grad_key.reshape(length, width_local).astype(jnp.bfloat16)
    value_low = grad_value.reshape(length, width_local).astype(jnp.bfloat16)
    grad_queries, grad_keys, grad_values = (
        lax.all_to_all(query_low, "head", split_axis=0, concat_axis=1, tiled=True),
        lax.all_to_all(key_low, "head", split_axis=0, concat_axis=1, tiled=True),
        lax.all_to_all(value_low, "head", split_axis=0, concat_axis=1, tiled=True),
    )
    return (grad_queries, grad_keys, grad_values)


def solution(mesh):
    in_specs = (
        P(("ctx", "head"), None),
        P(("ctx", "head"), None),
        P(("ctx", "head"), None),
        P(("ctx", "head"), None),
        P(("ctx", "head"), None),
        P("ctx", "head"),
    )
    out_specs = (P(("ctx", "head"), None), P(("ctx", "head"), None), P(("ctx", "head"), None))
    return jax.shard_map(local, mesh=mesh, in_specs=in_specs, out_specs=out_specs, check_vma=False)
```

profile of v0, /device:TPU:0, one launch (start us, length us, event | category | flops | bytes accessed | tf_op | source)
XLA Modules:
  0.0 270.9 jit_solution(956941482789978555)
XLA Ops:
  0.7 1.1 all_to_all.102
  2.4 4.2 %all-to-all-start = ((bf16[48,4,192]{2,0,1:T(8,128)(2,1)}), bf16[48,4,192]{2,0,1:T(8,128)(2,1)S(1)}, u32[]{:S(2)}, u32[]{:S(2)}) async-start(bf16[48,4,192]{2,0,1:T(8,128)(2,1)} %copy.93), calls=%async_computation | async-start | bytes 196608 | tf_op jit(solution)/shard_map/all_to_all | solution.py:67
  6.6 1.0 all_to_all.106
  8.3 2.6 all-to-all-done
  10.9 3.3 %all-to-all-start.1 = ((bf16[48,4,192]{2,0,1:T(8,128)(2,1)}), bf16[48,4,192]{2,0,1:T(8,128)(2,1)S(1)}, u32[]{:S(2)}, u32[]{:S(2)}) async-start(bf16[48,4,192]{2,0,1:T(8,128)(2,1)} %copy.95), calls=%async_computation.1 | async-start | bytes 196608 | tf_op jit(solution)/shard_map/all_to_all | solution.py:66
  15.1 3.4 %all-to-all-done.1 = bf16[48,4,192]{2,0,1:T(8,128)(2,1)S(1)} async-done(((bf16[48,4,192]{2,0,1:T(8,128)(2,1)}), bf16[48,4,192]{2,0,1:T(8,128)(2,1)S(1)}, u32[]{:S(2)}, u32[]{:S(2)}) %all-to-all-start.1) | async-done | bytes 73760 | tf_op jit(solution)/shard_map/all_to_all | solution.py:66
  18.5 3.3 %all-to-all-start.2 = ((bf16[48,4,192]{2,0,1:T(8,128)(2,1)}), bf16[48,4,192]{2,0,1:T(8,128)(2,1)S(1)}, u32[]{:S(2)}, u32[]{:S(2)}) async-start(bf16[48,4,192]{2,0,1:T(8,128)(2,1)} %copy.96), calls=%async_computation.2 | async-start | bytes 196608 | tf_op jit(solution)/shard_map/all_to_all | solution.py:68
  23.5 31.2 %all-gather = f32[8,192,3]{1,2,0:T(4,128)S(1)} all-gather(f32[1,192,3]{1,2,0:T(4,128)S(1)} %bitcast.126), channel_id=1, replica_groups=mesh['ctx'=8,'head'=4] {'ctx'}, dimensions={0}, use_global_device_ids=true | all-gather | bytes 20736 | tf_op jit(solution)/shard_map/all_gather | solution.py:95
  55.4 3.3 %all-to-all-start.3 = ((bf16[48,4,192]{2,0,1:T(8,128)(2,1)}), bf16[48,4,192]{2,0,1:T(8,128)(2,1)S(1)}, u32[]{:S(2)}, u32[]{:S(2)}) async-start(bf16[48,4,192]{2,0,1:T(8,128)(2,1)} %copy.98), calls=%async_computation.3 | async-start | bytes 196608 | tf_op jit(solution)/shard_map/all_to_all | solution.py:69
  58.7 32.2 %all_gather.18 = bf16[1536,192]{1,0:T(8,128)(2,1)S(1)} all-gather(bf16[192,192]{1,0:T(8,128)(2,1)S(1)} %bitcast.113), channel_id=1, replica_groups=mesh['ctx'=8,'head'=4] {'ctx'}, dimensions={0}, use_global_device_ids=true | all-gather | bytes 663552 | tf_op jit(solution)/shard_map/all_gather | solution.py:99
  90.9 3.9 %all-to-all-start.4 = ((bf16[48,4,192]{2,0,1:T(8,128)(2,1)}), bf16[48,4,192]{2,0,1:T(8,128)(2,1)}, u32[]{:S(2)}, u32[]{:S(2)}) async-start(bf16[48,4,192]{2,0,1:T(8,128)(2,1)} %copy.99), calls=%async_computation.4 | async-start | bytes 196608 | tf_op jit(solution)/shard_map/all_to_all | solution.py:70
  94.9 33.8 %all_gather.19 = bf16[1536,192]{1,0:T(8,128)(2,1)} all-gather(bf16[192,192]{1,0:T(8,128)(2,1)S(1)} %bitcast.115), channel_id=1, replica_groups=mesh['ctx'=8,'head'=4] {'ctx'}, dimensions={0}, use_global_device_ids=true | all-gather | bytes 663552 | tf_op jit(solution)/shard_map/all_gather | solution.py:100
  129.2 0.8 copy.100
  130.3 2.9 %reshape.83 = bf16[3,512,3,64]{3,2,1,0:T(4,128)(2,1)S(1)} reshape(bf16[1536,192]{1,0:T(8,128)(2,1)} %all_gather.19) | data formatting | bytes 1179648 | tf_op jit(solution)/shard_map/reshape;reshape | solution.py:19
  133.2 0.8 copy.102
  134.1 1.0 reshape.70
  135.2 0.9 convert_bitcast_fusion
  137.2 3.0 %while.24 = (s32[]{:T(128)}, f32[192,3,64]{0,2,1:T(8,128)S(1)}, bf16[3,512,3,64]{1,3,2,0:T(8,128)(2,1)S(1)}, bf16[192,3,64]{0,2,1:T(8,128)(2,1)S(1)}, f32[192,3]...) while((s32[]{:T(128)}, f32[192,3,64]{0,2,1:T(8,128)S(1)}, ...), condition=%wide.region_2.3_spmd.clone, body=%wide.region_1.2_spmd.clone.sunk | while | flops 114831360 | bytes 3499642 | solution.py:27
  140.4 0.8 copy.126
  141.2 3.9 %all-to-all-start.5 = ((bf16[4,48,192]{2,1,0:T(8,128)(2,1)}), bf16[4,48,192]{2,1,0:T(8,128)(2,1)}, u32[]{:S(2)}, u32[]{:S(2)}) async-start(bf16[4,48,192]{2,1,0:T(8,128)(2,1)} %copy.126), calls=%async_computation.5 | async-start | bytes 196608 | tf_op jit(solution)/shard_map/all_to_all | solution.py:116
  145.1 31.9 %all_gather.20 = bf16[1536,192]{1,0:T(8,128)(2,1)S(1)} all-gather(bf16[192,192]{1,0:T(8,128)(2,1)S(1)} %bitcast.118), channel_id=1, replica_groups=mesh['ctx'=8,'head'=4] {'ctx'}, dimensions={0}, use_global_device_ids=true | all-gather | bytes 663552 | tf_op jit(solution)/shard_map/all_gather | solution.py:105
  177.5 0.8 copy.112
  178.6 34.1 %all_gather.22 = bf16[1536,192]{1,0:T(8,128)(2,1)} all-gather(bf16[192,192]{1,0:T(8,128)(2,1)S(1)} %bitcast.120), channel_id=1, replica_groups=mesh['ctx'=8,'head'=4] {'ctx'}, dimensions={0}, use_global_device_ids=true | all-gather | bytes 663552 | tf_op jit(solution)/shard_map/all_gather | solution.py:106
  212.7 2.9 %reshape.86 = bf16[3,512,3,64]{3,2,1,0:T(4,128)(2,1)S(1)} reshape(bf16[1536,192]{1,0:T(8,128)(2,1)} %all_gather.22) | data formatting | bytes 1179648 | tf_op jit(solution)/shard_map/reshape;reshape | solution.py:19
  215.6 0.8 copy.115
  216.8 30.7 %all-gather.1 = f32[8,192,3]{1,2,0:T(4,128)S(1)} all-gather(f32[1,192,3]{1,2,0:T(4,128)S(1)} %copy.110), channel_id=1, replica_groups=mesh['ctx'=8,'head'=4] {'ctx'}, dimensions={0}, use_global_device_ids=true | all-gather | bytes 20736 | tf_op jit(solution)/shard_map/all_gather | solution.py:96
  247.6 6.3 %while.25 = (s32[]{:T(128)}, f32[192,3,64]{0,2,1:T(8,128)S(1)}, f32[192,3,64]{0,2,1:T(8,128)S(1)}, bf16[3,512,3,64]{1,3,2,0:T(8,128)(2,1)S(1)}, bf16[192,3,64]{0...) while((s32[]{:T(128)}, f32[192,3,64]{0,2,1:T(8,128)S(1)}, ...), condition=%wide.region_4.5_spmd.clone, body=%wide.region_3.4_spmd.clone.sunk | while | flops 152948736 | bytes 5277323 | solution.py:27
  254.9 3.4 %all-to-all-start.6 = ((bf16[4,48,192]{2,1,0:T(8,128)(2,1)}), bf16[4,48,192]{2,1,0:T(8,128)(2,1)S(1)}, u32[]{:S(2)}, u32[]{:S(2)}) async-start(bf16[4,48,192]{2,1,0:T(8,128)(2,1)} %copy.131), calls=%async_computation.6 | async-start | bytes 196608 | tf_op jit(solution)/shard_map/all_to_all | solution.py:117
  259.2 3.3 %all-to-all-done.6 = bf16[4,48,192]{2,1,0:T(8,128)(2,1)S(1)} async-done(((bf16[4,48,192]{2,1,0:T(8,128)(2,1)}), bf16[4,48,192]{2,1,0:T(8,128)(2,1)S(1)}, u32[]{:S(2)}, u32[]{:S(2)}) %all-to-all-start.6) | async-done | bytes 73760 | tf_op jit(solution)/shard_map/all_to_all | solution.py:117
  262.5 3.3 %all-to-all-start.7 = ((bf16[4,48,192]{2,1,0:T(8,128)(2,1)}), bf16[4,48,192]{2,1,0:T(8,128)(2,1)S(1)}, u32[]{:S(2)}, u32[]{:S(2)}) async-start(bf16[4,48,192]{2,1,0:T(8,128)(2,1)} %copy.132), calls=%async_computation.7 | async-start | bytes 196608 | tf_op jit(solution)/shard_map/all_to_all | solution.py:118
  265.9 0.9 copy.106
  268.4 1.8 all-to-all-done.7
  (93 shorter events, 21.0 us)
Async XLA Ops:
  0.6 13.6 %copy-start.9 = (bf16[48,768]{1,0:T(8,128)(2,1)S(1)}, bf16[48,768]{1,0:T(8,128)(2,1)}, u32[]{:S(2)}) copy-start(bf16[48,768]{1,0:T(8,128)(2,1)} %param.12) | copy-start | bytes 221188
  0.6 21.2 %copy-start.10 = (bf16[48,768]{1,0:T(8,128)(2,1)S(1)}, bf16[48,768]{1,0:T(8,128)(2,1)}, u32[]{:S(2)}) copy-start(bf16[48,768]{1,0:T(8,128)(2,1)} %param.14) | copy-start | bytes 221188
  0.7 22.0 %copy-start.11 = (bf16[48,768]{1,0:T(8,128)(2,1)S(1)}, bf16[48,768]{1,0:T(8,128)(2,1)}, u32[]{:S(2)}) copy-start(bf16[48,768]{1,0:T(8,128)(2,1)} %param.13) | copy-start | bytes 221188
  0.7 22.8 %copy-start.8 = (f32[192,3]{0,1:T(4,128)S(1)}, f32[192,3]{0,1:T(4,128)}, u32[]{:S(2)}) copy-start(f32[192,3]{0,1:T(4,128)} %param.15) | copy-start | bytes 6916
  2.4 8.5 %all-to-all-start = ((bf16[48,4,192]{2,0,1:T(8,128)(2,1)}), bf16[48,4,192]{2,0,1:T(8,128)(2,1)S(1)}, u32[]{:S(2)}, u32[]{:S(2)}) async-start(bf16[48,4,192]{2,0,1:T(8,128)(2,1)} %copy.93), calls=%async_computation | async-start | bytes 196608 | tf_op jit(solution)/shard_map/all_to_all | solution.py:67
  10.9 7.6 %all-to-all-start.1 = ((bf16[48,4,192]{2,0,1:T(8,128)(2,1)}), bf16[48,4,192]{2,0,1:T(8,128)(2,1)S(1)}, u32[]{:S(2)}, u32[]{:S(2)}) async-start(bf16[48,4,192]{2,0,1:T(8,128)(2,1)} %copy.95), calls=%async_computation.1 | async-start | bytes 196608 | tf_op jit(solution)/shard_map/all_to_all | solution.py:66
  18.5 111.5 %copy-start.2 = (bf16[48,4,192]{2,0,1:T(8,128)(2,1)}, bf16[48,4,192]{2,0,1:T(8,128)(2,1)S(1)}, u32[]{:S(2)}) copy-start(bf16[48,4,192]{2,0,1:T(8,128)(2,1)S(1)} %all-to-all-done.1) | copy-start | bytes 221188
  18.5 36.9 %all-to-all-start.2 = ((bf16[48,4,192]{2,0,1:T(8,128)(2,1)}), bf16[48,4,192]{2,0,1:T(8,128)(2,1)S(1)}, u32[]{:S(2)}, u32[]{:S(2)}) async-start(bf16[48,4,192]{2,0,1:T(8,128)(2,1)} %copy.96), calls=%async_computation.2 | async-start | bytes 196608 | tf_op jit(solution)/shard_map/all_to_all | solution.py:68
  55.4 39.5 %copy-start = (bf16[48,4,192]{2,0,1:T(8,128)(2,1)}, bf16[48,4,192]{2,0,1:T(8,128)(2,1)S(1)}, u32[]{:S(2)}) copy-start(bf16[48,4,192]{2,0,1:T(8,128)(2,1)S(1)} %all-to-all-done.2) | copy-start | bytes 221188
  55.4 35.5 %all-to-all-start.3 = ((bf16[48,4,192]{2,0,1:T(8,128)(2,1)}), bf16[48,4,192]{2,0,1:T(8,128)(2,1)S(1)}, u32[]{:S(2)}, u32[]{:S(2)}) async-start(bf16[48,4,192]{2,0,1:T(8,128)(2,1)} %copy.98), calls=%async_computation.3 | async-start | bytes 196608 | tf_op jit(solution)/shard_map/all_to_all | solution.py:69
  90.9 39.2 %copy-start.4 = (bf16[48,4,192]{2,0,1:T(8,128)(2,1)}, bf16[48,4,192]{2,0,1:T(8,128)(2,1)S(1)}, u32[]{:S(2)}) copy-start(bf16[48,4,192]{2,0,1:T(8,128)(2,1)S(1)} %all-to-all-done.3) | copy-start | bytes 221188
  90.9 44.3 %all-to-all-start.4 = ((bf16[48,4,192]{2,0,1:T(8,128)(2,1)}), bf16[48,4,192]{2,0,1:T(8,128)(2,1)}, u32[]{:S(2)}, u32[]{:S(2)}) async-start(bf16[48,4,192]{2,0,1:T(8,128)(2,1)} %copy.99), calls=%async_computation.4 | async-start | bytes 196608 | tf_op jit(solution)/shard_map/all_to_all | solution.py:70
  136.6 0.6 copy-start.6
  136.7 8.4 %copy-start.3 = (bf16[48,4,192]{2,0,1:T(8,128)(2,1)S(1)}, bf16[48,4,192]{2,0,1:T(8,128)(2,1)}, u32[]{:S(2)}) copy-start(bf16[48,4,192]{2,0,1:T(8,128)(2,1)} %copy-done.2) | copy-start | bytes 221188
  141.2 113.7 %all-to-all-start.5 = ((bf16[4,48,192]{2,1,0:T(8,128)(2,1)}), bf16[4,48,192]{2,1,0:T(8,128)(2,1)}, u32[]{:S(2)}, u32[]{:S(2)}) async-start(bf16[4,48,192]{2,1,0:T(8,128)(2,1)} %copy.126), calls=%async_computation.5 | async-start | bytes 196608 | tf_op jit(solution)/shard_map/all_to_all | solution.py:116
  177.5 1.1 copy-start.5
  215.6 0.9 copy-start.1
  215.6 1.1 copy-start.7
  254.9 7.7 %all-to-all-start.6 = ((bf16[4,48,192]{2,1,0:T(8,128)(2,1)}), bf16[4,48,192]{2,1,0:T(8,128)(2,1)S(1)}, u32[]{:S(2)}, u32[]{:S(2)}) async-start(bf16[4,48,192]{2,1,0:T(8,128)(2,1)} %copy.131), calls=%async_computation.6 | async-start | bytes 196608 | tf_op jit(solution)/shard_map/all_to_all | solution.py:117
  262.5 7.6 %all-to-all-start.7 = ((bf16[4,48,192]{2,1,0:T(8,128)(2,1)}), bf16[4,48,192]{2,1,0:T(8,128)(2,1)S(1)}, u32[]{:S(2)}, u32[]{:S(2)}) async-start(bf16[4,48,192]{2,1,0:T(8,128)(2,1)} %copy.132), calls=%async_computation.7 | async-start | bytes 196608 | tf_op jit(solution)/shard_map/all_to_all | solution.py:118
where the time goes:
time: 272 us; the launch traced here: 271 us
  blocking collectives  194 us (71%)
  starting transfers between devices  28.7 us (11%)
  local copies, waits for them, and re-layouts  27.9 us (10%)
  waiting for transfers between devices  11.2 us (4%)
  matrix products  6.71 us (2%)
    all_gather x1, blocking collectives, local(): lax.all_gather(moved[3], 'ctx', axis=0, tiled=True)  34.1 us
    all_gather x1, blocking collectives, local(): lax.all_gather(moved[2], 'ctx', axis=0, tiled=True)  33.8 us
    all_gather x1, blocking collectives, local(): lax.all_gather(moved[1], 'ctx', axis=0, tiled=True)  32.2 us
    all_gather x1, blocking collectives, local(): lax.all_gather(moved[0], 'ctx', axis=0, tiled=True)  31.9 us
    all_gather x1, blocking collectives, local(): lax.all_gather(logsumexp, 'ctx', axis=0, tiled=True)  31.2 us
    all_gather x1, blocking collectives, local(): lax.all_gather(deltas, 'ctx', axis=0, tiled=True)  30.7 us
    another operation x4, local copies, waits for them, and re-layouts, over_blocks(): matrix.reshape((length // block_size, block_size) + matrix.shape[1:])  6.74 us
  transfers between devices with their start and end apart: 8, of which 4 were waited for; matrix products, arithmetic and copies ran while one was open for 9% of the time, Pallas kernels for 0%

commit v1 on v0

v1 whole, which is shorter than its diff:
```python
import functools
import jax
import jax.numpy as jnp
from jax import lax
from jax.experimental import pallas as pl
from jax.experimental.pallas import tpu as pltpu
from jax.sharding import PartitionSpec as P

F32 = jnp.float32
BF16 = jnp.bfloat16
LANES = 128
NT = (((1,), (1,)), ((), ()))
TN = (((0,), (0,)), ((), ()))
NN = (((1,), (0,)), ((), ()))
VMEM = pl.BlockSpec(memory_space=pltpu.VMEM)


def dot(a, b, dims):
    return lax.dot_general(a, b, dims, preferred_element_type=F32)


def round_up(n, m):
    return -(-n // m) * m


class Sizes:
    def __init__(self, rows, width, heads_group, group, ctx):
        self.rows, self.width = rows, width
        self.group, self.ctx = group, ctx
        self.heads_group = heads_group
        self.heads = heads_group * group
        self.dim = width // self.heads
        self.tiles = width // LANES
        self.span = rows * group
        self.span_tiles = -(-self.span // LANES)
        self.part = self.tiles * rows
        self.lse_rows = 3 * heads_group * self.span_tiles
        self.extra = round_up(self.lse_rows + 2 * self.heads, 16)
        self.high = ctx // 2


def split3(x):
    hi = x.astype(BF16).astype(F32)
    rest = x - hi
    mid = rest.astype(BF16).astype(F32)
    return hi, mid, rest - mid


def pack_kernel(s, q_ref, k_ref, v_ref, o_ref, g_ref, lse_ref, qg_ref, kv_ref, wide, small):
    r = s.rows
    for t in range(s.tiles):
        lanes = slice(t * LANES, (t + 1) * LANES)
        rows = slice(t * r, (t + 1) * r)
        more = slice(s.part + t * r, s.part + (t + 1) * r)
        qg_ref[rows, :] = q_ref[:, lanes]
        qg_ref[more, :] = g_ref[:, lanes]
        kv_ref[rows, :] = k_ref[:, lanes]
        kv_ref[more, :] = v_ref[:, lanes]
    prod = g_ref[...].astype(F32) * o_ref[...].astype(F32)
    hi = prod.astype(BF16)
    lo = (prod - hi.astype(F32)).astype(BF16)
    shape = (round_up(s.heads, 16), s.width)
    pick = lax.broadcasted_iota(jnp.int32, shape, 1) // s.dim
    pick = (pick == lax.broadcasted_iota(jnp.int32, shape, 0)).astype(F32).astype(BF16)
    delta = dot(pick, hi, NT) + dot(pick, lo, NT)
    d_hi, d_mid, _ = split3(delta)
    wide[...] = jnp.zeros(wide.shape, F32)
    wide[: s.span, : s.heads_group] = lse_ref[...]
    lse = wide[...].T[:8]
    small[...] = jnp.zeros(small.shape, F32)
    at = 0
    for t in range(s.span_tiles):
        for piece in split3(lse[:, t * LANES : (t + 1) * LANES]):
            small[at : at + s.heads_group, :] = piece[: s.heads_group]
            at += s.heads_group
    small[at : at + s.heads, : s.rows] = d_hi[: s.heads]
    small[at + s.heads : at + 2 * s.heads, : s.rows] = d_mid[: s.heads]
    qg_ref[2 * s.part :, :] = small[...].astype(BF16)


def pack(s, q, k, v, o, g, lse):
    return pl.pallas_call(
        functools.partial(pack_kernel, s),
        out_shape=(
            jax.ShapeDtypeStruct((2 * s.part + s.extra, LANES), BF16),
            jax.ShapeDtypeStruct((2 * s.part, LANES), BF16),
        ),
        in_specs=[VMEM] * 6,
        out_specs=[VMEM] * 2,
        scratch_shapes=[
            pltpu.VMEM((round_up(s.span, LANES), LANES), F32),
            pltpu.VMEM((s.extra, LANES), F32),
        ],
    )(q, k, v, o, g, lse)


def attend_kernel(s, blocks, first, *refs):
    r, n = s.rows, s.group
    refs = list(refs)
    take = lambda count: [refs.pop(0) for _ in range(count)]
    qg, kv = take(n), take(blocks)
    (old,) = take(1) if not first else (None,)
    keep, (send,) = take(n // 2), take(1)
    sums = take(1 if first else blocks)
    qs, gs, dqs, norms, deltas = refs
    me = lax.axis_index("head")
    scale = s.dim**-0.5
    wide = s.span_tiles * LANES
    h = s.heads_group
    total = jnp.zeros((s.heads, wide), F32)
    for off in range(n):
        who = lax.bitwise_xor(me, off)
        at = pl.multiple_of(who * r, 16)
        for t in range(s.tiles):
            q = qg[off][t * r : (t + 1) * r, :]
            qs[t, pl.ds(at, r), :] = (q.astype(F32) * scale).astype(BF16)
            gs[t, pl.ds(at, r), :] = qg[off][s.part + t * r : s.part + (t + 1) * r, :]
        small = qg[off][2 * s.part :, :].astype(F32)
        pieces = []
        for t in range(s.span_tiles):
            b = 3 * h * t
            pieces.append(small[b : b + h] + small[b + h : b + 2 * h] + small[b + 2 * h : b + 3 * h])
        norms[who, :h, :] = jnp.concatenate(pieces, axis=1)
        b = s.lse_rows
        delta = small[b : b + s.heads] + small[b + s.heads : b + 2 * s.heads]
        if wide > LANES:
            delta = jnp.concatenate([delta, jnp.zeros((s.heads, wide - LANES), F32)], axis=1)
        total = total + pltpu.roll(delta, who * r, 1)
    deltas[...] = total
    half = lax.broadcasted_iota(jnp.int32, (blocks * r, LANES), 1) < s.dim
    zero = jnp.zeros((), BF16)
    for t in range(s.tiles):
        rows = slice(t * r, (t + 1) * r)
        more = slice(s.part + t * r, s.part + (t + 1) * r)
        k = jnp.concatenate([ref[rows, :] for ref in kv], axis=0)
        v = jnp.concatenate([ref[more, :] for ref in kv], axis=0)
        q, g = qs[t], gs[t]
        dk, dv, dq = [], [], None
        for e in range(2):
            head = 2 * t + e
            mask = half if e == 0 else jnp.logical_not(half)
            k_one = jnp.where(mask, k, zero)
            v_one = jnp.where(mask, v, zero)
            j = head % h
            norm = norms[head // h, j : j + 1, : s.span]
            weights = jnp.exp(dot(k_one, q, NT) - norm)
            dweights = dot(v_one, g, NT)
            dscores = (weights * (dweights - deltas[head : head + 1, : s.span])).astype(BF16)
            dv.append(dot(weights.astype(BF16), g, NN))
            dk.append(dot(dscores, q, NN))
            term = dot(dscores, k_one, TN)
            dq = term if dq is None else dq + term
        dqs[t] = dq * scale
        for where, pair in ((rows, dk), (more, dv)):
            both = jnp.where(half, pair[0], pair[1])
            for i in range(blocks):
                piece = both[i * r : (i + 1) * r]
                if first:
                    sums[0][2 * s.part * i + where.start : 2 * s.part * i + where.stop, :] = piece
                else:
                    piece = piece + old[2 * s.part * i + where.start : 2 * s.part * i + where.stop, :]
                    sums[i][where, :] = piece.astype(sums[i].dtype)
    for off in range(n):
        at = pl.multiple_of(lax.bitwise_xor(me, off) * r, 16)
        for t in range(s.tiles):
            piece = dqs[t, pl.ds(at, r), :]
            i = off // 2
            if off % 2 == 0:
                keep[i][t * r : (t + 1) * r, :] = piece
            else:
                send[i * s.part + t * r : i * s.part + (t + 1) * r, :] = piece.astype(BF16)


def attend(s, qg, kv, old):
    blocks = len(kv)
    first = old is None
    out = [jax.ShapeDtypeStruct((s.part, LANES), F32)] * (s.group // 2)
    out.append(jax.ShapeDtypeStruct((s.group // 2 * s.part, LANES), BF16))
    if first:
        out.append(jax.ShapeDtypeStruct((blocks * 2 * s.part, LANES), F32))
    else:
        out.append(jax.ShapeDtypeStruct((2 * s.part, LANES), F32))
        out += [jax.ShapeDtypeStruct((2 * s.part, LANES), BF16)] * (blocks - 1)
    operands = list(qg) + list(kv) + ([] if first else [old])
    pairs = s.heads * s.span * blocks * s.rows
    result = pl.pallas_call(
        functools.partial(attend_kernel, s, blocks, first),
        out_shape=out,
        in_specs=[VMEM] * len(operands),
        out_specs=[VMEM] * len(out),
        scratch_shapes=[
            pltpu.VMEM((s.tiles, s.span, LANES), BF16),
            pltpu.VMEM((s.tiles, s.span, LANES), BF16),
            pltpu.VMEM((s.tiles, s.span, LANES), F32),
            pltpu.VMEM((s.group, 8, s.span_tiles * LANES), F32),
            pltpu.VMEM((s.heads, s.span_tiles * LANES), F32),
        ],
        compiler_params=pltpu.CompilerParams(vmem_limit_bytes=48 * 2**20),
        cost_estimate=pl.CostEstimate(
            flops=20 * pairs * s.dim, bytes_accessed=4 * s.part * LANES * 8, transcendentals=pairs
        ),
    )(*operands)
    count = s.group // 2
    return result[:count], result[count], result[count + 1 :]


def core_kernel(s, keep_own, *refs):
    count = s.group // 2
    recv = refs[count]
    for i in range(count):
        total = refs[i][...] + recv[i * s.part : (i + 1) * s.part, :].astype(F32)
        refs[count + 1 + i][...] = total.astype(refs[count + 1 + i].dtype)


def core_add(s, keep, recv, keep_own):
    count = len(keep)
    out = [
        jax.ShapeDtypeStruct((s.part, LANES), F32 if keep_own and i == 0 else BF16)
        for i in range(count)
    ]
    return pl.pallas_call(
        functools.partial(core_kernel, s, keep_own),
        out_shape=out,
        in_specs=[VMEM] * (count + 1),
        out_specs=[VMEM] * count,
    )(*keep, recv)


def final_kernel(s, n_dq, n_kv, *refs):
    dq, kv = refs[:n_dq], refs[n_dq : n_dq + n_kv]
    outs = refs[n_dq + n_kv :]
    r = s.rows
    for out, sources, base in ((outs[0], dq, 0), (outs[1], kv, 0), (outs[2], kv, s.part)):
        for t in range(s.tiles):
            rows = slice(base + t * r, base + (t + 1) * r)
            total = sources[0][rows, :].astype(F32)
            for ref in sources[1:]:
                total = total + ref[rows, :].astype(F32)
            out[:, t * LANES : (t + 1) * LANES] = total.astype(BF16)


def finish(s, dq, kv):
    return pl.pallas_call(
        functools.partial(final_kernel, s, len(dq), len(kv)),
        out_shape=[jax.ShapeDtypeStruct((s.rows, s.width), BF16)] * 3,
        in_specs=[VMEM] * (len(dq) + len(kv)),
        out_specs=[VMEM] * 3,
    )(*dq, *kv)


def local(queries, keys, values, attended, grad_out, logsumexp):
    group, ctx = lax.axis_size("head"), lax.axis_size("ctx")
    s = Sizes(queries.shape[0], queries.shape[1], logsumexp.shape[1], group, ctx)

    def move(x, ctx_off, head_off):
        if ctx_off == 0:
            return lax.ppermute(x, "head", [(i, i ^ head_off) for i in range(group)])
        if head_off == 0:
            return lax.ppermute(x, "ctx", [(i, i ^ ctx_off) for i in range(ctx)])
        pairs = [
            (i * group + j, (i ^ ctx_off) * group + (j ^ head_off))
            for i in range(ctx)
            for j in range(group)
        ]
        return lax.ppermute(x, ("ctx", "head"), pairs)

    qg_own, kv_own = pack(s, queries, keys, values, attended, grad_out, logsumexp)
    far = {0: move(qg_own, s.high, 0)}
    kv = {0: kv_own}
    bit = s.high // 2
    while bit:
        for off in sorted(kv):
            kv[off + bit] = move(kv[off], bit, 0)
        bit //= 2
    near = {0: qg_own}
    bit = group // 2
    while bit:
        for blocks in (near, far):
            for off in sorted(blocks):
                blocks[off + bit] = move(blocks[off], 0, bit)
        bit //= 2
    kv = [kv[off] for off in range(s.high)]
    keep0, send0, sums0 = attend(s, [near[i] for i in range(group)], kv, None)
    keep1, send1, sums1 = attend(s, [far[i] for i in range(group)], kv, sums0[0])
    dq = core_add(s, keep0, move(send0, 0, 1), True)
    total_q = [dq[0]] + [move(dq[i], 0, 2 * i) for i in range(1, group // 2)]
    dq = core_add(s, keep1, move(send1, 0, 1), False)
    total_q += [move(dq[i], s.high, 2 * i) for i in range(group // 2)]
    total_kv = [sums1[0]] + [move(sums1[off], off, 0) for off in range(1, s.high)]
    return tuple(finish(s, total_q, total_kv))


def solution(mesh):
    rows = P(("ctx", "head"), None)
    return jax.shard_map(
        local,
        mesh=mesh,
        in_specs=(rows, rows, rows, rows, rows, P("ctx", "head")),
        out_specs=(rows, rows, rows),
        check_vma=False,
    )
```

time: 272 us -> 59.2 us (0.22)
  blocking collectives: 194 us -> 0 us
  local copies, waits for them, and re-layouts: 27.9 us -> 7.24 us
  Pallas kernels: 0 us -> 13.2 us
  starting transfers between devices: 28.7 us -> 20.2 us
  matrix products: 6.71 us -> 0 us
  waiting for transfers between devices: 11.2 us -> 17.5 us
    all_gather x6 -> x0, blocking collectives: 194 us -> none  [the longest x1 34.1 us: local(): lax.all_gather(moved[3], 'ctx', axis=0, tiled=True)]
    all_to_all x8 -> x0, starting transfers between devices: 28.7 us -> none  [the longest x1 4.24 us: local(): lax.all_to_all(keys, 'head', split_axis=1, concat_axis=0, tiled=True)]
    ppermute x0 -> x18, starting transfers between devices: none -> 20.2 us  [the longest x8 13.5 us: move(): return lax.ppermute(x, 'ctx', [(i, i ^ ctx_off) for i in range(ctx)])]
    ppermute x0 -> x18, waiting for transfers between devices: none -> 17.5 us  [the longest x8 12.5 us: move(): return lax.ppermute(x, 'ctx', [(i, i ^ ctx_off) for i in range(ctx)])]
    pallas_call x0 -> x6, Pallas kernels: none -> 13.2 us  [the longest x2 5.78 us: attend(): pl.pallas_call(functools.partial(attend_kernel, s, blocks, first), out_sh...]
    all_to_all x8 -> x0, waiting for transfers between devices: 11.2 us -> none  [the longest x1 3.44 us: local(): lax.all_to_all(queries, 'head', split_axis=1, concat_axis=0, tiled=True)]
    all_to_all x16 -> x0, local copies, waits for them, and re-layouts: 9.11 us -> none  [the longest x2 1.73 us: local(): lax.all_to_all(keys, 'head', split_axis=1, concat_axis=0, tiled=True)]
    another operation x4 -> x0, local copies, waits for them, and re-layouts: 6.74 us -> none  [over_blocks(): matrix.reshape((length // block_size, block_size) + matrix.shape[1:])]
  transfers between devices with their start and end apart: 8 -> 18, of which waited for: 4 -> 6; matrix products, arithmetic and copies ran while one was open for 9% -> 0% of each run, Pallas kernels for 0% -> 16%
where the time goes in v1:
time: 59.2 us; the launch traced here: 58.9 us
  starting transfers between devices  20.2 us (34%)
  waiting for transfers between devices  17.5 us (30%)
  Pallas kernels  13.2 us (22%)
  local copies, waits for them, and re-layouts  7.24 us (12%)
  between operations  0.78 us (1%)
    ppermute x8, starting transfers between devices, move(): return lax.ppermute(x, 'ctx', [(i, i ^ ctx_off) for i in range(ctx)])  13.5 us
    ppermute x8, waiting for transfers between devices, move(): return lax.ppermute(x, 'ctx', [(i, i ^ ctx_off) for i in range(ctx)])  12.5 us
    unnamed x33, local copies, waits for them, and re-layouts  7.24 us
    pallas_call x2, Pallas kernels, attend(): pl.pallas_call(functools.partial(attend_kernel, s, blocks, first), out_sh...  5.78 us
    ppermute x9, starting transfers between devices, move(): return lax.ppermute(x, 'head', [(i, i ^ head_off) for i in range(group)])  5.12 us
    ppermute x1, waiting for transfers between devices, move(): return lax.ppermute(x, ('ctx', 'head'), pairs)  4.99 us
    pallas_call x2, Pallas kernels, core_add(): pl.pallas_call(functools.partial(core_kernel, s, keep_own), out_shape=out...  3.47 us
    pallas_call x1, Pallas kernels, finish(): pl.pallas_call(functools.partial(final_kernel, s, len(dq), len(kv)), out_...  2.03 us
  transfers between devices with their start and end apart: 18, of which 6 were waited for; matrix products, arithmetic and copies ran while one was open for 0% of the time, Pallas kernels for 16%

profile of v1, /device:TPU:0, one launch (start us, length us, event | category | flops | bytes accessed | tf_op | source)
XLA Modules:
  0.0 58.9 jit_solution(15504949904913874161)
XLA Ops:
  0.6 1.5 %copy.9.lse_ref = f32[192,3]{1,0:T(8,128)} copy(f32[192,3]{0,1:T(4,128)} %param.11) | data formatting | bytes 4608 | tf_op args[5]
  2.1 1.9 %shard_map.85 = (bf16[624,128]{1,0:T(8,128)(2,1)}, bf16[576,128]{1,0:T(8,128)(2,1)}) custom-call(bf16[48,768]{1,0:T(8,128)(2,1)} %q_ref.1, bf16[48,768]{1,0:T(8,128)(2,1)} %k_ref.1, bf16[48,768]{1,0:T(8,128)(2,1)} %v_ref.1, bf16[48,768]{1,0:T(8,128)(2,1)} %o_ref.1, bf16[48,768]{1,0:T(8,128)(2,1)} %g_ref.1, f32[192,3]{1,0:T(8,128)} %copy.9.lse_ref), custom_call_target="tpu_custom_call" | custom-call | tf_op jit(solution)/shard_map/pallas_call | solution.py:82
  4.0 4.0 %collective-permute-start.8 = (bf16[624,128]{1,0:T(8,128)(2,1)}, bf16[624,128]{1,0:T(8,128)(2,1)S(1)}, u32[]{:S(2)}, u32[]{:S(2)}) collective-permute-start(bf16[624,128]{1,0:T(8,128)(2,1)} %get-tuple-element.20.refs_0_), channel_id=1, source_target_pairs={{0,16},{4,20},{8,24},{12,28},{16,0},{20,4},{24,8},{28,12},{1,17},{... | collective-permute-start | bytes 479240 | tf_op jit(solution)/shard_map/ppermute | solution.py:259
  8.0 1.5 %collective-permute-start.1 = (bf16[624,128]{1,0:T(8,128)(2,1)}, bf16[624,128]{1,0:T(8,128)(2,1)S(1)}, u32[]{:S(2)}, u32[]{:S(2)}) collective-permute-start(bf16[624,128]{1,0:T(8,128)(2,1)} %get-tuple-element.20.refs_0_), channel_id=1, source_target_pairs={{0,2},{1,3},{2,0},{3,1},{4,6},{5,7},{6,4},{7,5},{8,10},{9,11},{10,... | collective-permute-start | bytes 479240 | tf_op jit(solution)/shard_map/ppermute | solution.py:257
  9.6 1.6 %collective-permute-start.4 = (bf16[576,128]{1,0:T(8,128)(2,1)}, bf16[576,128]{1,0:T(8,128)(2,1)S(1)}, u32[]{:S(2)}, u32[]{:S(2)}) collective-permute-start(bf16[576,128]{1,0:T(8,128)(2,1)} %get-tuple-element.21.refs_4_), channel_id=1, source_target_pairs={{0,8},{4,12},{8,0},{12,4},{16,24},{20,28},{24,16},{28,20},{1,9},{5... | collective-permute-start | bytes 442376 | tf_op jit(solution)/shard_map/ppermute | solution.py:259
  11.1 4.8 %collective-permute-done.8.refs_0_ = bf16[624,128]{1,0:T(8,128)(2,1)S(1)} collective-permute-done((bf16[624,128]{1,0:T(8,128)(2,1)}, bf16[624,128]{1,0:T(8,128)(2,1)S(1)}, u32[]{:S(2)}, u32[]{:S(2)}) %collective-permute-start.8) | collective-permute-done | bytes 159776 | tf_op jit(solution)/shard_map/ppermute | solution.py:259
  15.9 1.6 %collective-permute-start.10 = (bf16[624,128]{1,0:T(8,128)(2,1)S(1)}, bf16[624,128]{1,0:T(8,128)(2,1)S(1)}, u32[]{:S(2)}, u32[]{:S(2)}) collective-permute-start(bf16[624,128]{1,0:T(8,128)(2,1)S(1)} %collective-permute-done.8.refs_0_), channel_id=1, source_target_pairs={{0,2},{1,3},{2,0},{3,1},{4,6},{5,7},{6,4},{7,5},{8,10},{9,11},{10,... | collective-permute-start | bytes 479240 | tf_op jit(solution)/shard_map/ppermute | solution.py:257
  17.5 1.5 %collective-permute-start.3 = (bf16[576,128]{1,0:T(8,128)(2,1)}, bf16[576,128]{1,0:T(8,128)(2,1)S(1)}, u32[]{:S(2)}, u32[]{:S(2)}) collective-permute-start(bf16[576,128]{1,0:T(8,128)(2,1)} %get-tuple-element.21.refs_4_), channel_id=1, source_target_pairs={{0,4},{4,0},{8,12},{12,8},{16,20},{20,16},{24,28},{28,24},{1,5},{5... | collective-permute-start | bytes 442376 | tf_op jit(solution)/shard_map/ppermute | solution.py:259
  19.5 0.5 collective-permute-start.5
  20.0 3.5 %collective-permute-done.3.refs_5_ = bf16[576,128]{1,0:T(8,128)(2,1)S(1)} collective-permute-done((bf16[576,128]{1,0:T(8,128)(2,1)}, bf16[576,128]{1,0:T(8,128)(2,1)S(1)}, u32[]{:S(2)}, u32[]{:S(2)}) %collective-permute-start.3) | collective-permute-done | bytes 147488 | tf_op jit(solution)/shard_map/ppermute | solution.py:259
  24.0 1.9 %collective-permute-done.5.refs_7_ = bf16[576,128]{1,0:T(8,128)(2,1)S(1)} collective-permute-done((bf16[576,128]{1,0:T(8,128)(2,1)S(1)}, bf16[576,128]{1,0:T(8,128)(2,1)S(1)}, u32[]{:S(2)}, u32[]{:S(2)}) %collective-permute-start.5) | collective-permute-done | bytes 147488 | tf_op jit(solution)/shard_map/ppermute | solution.py:259
  26.0 0.9 %copy-done.1 = bf16[576,128]{1,0:T(8,128)(2,1)S(1)} copy-done((bf16[576,128]{1,0:T(8,128)(2,1)S(1)}, bf16[576,128]{1,0:T(8,128)(2,1)}, u32[]{:S(2)}) %copy-start.1) | copy-done | bytes 147480
  26.9 0.9 %copy-done.7 = bf16[624,128]{1,0:T(8,128)(2,1)S(1)} copy-done((bf16[624,128]{1,0:T(8,128)(2,1)S(1)}, bf16[624,128]{1,0:T(8,128)(2,1)}, u32[]{:S(2)}) %copy-start.7) | copy-done | bytes 159768
  27.8 2.9 %shard_map.86 = (f32[288,128]{1,0:T(8,128)S(1)}, f32[288,128]{1,0:T(8,128)S(1)}, bf16[576,128]{1,0:T(8,128)(2,1)S(1)}, f32[2304,128]{1,0:T(8,128)S(1)}) custom-call(bf16[624,128]{1,0:T(8,128)(2,1)S(1)} %copy-done.7, bf16[624,128]{1,0:T(8,128)(2,1)S(1)} %collective-permute-done.refs_1_, bf16[624,128]{1,0:T(8,128)(2,1)S(1)} %collective-permute-done.1.refs_2_, ...), custom_call_target="tpu_custom_call" | custom-call | flops 566231040 | bytes 1179648 | tf_op jit(solution)/shard_map/pallas_call | solution.py:186
  30.8 2.9 %shard_map.88 = (f32[288,128]{1,0:T(8,128)S(1)}, f32[288,128]{1,0:T(8,128)S(1)}, bf16[576,128]{1,0:T(8,128)(2,1)S(1)}, f32[576,128]{1,0:T(8,128)S(1)}, bf16[576,...) custom-call(bf16[624,128]{1,0:T(8,128)(2,1)S(1)} %collective-permute-done.8.refs_0_, ...), custom_call_target="tpu_custom_call" | custom-call | flops 566231040 | bytes 1179648 | tf_op jit(solution)/shard_map/pallas_call | solution.py:186
  33.8 0.7 %copy-done = f32[576,128]{1,0:T(8,128)} copy-done((f32[576,128]{1,0:T(8,128)}, f32[576,128]{1,0:T(8,128)S(1)}, u32[]{:S(2)}) %copy-start) | copy-done | bytes 294936
  34.5 0.7 %copy-done.3 = f32[288,128]{1,0:T(8,128)} copy-done((f32[288,128]{1,0:T(8,128)}, f32[288,128]{1,0:T(8,128)S(1)}, u32[]{:S(2)}) %copy-start.3) | copy-done | bytes 147480
  35.2 0.6 %copy-done.4 = f32[288,128]{1,0:T(8,128)} copy-done((f32[288,128]{1,0:T(8,128)}, f32[288,128]{1,0:T(8,128)S(1)}, u32[]{:S(2)}) %copy-start.4) | copy-done | bytes 147480
  36.3 0.7 %copy-done.11 = bf16[576,128]{1,0:T(8,128)(2,1)} copy-done((bf16[576,128]{1,0:T(8,128)(2,1)}, bf16[576,128]{1,0:T(8,128)(2,1)S(1)}, u32[]{:S(2)}) %copy-start.11) | copy-done | bytes 147480
  36.9 1.7 %shard_map.87 = (f32[288,128]{1,0:T(8,128)}, bf16[288,128]{1,0:T(8,128)(2,1)}) custom-call(f32[288,128]{1,0:T(8,128)} %copy-done.5, f32[288,128]{1,0:T(8,128)} %copy-done.6, bf16[576,128]{1,0:T(8,128)(2,1)} %copy-done.11), custom_call_target="tpu_custom_call" | custom-call | tf_op jit(solution)/shard_map/pallas_call | solution.py:221
  39.2 1.4 %collective-permute-start.15 = (bf16[576,128]{1,0:T(8,128)(2,1)S(1)}, bf16[576,128]{1,0:T(8,128)(2,1)S(1)}, u32[]{:S(2)}, u32[]{:S(2)}) collective-permute-start(bf16[576,128]{1,0:T(8,128)(2,1)S(1)} %get-tuple-element.34), channel_id=1, source_target_pairs={{0,4},{4,0},{8,12},{12,8},{16,20},{20,16},{24,28},{28,24},{1,5},{5... | collective-permute-start | bytes 442376 | tf_op jit(solution)/shard_map/ppermute | solution.py:259
  40.6 1.2 %collective-permute-start.16 = (bf16[576,128]{1,0:T(8,128)(2,1)S(1)}, bf16[576,128]{1,0:T(8,128)(2,1)S(1)}, u32[]{:S(2)}, u32[]{:S(2)}) collective-permute-start(bf16[576,128]{1,0:T(8,128)(2,1)S(1)} %get-tuple-element.35), channel_id=1, source_target_pairs={{0,8},{4,12},{8,0},{12,4},{16,24},{20,28},{24,16},{28,20},{1,9},{5... | collective-permute-start | bytes 442376 | tf_op jit(solution)/shard_map/ppermute | solution.py:259
  41.8 0.9 %collective-permute-start.17 = (bf16[576,128]{1,0:T(8,128)(2,1)S(1)}, bf16[576,128]{1,0:T(8,128)(2,1)S(1)}, u32[]{:S(2)}, u32[]{:S(2)}) collective-permute-start(bf16[576,128]{1,0:T(8,128)(2,1)S(1)} %get-tuple-element.36), channel_id=1, source_target_pairs={{0,12},{4,8},{8,4},{12,0},{16,28},{20,24},{24,20},{28,16},{1,13},{... | collective-permute-start | bytes 442376 | tf_op jit(solution)/shard_map/ppermute | solution.py:259
  42.6 0.7 %copy-done.12 = bf16[576,128]{1,0:T(8,128)(2,1)} copy-done((bf16[576,128]{1,0:T(8,128)(2,1)}, bf16[576,128]{1,0:T(8,128)(2,1)S(1)}, u32[]{:S(2)}) %copy-start.12) | copy-done | bytes 147480
  43.3 1.7 %shard_map.89 = (bf16[288,128]{1,0:T(8,128)(2,1)}, bf16[288,128]{1,0:T(8,128)(2,1)}) custom-call(f32[288,128]{1,0:T(8,128)} %copy-done.3, f32[288,128]{1,0:T(8,128)} %copy-done.4, bf16[576,128]{1,0:T(8,128)(2,1)} %copy-done.12), custom_call_target="tpu_custom_call" | custom-call | tf_op jit(solution)/shard_map/pallas_call | solution.py:221
  45.0 2.4 %collective-permute-start.13 = (bf16[288,128]{1,0:T(8,128)(2,1)}, bf16[288,128]{1,0:T(8,128)(2,1)S(1)}, u32[]{:S(2)}, u32[]{:S(2)}) collective-permute-start(bf16[288,128]{1,0:T(8,128)(2,1)} %get-tuple-element.31), channel_id=1, source_target_pairs={{0,16},{4,20},{8,24},{12,28},{16,0},{20,4},{24,8},{28,12},{1,17},{... | collective-permute-start | bytes 221192 | tf_op jit(solution)/shard_map/ppermute | solution.py:259
  47.4 1.5 %collective-permute-start.14 = (bf16[288,128]{1,0:T(8,128)(2,1)}, bf16[288,128]{1,0:T(8,128)(2,1)S(1)}, u32[]{:S(2)}, u32[]{:S(2)}) collective-permute-start(bf16[288,128]{1,0:T(8,128)(2,1)} %get-tuple-element.32), channel_id=1, source_target_pairs={{0,18},{1,19},{2,16},{3,17},{4,22},{5,23},{6,20},{7,21},{8,26},{9,... | collective-permute-start | bytes 221192 | tf_op jit(solution)/shard_map/ppermute | solution.py:265
  49.0 0.8 %collective-permute-done.17.refs_7_ = bf16[576,128]{1,0:T(8,128)(2,1)S(1)} collective-permute-done((bf16[576,128]{1,0:T(8,128)(2,1)S(1)}, bf16[576,128]{1,0:T(8,128)(2,1)S(1)}, u32[]{:S(2)}, u32[]{:S(2)}) %collective-permute-start.17) | collective-permute-done | bytes 147488 | tf_op jit(solution)/shard_map/ppermute | solution.py:259
  49.8 1.4 %collective-permute-done.13.refs_2_ = bf16[288,128]{1,0:T(8,128)(2,1)S(1)} collective-permute-done((bf16[288,128]{1,0:T(8,128)(2,1)}, bf16[288,128]{1,0:T(8,128)(2,1)S(1)}, u32[]{:S(2)}, u32[]{:S(2)}) %collective-permute-start.13) | collective-permute-done | bytes 73760 | tf_op jit(solution)/shard_map/ppermute | solution.py:259
  51.2 5.0 %collective-permute-done.14.refs_3_ = bf16[288,128]{1,0:T(8,128)(2,1)S(1)} collective-permute-done((bf16[288,128]{1,0:T(8,128)(2,1)}, bf16[288,128]{1,0:T(8,128)(2,1)S(1)}, u32[]{:S(2)}, u32[]{:S(2)}) %collective-permute-start.14) | collective-permute-done | bytes 73760 | tf_op jit(solution)/shard_map/ppermute | solution.py:265
  56.3 0.6 copy-done.15
  56.8 2.0 %shard_map.90 = (bf16[48,768]{1,0:T(8,128)(2,1)}, bf16[48,768]{1,0:T(8,128)(2,1)}, bf16[48,768]{1,0:T(8,128)(2,1)}) custom-call(f32[288,128]{1,0:T(8,128)} %get-tuple-element.25.refs_0_, bf16[288,128]{1,0:T(8,128)(2,1)} %copy-done.13, bf16[288,128]{1,0:T(8,128)(2,1)} %copy-done.14, bf16[288,128]{1,0:T(8,128)(2,1)} %copy-done.15, f32[576,128]{1,0:T(8,128)} %copy-done, ...), custom_call_target="tpu_custom_call" | custom-call | tf_op jit(solution)/shard_map/pallas_call | solution.py:243
  (43 shorter events, 2.1 us)
Async XLA Ops:
  4.0 11.9 %collective-permute-start.8 = (bf16[624,128]{1,0:T(8,128)(2,1)}, bf16[624,128]{1,0:T(8,128)(2,1)S(1)}, u32[]{:S(2)}, u32[]{:S(2)}) collective-permute-start(bf16[624,128]{1,0:T(8,128)(2,1)} %get-tuple-element.20.refs_0_), channel_id=1, source_target_pairs={{0,16},{4,20},{8,24},{12,28},{16,0},{20,4},{24,8},{28,12},{1,17},{... | collective-permute-start | bytes 479240 | tf_op jit(solution)/shard_map/ppermute | solution.py:259
  8.0 10.9 %collective-permute-start.1 = (bf16[624,128]{1,0:T(8,128)(2,1)}, bf16[624,128]{1,0:T(8,128)(2,1)S(1)}, u32[]{:S(2)}, u32[]{:S(2)}) collective-permute-start(bf16[624,128]{1,0:T(8,128)(2,1)} %get-tuple-element.20.refs_0_), channel_id=1, source_target_pairs={{0,2},{1,3},{2,0},{3,1},{4,6},{5,7},{6,4},{7,5},{8,10},{9,11},{10,... | collective-permute-start | bytes 479240 | tf_op jit(solution)/shard_map/ppermute | solution.py:257
  9.6 9.9 %collective-permute-start.4 = (bf16[576,128]{1,0:T(8,128)(2,1)}, bf16[576,128]{1,0:T(8,128)(2,1)S(1)}, u32[]{:S(2)}, u32[]{:S(2)}) collective-permute-start(bf16[576,128]{1,0:T(8,128)(2,1)} %get-tuple-element.21.refs_4_), channel_id=1, source_target_pairs={{0,8},{4,12},{8,0},{12,4},{16,24},{20,28},{24,16},{28,20},{1,9},{5... | collective-permute-start | bytes 442376 | tf_op jit(solution)/shard_map/ppermute | solution.py:259
  15.9 7.6 %collective-permute-start.10 = (bf16[624,128]{1,0:T(8,128)(2,1)S(1)}, bf16[624,128]{1,0:T(8,128)(2,1)S(1)}, u32[]{:S(2)}, u32[]{:S(2)}) collective-permute-start(bf16[624,128]{1,0:T(8,128)(2,1)S(1)} %collective-permute-done.8.refs_0_), channel_id=1, source_target_pairs={{0,2},{1,3},{2,0},{3,1},{4,6},{5,7},{6,4},{7,5},{8,10},{9,11},{10,... | collective-permute-start | bytes 479240 | tf_op jit(solution)/shard_map/ppermute | solution.py:257
  17.5 6.1 %collective-permute-start.3 = (bf16[576,128]{1,0:T(8,128)(2,1)}, bf16[576,128]{1,0:T(8,128)(2,1)S(1)}, u32[]{:S(2)}, u32[]{:S(2)}) collective-permute-start(bf16[576,128]{1,0:T(8,128)(2,1)} %get-tuple-element.21.refs_4_), channel_id=1, source_target_pairs={{0,4},{4,0},{8,12},{12,8},{16,20},{20,16},{24,28},{28,24},{1,5},{5... | collective-permute-start | bytes 442376 | tf_op jit(solution)/shard_map/ppermute | solution.py:259
  19.0 5.1 %collective-permute-start = (bf16[624,128]{1,0:T(8,128)(2,1)}, bf16[624,128]{1,0:T(8,128)(2,1)S(1)}, u32[]{:S(2)}, u32[]{:S(2)}) collective-permute-start(bf16[624,128]{1,0:T(8,128)(2,1)} %get-tuple-element.20.refs_0_), channel_id=1, source_target_pairs={{0,1},{1,0},{2,3},{3,2},{4,5},{5,4},{6,7},{7,6},{8,9},{9,8},{10,11... | collective-permute-start | bytes 479240 | tf_op jit(solution)/shard_map/ppermute | solution.py:257
  19.0 7.0 %collective-permute-start.2 = (bf16[624,128]{1,0:T(8,128)(2,1)S(1)}, bf16[624,128]{1,0:T(8,128)(2,1)S(1)}, u32[]{:S(2)}, u32[]{:S(2)}) collective-permute-start(bf16[624,128]{1,0:T(8,128)(2,1)S(1)} %collective-permute-done.1.refs_2_), channel_id=1, source_target_pairs={{0,1},{1,0},{2,3},{3,2},{4,5},{5,4},{6,7},{7,6},{8,9},{9,8},{10,11... | collective-permute-start | bytes 479240 | tf_op jit(solution)/shard_map/ppermute | solution.py:257
  19.5 6.5 %collective-permute-start.5 = (bf16[576,128]{1,0:T(8,128)(2,1)S(1)}, bf16[576,128]{1,0:T(8,128)(2,1)S(1)}, u32[]{:S(2)}, u32[]{:S(2)}) collective-permute-start(bf16[576,128]{1,0:T(8,128)(2,1)S(1)} %collective-permute-done.4.refs_6_), channel_id=1, source_target_pairs={{0,4},{4,0},{8,12},{12,8},{16,20},{20,16},{24,28},{28,24},{1,5},{5... | collective-permute-start | bytes 442376 | tf_op jit(solution)/shard_map/ppermute | solution.py:259
  23.5 7.3 %collective-permute-start.9 = (bf16[624,128]{1,0:T(8,128)(2,1)S(1)}, bf16[624,128]{1,0:T(8,128)(2,1)S(1)}, u32[]{:S(2)}, u32[]{:S(2)}) collective-permute-start(bf16[624,128]{1,0:T(8,128)(2,1)S(1)} %collective-permute-done.8.refs_0_), channel_id=1, source_target_pairs={{0,1},{1,0},{2,3},{3,2},{4,5},{5,4},{6,7},{7,6},{8,9},{9,8},{10,11... | collective-permute-start | bytes 479240 | tf_op jit(solution)/shard_map/ppermute | solution.py:257
  23.5 7.3 %collective-permute-start.11 = (bf16[624,128]{1,0:T(8,128)(2,1)S(1)}, bf16[624,128]{1,0:T(8,128)(2,1)S(1)}, u32[]{:S(2)}, u32[]{:S(2)}) collective-permute-start(bf16[624,128]{1,0:T(8,128)(2,1)S(1)} %collective-permute-done.10.refs_2_), channel_id=1, source_target_pairs={{0,1},{1,0},{2,3},{3,2},{4,5},{5,4},{6,7},{7,6},{8,9},{9,8},{10,11... | collective-permute-start | bytes 479240 | tf_op jit(solution)/shard_map/ppermute | solution.py:257
  26.0 0.9 %copy-start.1 = (bf16[576,128]{1,0:T(8,128)(2,1)S(1)}, bf16[576,128]{1,0:T(8,128)(2,1)}, u32[]{:S(2)}) copy-start(bf16[576,128]{1,0:T(8,128)(2,1)} %get-tuple-element.21.refs_4_) | copy-start | bytes 442372
  26.9 0.9 %copy-start.7 = (bf16[624,128]{1,0:T(8,128)(2,1)S(1)}, bf16[624,128]{1,0:T(8,128)(2,1)}, u32[]{:S(2)}) copy-start(bf16[624,128]{1,0:T(8,128)(2,1)} %get-tuple-element.20.refs_0_) | copy-start | bytes 479236
  27.8 3.0 %copy-start.2 = (bf16[576,128]{1,0:T(8,128)(2,1)S(1)}, bf16[576,128]{1,0:T(8,128)(2,1)}, u32[]{:S(2)}) copy-start(bf16[576,128]{1,0:T(8,128)(2,1)} %get-tuple-element.21.refs_4_) | copy-start | bytes 442372
  30.7 3.0 %copy-start.5 = (f32[288,128]{1,0:T(8,128)}, f32[288,128]{1,0:T(8,128)S(1)}, u32[]{:S(2)}) copy-start(f32[288,128]{1,0:T(8,128)S(1)} %get-tuple-element.22.refs_0_) | copy-start | bytes 442372
  30.7 3.0 %copy-start.6 = (f32[288,128]{1,0:T(8,128)}, f32[288,128]{1,0:T(8,128)S(1)}, u32[]{:S(2)}) copy-start(f32[288,128]{1,0:T(8,128)S(1)} %get-tuple-element.23.refs_1_) | copy-start | bytes 442372
  30.7 5.5 %collective-permute-start.6 = (bf16[576,128]{1,0:T(8,128)(2,1)S(1)}, bf16[576,128]{1,0:T(8,128)(2,1)S(1)}, u32[]{:S(2)}, u32[]{:S(2)}) collective-permute-start(bf16[576,128]{1,0:T(8,128)(2,1)S(1)} %get-tuple-element.24), channel_id=1, source_target_pairs={{0,1},{1,0},{2,3},{3,2},{4,5},{5,4},{6,7},{7,6},{8,9},{9,8},{10,11... | collective-permute-start | bytes 442376 | tf_op jit(solution)/shard_map/ppermute | solution.py:257
  33.8 0.7 %copy-start = (f32[576,128]{1,0:T(8,128)}, f32[576,128]{1,0:T(8,128)S(1)}, u32[]{:S(2)}) copy-start(f32[576,128]{1,0:T(8,128)S(1)} %get-tuple-element.33.refs_4_) | copy-start | bytes 884740
  34.5 0.7 %copy-start.3 = (f32[288,128]{1,0:T(8,128)}, f32[288,128]{1,0:T(8,128)S(1)}, u32[]{:S(2)}) copy-start(f32[288,128]{1,0:T(8,128)S(1)} %get-tuple-element.28.refs_0_) | copy-start | bytes 442372
  35.8 6.8 %collective-permute-start.12 = (bf16[576,128]{1,0:T(8,128)(2,1)S(1)}, bf16[576,128]{1,0:T(8,128)(2,1)S(1)}, u32[]{:S(2)}, u32[]{:S(2)}) collective-permute-start(bf16[576,128]{1,0:T(8,128)(2,1)S(1)} %get-tuple-element.30), channel_id=1, source_target_pairs={{0,1},{1,0},{2,3},{3,2},{4,5},{5,4},{6,7},{7,6},{8,9},{9,8},{10,11... | collective-permute-start | bytes 442376 | tf_op jit(solution)/shard_map/ppermute | solution.py:257
  36.3 0.7 %copy-start.11 = (bf16[576,128]{1,0:T(8,128)(2,1)}, bf16[576,128]{1,0:T(8,128)(2,1)S(1)}, u32[]{:S(2)}) copy-start(bf16[576,128]{1,0:T(8,128)(2,1)S(1)} %collective-permute-done.6.refs_2_) | copy-start | bytes 442372
  38.7 8.7 %collective-permute-start.7 = (bf16[288,128]{1,0:T(8,128)(2,1)}, bf16[288,128]{1,0:T(8,128)(2,1)S(1)}, u32[]{:S(2)}, u32[]{:S(2)}) collective-permute-start(bf16[288,128]{1,0:T(8,128)(2,1)} %get-tuple-element.26), channel_id=1, source_target_pairs={{0,2},{1,3},{2,0},{3,1},{4,6},{5,7},{6,4},{7,5},{8,10},{9,11},{10,... | collective-permute-start | bytes 221192 | tf_op jit(solution)/shard_map/ppermute | solution.py:257
  39.2 9.8 %collective-permute-start.15 = (bf16[576,128]{1,0:T(8,128)(2,1)S(1)}, bf16[576,128]{1,0:T(8,128)(2,1)S(1)}, u32[]{:S(2)}, u32[]{:S(2)}) collective-permute-start(bf16[576,128]{1,0:T(8,128)(2,1)S(1)} %get-tuple-element.34), channel_id=1, source_target_pairs={{0,4},{4,0},{8,12},{12,8},{16,20},{20,16},{24,28},{28,24},{1,5},{5... | collective-permute-start | bytes 442376 | tf_op jit(solution)/shard_map/ppermute | solution.py:259
  40.6 8.4 %collective-permute-start.16 = (bf16[576,128]{1,0:T(8,128)(2,1)S(1)}, bf16[576,128]{1,0:T(8,128)(2,1)S(1)}, u32[]{:S(2)}, u32[]{:S(2)}) collective-permute-start(bf16[576,128]{1,0:T(8,128)(2,1)S(1)} %get-tuple-element.35), channel_id=1, source_target_pairs={{0,8},{4,12},{8,0},{12,4},{16,24},{20,28},{24,16},{28,20},{1,9},{5... | collective-permute-start | bytes 442376 | tf_op jit(solution)/shard_map/ppermute | solution.py:259
  41.8 8.0 %collective-permute-start.17 = (bf16[576,128]{1,0:T(8,128)(2,1)S(1)}, bf16[576,128]{1,0:T(8,128)(2,1)S(1)}, u32[]{:S(2)}, u32[]{:S(2)}) collective-permute-start(bf16[576,128]{1,0:T(8,128)(2,1)S(1)} %get-tuple-element.36), channel_id=1, source_target_pairs={{0,12},{4,8},{8,4},{12,0},{16,28},{20,24},{24,20},{28,16},{1,13},{... | collective-permute-start | bytes 442376 | tf_op jit(solution)/shard_map/ppermute | solution.py:259
  42.6 0.7 %copy-start.12 = (bf16[576,128]{1,0:T(8,128)(2,1)}, bf16[576,128]{1,0:T(8,128)(2,1)S(1)}, u32[]{:S(2)}) copy-start(bf16[576,128]{1,0:T(8,128)(2,1)S(1)} %collective-permute-done.12.refs_2_) | copy-start | bytes 442372
  45.0 6.2 %collective-permute-start.13 = (bf16[288,128]{1,0:T(8,128)(2,1)}, bf16[288,128]{1,0:T(8,128)(2,1)S(1)}, u32[]{:S(2)}, u32[]{:S(2)}) collective-permute-start(bf16[288,128]{1,0:T(8,128)(2,1)} %get-tuple-element.31), channel_id=1, source_target_pairs={{0,16},{4,20},{8,24},{12,28},{16,0},{20,4},{24,8},{28,12},{1,17},{... | collective-permute-start | bytes 221192 | tf_op jit(solution)/shard_map/ppermute | solution.py:259
  47.4 8.8 %copy-start.13 = (bf16[288,128]{1,0:T(8,128)(2,1)}, bf16[288,128]{1,0:T(8,128)(2,1)S(1)}, u32[]{:S(2)}) copy-start(bf16[288,128]{1,0:T(8,128)(2,1)S(1)} %collective-permute-done.7.refs_1_) | copy-start | bytes 221188
  47.4 8.8 %collective-permute-start.14 = (bf16[288,128]{1,0:T(8,128)(2,1)}, bf16[288,128]{1,0:T(8,128)(2,1)S(1)}, u32[]{:S(2)}, u32[]{:S(2)}) collective-permute-start(bf16[288,128]{1,0:T(8,128)(2,1)} %get-tuple-element.32), channel_id=1, source_target_pairs={{0,18},{1,19},{2,16},{3,17},{4,22},{5,23},{6,20},{7,21},{8,26},{9,... | collective-permute-start | bytes 221192 | tf_op jit(solution)/shard_map/ppermute | solution.py:265
  49.0 7.3 %copy-start.8 = (bf16[576,128]{1,0:T(8,128)(2,1)}, bf16[576,128]{1,0:T(8,128)(2,1)S(1)}, u32[]{:S(2)}) copy-start(bf16[576,128]{1,0:T(8,128)(2,1)S(1)} %collective-permute-done.15.refs_5_) | copy-start | bytes 442372
  49.0 7.3 %copy-start.9 = (bf16[576,128]{1,0:T(8,128)(2,1)}, bf16[576,128]{1,0:T(8,128)(2,1)S(1)}, u32[]{:S(2)}) copy-start(bf16[576,128]{1,0:T(8,128)(2,1)S(1)} %collective-permute-done.16.refs_6_) | copy-start | bytes 442372
  49.8 6.5 %copy-start.10 = (bf16[576,128]{1,0:T(8,128)(2,1)}, bf16[576,128]{1,0:T(8,128)(2,1)S(1)}, u32[]{:S(2)}) copy-start(bf16[576,128]{1,0:T(8,128)(2,1)S(1)} %collective-permute-done.17.refs_7_) | copy-start | bytes 442372
  51.2 5.0 %copy-start.14 = (bf16[288,128]{1,0:T(8,128)(2,1)}, bf16[288,128]{1,0:T(8,128)(2,1)S(1)}, u32[]{:S(2)}) copy-start(bf16[288,128]{1,0:T(8,128)(2,1)S(1)} %collective-permute-done.13.refs_2_) | copy-start | bytes 221188
  (2 other events, 1.3 us)

commit v2 on v1

--- a/solution.py
+++ b/solution.py
@@ -38,6 +38,11 @@
         self.extra = round_up(self.lse_rows + 2 * self.heads, 16)
         self.high = ctx // 2
 
+    def grant(self, blocks):
+        scratch = 8 * self.tiles * self.span * LANES
+        pairs = blocks * self.rows * round_up(self.span, LANES)
+        return 2 * scratch + 32 * pairs + 2**20
+
 
 def split3(x):
     hi = x.astype(BF16).astype(F32)
@@ -46,8 +51,48 @@
     return hi, mid, rest - mid
 
 
-def pack_kernel(s, q_ref, k_ref, v_ref, o_ref, g_ref, lse_ref, qg_ref, kv_ref, wide, small):
+def pack_kernel(s, q_in, k_in, v_in, o_in, g_in, lse_in, qg_ref, kv_ref, *scratch):
+    q_ref, k_ref, v_ref, o_ref, g_ref, lse_ref, small, sems = scratch
+    copies = [
+        pltpu.make_async_copy(source, target, sems.at[i])
+        for i, (source, target) in enumerate(
+            (
+                (g_in, g_ref),
+                (o_in, o_ref),
+                (lse_in, lse_ref),
+                (q_in, q_ref),
+                (k_in, k_ref),
+                (v_in, v_ref),
+            )
+        )
+    ]
+    for copy in copies:
+        copy.start()
     r = s.rows
+    copies[0].wait()
+    copies[1].wait()
+    prod = g_ref[...].astype(F32) * o_ref[...].astype(F32)
+    hi = prod.astype(BF16)
+    lo = (prod - hi.astype(F32)).astype(BF16)
+    shape = (round_up(s.heads, 16), s.width)
+    pick = lax.broadcasted_iota(jnp.int32, shape, 1) // s.dim
+    pick = (pick == lax.broadcasted_iota(jnp.int32, shape, 0)).astype(F32).astype(BF16)
+    delta = dot(pick, hi, NT) + dot(pick, lo, NT)
+    d_hi, d_mid, _ = split3(delta)
+    small[...] = jnp.zeros(small.shape, F32)
+    copies[2].wait()
+    h = s.heads_group
+    at = 0
+    for t in range(s.span_tiles):
+        lanes = min(LANES, s.span - t * LANES)
+        for piece in split3(lse_ref[:, t * LANES : t * LANES + lanes]):
+            small[at : at + h, :lanes] = piece
+            at += h
+    small[at : at + s.heads, :r] = d_hi[: s.heads]
+    small[at + s.heads : at + 2 * s.heads, :r] = d_mid[: s.heads]
+    qg_ref[2 * s.part :, :] = small[...].astype(BF16)
+    for copy in copies[3:]:
+        copy.wait()
     for t in range(s.tiles):
         lanes = slice(t * LANES, (t + 1) * LANES)
         rows = slice(t * r, (t + 1) * r)
@@ -56,26 +101,10 @@
         qg_ref[more, :] = g_ref[:, lanes]
         kv_ref[rows, :] = k_ref[:, lanes]
         kv_ref[more, :] = v_ref[:, lanes]
-    prod = g_ref[...].astype(F32) * o_ref[...].astype(F32)
-    hi = prod.astype(BF16)
-    lo = (prod - hi.astype(F32)).astype(BF16)
-    shape = (round_up(s.heads, 16), s.width)
-    pick = lax.broadcasted_iota(jnp.int32, shape, 1) // s.dim
-    pick = (pick == lax.broadcasted_iota(jnp.int32, shape, 0)).astype(F32).astype(BF16)
-    delta = dot(pick, hi, NT) + dot(pick, lo, NT)
-    d_hi, d_mid, _ = split3(delta)
-    wide[...] = jnp.zeros(wide.shape, F32)
-    wide[: s.span, : s.heads_group] = lse_ref[...]
-    lse = wide[...].T[:8]
-    small[...] = jnp.zeros(small.shape, F32)
-    at = 0
-    for t in range(s.span_tiles):
-        for piece in split3(lse[:, t * LANES : (t + 1) * LANES]):
-            small[at : at + s.heads_group, :] = piece[: s.heads_group]
-            at += s.heads_group
-    small[at : at + s.heads, : s.rows] = d_hi[: s.heads]
-    small[at + s.heads : at + 2 * s.heads, : s.rows] = d_mid[: s.heads]
-    qg_ref[2 * s.part :, :] = small[...].astype(BF16)
+
+
+def in_hbm(x):
+    return pltpu.with_memory_space_constraint(x, pltpu.HBM)
 
 
 def pack(s, q, k, v, o, g, lse):
@@ -85,13 +114,16 @@
             jax.ShapeDtypeStruct((2 * s.part + s.extra, LANES), BF16),
             jax.ShapeDtypeStruct((2 * s.part, LANES), BF16),
         ),
-        in_specs=[VMEM] * 6,
+        in_specs=[pl.BlockSpec(memory_space=pl.ANY)] * 6,
         out_specs=[VMEM] * 2,
-        scratch_shapes=[
-            pltpu.VMEM((round_up(s.span, LANES), LANES), F32),
+        scratch_shapes=[pltpu.VMEM((s.rows, s.width), BF16)] * 5
+        + [
+            pltpu.VMEM((s.heads_group, s.span), F32),
             pltpu.VMEM((s.extra, LANES), F32),
+            pltpu.SemaphoreType.DMA((6,)),
         ],
-    )(q, k, v, o, g, lse)
+        compiler_params=pltpu.CompilerParams(vmem_limit_bytes=2 * 2**20),
+    )(*[in_hbm(x) for x in (q, k, v, o, g, jnp.transpose(lse))])
 
 
 def attend_kernel(s, blocks, first, *refs):
@@ -127,32 +159,42 @@
             delta = jnp.concatenate([delta, jnp.zeros((s.heads, wide - LANES), F32)], axis=1)
         total = total + pltpu.roll(delta, who * r, 1)
     deltas[...] = total
-    half = lax.broadcasted_iota(jnp.int32, (blocks * r, LANES), 1) < s.dim
+    size = blocks * r
+    lane = lax.broadcasted_iota(jnp.int32, (2 * size, LANES), 1) < s.dim
+    first_head = lax.broadcasted_iota(jnp.int32, (2 * size, LANES), 0) < size
+    own_lanes = lane == first_head
+    half = lane[:size]
     zero = jnp.zeros((), BF16)
+
+    def pair(block):
+        return jnp.where(own_lanes, jnp.concatenate([block, block], axis=0), zero)
+
     for t in range(s.tiles):
         rows = slice(t * r, (t + 1) * r)
         more = slice(s.part + t * r, s.part + (t + 1) * r)
-        k = jnp.concatenate([ref[rows, :] for ref in kv], axis=0)
-        v = jnp.concatenate([ref[more, :] for ref in kv], axis=0)
+        k = pair(jnp.concatenate([ref[rows, :] for ref in kv], axis=0))
+        v = pair(jnp.concatenate([ref[more, :] for ref in kv], axis=0))
         q, g = qs[t], gs[t]
-        dk, dv, dq = [], [], None
+        scores = dot(k, q, NT)
+        dweights = dot(v, g, NT)
+        low, dscores = [], []
         for e in range(2):
             head = 2 * t + e
-            mask = half if e == 0 else jnp.logical_not(half)
-            k_one = jnp.where(mask, k, zero)
-            v_one = jnp.where(mask, v, zero)
+            mine = slice(e * size, (e + 1) * size)
             j = head % h
-            norm = norms[head // h, j : j + 1, : s.span]
-            weights = jnp.exp(dot(k_one, q, NT) - norm)
-            dweights = dot(v_one, g, NT)
-            dscores = (weights * (dweights - deltas[head : head + 1, : s.span])).astype(BF16)
-            dv.append(dot(weights.astype(BF16), g, NN))
-            dk.append(dot(dscores, q, NN))
-            term = dot(dscores, k_one, TN)
-            dq = term if dq is None else dq + term
+            weights = jnp.exp(scores[mine] - norms[head // h, j : j + 1, : s.span])
+            low.append(weights.astype(BF16))
+            gap = dweights[mine] - deltas[head : head + 1, : s.span]
+            dscores.append((weights * gap).astype(BF16))
+        low = jnp.concatenate(low, axis=0)
+        dscores = jnp.concatenate(dscores, axis=0)
+        dv = dot(low, g, NN)
+        dk = dot(dscores, q, NN)
+        dv, dk = [dv[:size], dv[size:]], [dk[:size], dk[size:]]
+        dq = dot(dscores, k, TN)
         dqs[t] = dq * scale
-        for where, pair in ((rows, dk), (more, dv)):
-            both = jnp.where(half, pair[0], pair[1])
+        for where, parts in ((rows, dk), (more, dv)):
+            both = jnp.where(half, parts[0], parts[1])
             for i in range(blocks):
                 piece = both[i * r : (i + 1) * r]
                 if first:
@@ -195,9 +237,9 @@
             pltpu.VMEM((s.group, 8, s.span_tiles * LANES), F32),
             pltpu.VMEM((s.heads, s.span_tiles * LANES), F32),
         ],
-        compiler_params=pltpu.CompilerParams(vmem_limit_bytes=48 * 2**20),
+        compiler_params=pltpu.CompilerParams(vmem_limit_bytes=s.grant(blocks)),
         cost_estimate=pl.CostEstimate(
-            flops=20 * pairs * s.dim, bytes_accessed=4 * s.part * LANES * 8, transcendentals=pairs
+            flops=200 * pairs * s.dim, bytes_accessed=4 * s.part * LANES * 8, transcendentals=pairs
         ),
     )(*operands)
     count = s.group // 2
@@ -223,6 +265,7 @@
         out_shape=out,
         in_specs=[VMEM] * (count + 1),
         out_specs=[VMEM] * count,
+        compiler_params=pltpu.CompilerParams(vmem_limit_bytes=2**20),
     )(*keep, recv)
 
 
@@ -245,6 +288,7 @@
         out_shape=[jax.ShapeDtypeStruct((s.rows, s.width), BF16)] * 3,
         in_specs=[VMEM] * (len(dq) + len(kv)),
         out_specs=[VMEM] * 3,
+        compiler_params=pltpu.CompilerParams(vmem_limit_bytes=2**20),
     )(*dq, *kv)
 
 
@@ -264,23 +308,27 @@
         ]
         return lax.ppermute(x, ("ctx", "head"), pairs)
 
+    tie = lax.optimization_barrier
     qg_own, kv_own = pack(s, queries, keys, values, attended, grad_out, logsumexp)
+    bits = [1 << i for i in reversed(range(s.high.bit_length() - 1))]
     far = {0: move(qg_own, s.high, 0)}
     kv = {0: kv_own}
-    bit = s.high // 2
-    while bit:
-        for off in sorted(kv):
+    kv.update({bit: move(kv_own, bit, 0) for bit in bits})
+    near = {0: qg_own, group // 2: move(qg_own, 0, group // 2)}
+    for bit in bits:
+        for off in sorted(off for off in kv if off % (2 * bit) == 0 and off):
             kv[off + bit] = move(kv[off], bit, 0)
-        bit //= 2
-    near = {0: qg_own}
     bit = group // 2
     while bit:
-        for blocks in (near, far):
-            for off in sorted(blocks):
-                blocks[off + bit] = move(blocks[off], 0, bit)
+        for blocks in (far, near):
+            for off in sorted(off for off in blocks if off % (2 * bit) == 0):
+                if off + bit not in blocks and not (blocks is far and bit == 1 and off == group // 2):
+                    blocks[off + bit] = move(blocks[off], 0, bit)
         bit //= 2
     kv = [kv[off] for off in range(s.high)]
     keep0, send0, sums0 = attend(s, [near[i] for i in range(group)], kv, None)
+    keep0, send0, sums0, far = tie((keep0, send0, sums0, far))
+    far[group // 2 + 1] = move(far[group // 2], 0, 1)
     keep1, send1, sums1 = attend(s, [far[i] for i in range(group)], kv, sums0[0])
     dq = core_add(s, keep0, move(send0, 0, 1), True)
     total_q = [dq[0]] + [move(dq[i], 0, 2 * i) for i in range(1, group // 2)]

time: 59.2 us -> 40.9 us (0.69)
  local copies, waits for them, and re-layouts: 7.24 us -> 0 us
  Pallas kernels: 13.2 us -> 6.55 us
  waiting for transfers between devices: 17.5 us -> 13.4 us
    unnamed x33 -> x0, local copies, waits for them, and re-layouts: 7.24 us -> none
    ppermute x1, waiting for transfers between devices: 4.99 us -> 0.01 us  [move(): return lax.ppermute(x, ('ctx', 'head'), pairs)]
    pallas_call x2, Pallas kernels: 3.47 us -> 0.06 us  [core_add(): pl.pallas_call(functools.partial(core_kernel, s, keep_own), out_shape=out...]
    ppermute x9, waiting for transfers between devices: 0.02 us -> 1.54 us  [move(): return lax.ppermute(x, 'head', [(i, i ^ head_off) for i in range(group)])]
    pallas_call x1, Pallas kernels: 2.03 us -> 0.75 us  [finish(): pl.pallas_call(functools.partial(final_kernel, s, len(dq), len(kv)), out_...]
    pallas_call x2, Pallas kernels: 5.78 us -> 4.53 us  [attend(): pl.pallas_call(functools.partial(attend_kernel, s, blocks, first), out_sh...]
    ppermute x1, starting transfers between devices: 1.53 us -> 0.66 us  [move(): return lax.ppermute(x, ('ctx', 'head'), pairs)]
    ppermute x9, starting transfers between devices: 5.12 us -> 6 us  [move(): return lax.ppermute(x, 'head', [(i, i ^ head_off) for i in range(group)])]
  transfers between devices with their start and end apart: 18 -> 18, of which waited for: 6 -> 7; matrix products, arithmetic and copies ran while one was open for 0% -> 0% of each run, Pallas kernels for 16% -> 11%
where the time goes in v2:
time: 40.9 us; the launch traced here: 40.6 us
  starting transfers between devices  19.9 us (49%)
  waiting for transfers between devices  13.4 us (33%)
  Pallas kernels  6.55 us (16%)
  between operations  0.69 us (2%)
    ppermute x8, starting transfers between devices, move(): return lax.ppermute(x, 'ctx', [(i, i ^ ctx_off) for i in range(ctx)])  13.3 us
    ppermute x8, waiting for transfers between devices, move(): return lax.ppermute(x, 'ctx', [(i, i ^ ctx_off) for i in range(ctx)])  11.9 us
    ppermute x9, starting transfers between devices, move(): return lax.ppermute(x, 'head', [(i, i ^ head_off) for i in range(group)])  6 us
    pallas_call x2, Pallas kernels, attend(): pl.pallas_call(functools.partial(attend_kernel, s, blocks, first), out_sh...  4.53 us
    ppermute x9, waiting for transfers between devices, move(): return lax.ppermute(x, 'head', [(i, i ^ head_off) for i in range(group)])  1.54 us
    pallas_call x1, Pallas kernels, pack(): pl.pallas_call(functools.partial(pack_kernel, s), out_shape=(jax.ShapeDty...  1.21 us
  transfers between devices with their start and end apart: 18, of which 7 were waited for; matrix products, arithmetic and copies ran while one was open for 0% of the time, Pallas kernels for 11%

profile of v2, /device:TPU:0, one launch (start us, length us, event | category | flops | bytes accessed | tf_op | source)
XLA Modules:
  0.0 40.6 jit_solution(2364088253571096952)
XLA Ops:
  0.6 1.2 %shard_map.85 = (bf16[624,128]{1,0:T(8,128)(2,1)S(1)}, bf16[576,128]{1,0:T(8,128)(2,1)S(1)}) custom-call(bf16[48,768]{1,0:T(8,128)(2,1)} %q_in.1, bf16[48,768]{1,0:T(8,128)(2,1)} %k_in.1, bf16[48,768]{1,0:T(8,128)(2,1)} %v_in.1, bf16[48,768]{1,0:T(8,128)(2,1)} %o_in.1, bf16[48,768]{1,0:T(8,128)(2,1)} %g_in.1, f32[3,192]{1,0:T(4,128)} %bitcast.1), custom_call_target="tpu_custom_call" | custom-call | tf_op jit(solution)/shard_map/pallas_call | solution.py:111
  1.9 3.0 %collective-permute-start.1 = (bf16[624,128]{1,0:T(8,128)(2,1)S(1)}, bf16[624,128]{1,0:T(8,128)(2,1)S(1)}, u32[]{:S(2)}, u32[]{:S(2)}) collective-permute-start(bf16[624,128]{1,0:T(8,128)(2,1)S(1)} %get-tuple-element.27.refs_0_), channel_id=1, source_target_pairs={{0,2},{1,3},{2,0},{3,1},{4,6},{5,7},{6,4},{7,5},{8,10},{9,11},{10,... | collective-permute-start | bytes 479240 | tf_op jit(solution)/shard_map/ppermute | solution.py:301
  4.9 1.6 %collective-permute-start.4 = (bf16[576,128]{1,0:T(8,128)(2,1)S(1)}, bf16[576,128]{1,0:T(8,128)(2,1)S(1)}, u32[]{:S(2)}, u32[]{:S(2)}) collective-permute-start(bf16[576,128]{1,0:T(8,128)(2,1)S(1)} %get-tuple-element.28.refs_4_), channel_id=1, source_target_pairs={{0,8},{4,12},{8,0},{12,4},{16,24},{20,28},{24,16},{28,20},{1,9},{5... | collective-permute-start | bytes 442376 | tf_op jit(solution)/shard_map/ppermute | solution.py:303
  6.5 2.6 %collective-permute-start.6 = (bf16[624,128]{1,0:T(8,128)(2,1)S(1)}, bf16[624,128]{1,0:T(8,128)(2,1)S(1)}, u32[]{:S(2)}, u32[]{:S(2)}) collective-permute-start(bf16[624,128]{1,0:T(8,128)(2,1)S(1)} %get-tuple-element.27.refs_0_), channel_id=1, source_target_pairs={{0,16},{4,20},{8,24},{12,28},{16,0},{20,4},{24,8},{28,12},{1,17},{... | collective-permute-start | bytes 479240 | tf_op jit(solution)/shard_map/ppermute | solution.py:303
  9.1 0.0 collective-permute-start
  9.1 0.0 collective-permute-done.1.refs_2_
  9.1 0.5 %collective-permute-start.2 = (bf16[624,128]{1,0:T(8,128)(2,1)S(1)}, bf16[624,128]{1,0:T(8,128)(2,1)S(1)}, u32[]{:S(2)}, u32[]{:S(2)}) collective-permute-start(bf16[624,128]{1,0:T(8,128)(2,1)S(1)} %collective-permute-done.1.refs_2_), channel_id=1, source_target_pairs={{0,1},{1,0},{2,3},{3,2},{4,5},{5,4},{6,7},{7,6},{8,9},{9,8},{10,11... | collective-permute-start | bytes 479240 | tf_op jit(solution)/shard_map/ppermute | solution.py:301
  9.6 1.5 %collective-permute-start.3 = (bf16[576,128]{1,0:T(8,128)(2,1)S(1)}, bf16[576,128]{1,0:T(8,128)(2,1)S(1)}, u32[]{:S(2)}, u32[]{:S(2)}) collective-permute-start(bf16[576,128]{1,0:T(8,128)(2,1)S(1)} %get-tuple-element.28.refs_4_), channel_id=1, source_target_pairs={{0,4},{4,0},{8,12},{12,8},{16,20},{20,16},{24,28},{28,24},{1,5},{5... | collective-permute-start | bytes 442376 | tf_op jit(solution)/shard_map/ppermute | solution.py:303
  11.1 1.5 %collective-permute-done.4.refs_6_ = bf16[576,128]{1,0:T(8,128)(2,1)S(1)} collective-permute-done((bf16[576,128]{1,0:T(8,128)(2,1)S(1)}, bf16[576,128]{1,0:T(8,128)(2,1)S(1)}, u32[]{:S(2)}, u32[]{:S(2)}) %collective-permute-start.4) | collective-permute-done | bytes 147488 | tf_op jit(solution)/shard_map/ppermute | solution.py:303
  12.6 1.5 %collective-permute-start.5 = (bf16[576,128]{1,0:T(8,128)(2,1)S(1)}, bf16[576,128]{1,0:T(8,128)(2,1)S(1)}, u32[]{:S(2)}, u32[]{:S(2)}) collective-permute-start(bf16[576,128]{1,0:T(8,128)(2,1)S(1)} %collective-permute-done.4.refs_6_), channel_id=1, source_target_pairs={{0,4},{4,0},{8,12},{12,8},{16,20},{20,16},{24,28},{28,24},{1,5},{5... | collective-permute-start | bytes 442376 | tf_op jit(solution)/shard_map/ppermute | solution.py:303
  14.1 2.0 %collective-permute-done.6.refs_0_ = bf16[624,128]{1,0:T(8,128)(2,1)S(1)} collective-permute-done((bf16[624,128]{1,0:T(8,128)(2,1)S(1)}, bf16[624,128]{1,0:T(8,128)(2,1)S(1)}, u32[]{:S(2)}, u32[]{:S(2)}) %collective-permute-start.6) | collective-permute-done | bytes 159776 | tf_op jit(solution)/shard_map/ppermute | solution.py:303
  16.1 0.5 %collective-permute-start.8 = (bf16[624,128]{1,0:T(8,128)(2,1)S(1)}, bf16[624,128]{1,0:T(8,128)(2,1)S(1)}, u32[]{:S(2)}, u32[]{:S(2)}) collective-permute-start(bf16[624,128]{1,0:T(8,128)(2,1)S(1)} %collective-permute-done.6.refs_0_), channel_id=1, source_target_pairs={{0,2},{1,3},{2,0},{3,1},{4,6},{5,7},{6,4},{7,5},{8,10},{9,11},{10,... | collective-permute-start | bytes 479240 | tf_op jit(solution)/shard_map/ppermute | solution.py:301
  16.6 0.0 collective-permute-start.7
  16.6 0.0 collective-permute-done.refs_1_
  16.6 1.8 %collective-permute-done.5.refs_7_ = bf16[576,128]{1,0:T(8,128)(2,1)S(1)} collective-permute-done((bf16[576,128]{1,0:T(8,128)(2,1)S(1)}, bf16[576,128]{1,0:T(8,128)(2,1)S(1)}, u32[]{:S(2)}, u32[]{:S(2)}) %collective-permute-start.5) | collective-permute-done | bytes 147488 | tf_op jit(solution)/shard_map/ppermute | solution.py:303
  18.5 0.0 collective-permute-done.2.refs_3_
  18.5 2.3 %shard_map.86 = (f32[288,128]{1,0:T(8,128)S(1)}, f32[288,128]{1,0:T(8,128)S(1)}, bf16[576,128]{1,0:T(8,128)(2,1)S(1)}, f32[2304,128]{1,0:T(8,128)S(1)}) custom-call(bf16[624,128]{1,0:T(8,128)(2,1)S(1)} %get-tuple-element.27.refs_0_, bf16[624,128]{1,0:T(8,128)(2,1)S(1)} %collective-permute-done.refs_1_, bf16[624,128]{1,0:T(8,128)(2,1)S(1)} %collective-permute-done.1.refs_2_, ...), custom_call_target="tpu_custom_call" | custom-call | flops 5662310400 | bytes 1179648 | tf_op jit(solution)/shard_map/pallas_call | solution.py:228
  20.8 0.6 %collective-permute-done.8.refs_2_ = bf16[624,128]{1,0:T(8,128)(2,1)S(1)} collective-permute-done((bf16[624,128]{1,0:T(8,128)(2,1)S(1)}, bf16[624,128]{1,0:T(8,128)(2,1)S(1)}, u32[]{:S(2)}, u32[]{:S(2)}) %collective-permute-start.8) | collective-permute-done | bytes 159776 | tf_op jit(solution)/shard_map/ppermute | solution.py:301
  21.4 0.0 collective-permute-done.7.refs_1_
  21.4 0.5 %collective-permute-start.9 = (bf16[576,128]{1,0:T(8,128)(2,1)S(1)}, bf16[576,128]{1,0:T(8,128)(2,1)S(1)}, u32[]{:S(2)}, u32[]{:S(2)}) collective-permute-start(bf16[576,128]{1,0:T(8,128)(2,1)S(1)} %get-tuple-element.35), channel_id=1, source_target_pairs={{0,1},{1,0},{2,3},{3,2},{4,5},{5,4},{6,7},{7,6},{8,9},{9,8},{10,11... | collective-permute-start | bytes 442376 | tf_op jit(solution)/shard_map/ppermute | solution.py:301
  21.9 0.9 %collective-permute-done.11.refs_3_ = bf16[624,128]{1,0:T(8,128)(2,1)S(1)} collective-permute-done((bf16[624,128]{1,0:T(8,128)(2,1)S(1)}, bf16[624,128]{1,0:T(8,128)(2,1)S(1)}, u32[]{:S(2)}, u32[]{:S(2)}) %collective-permute-start.11) | collective-permute-done | bytes 159776 | tf_op jit(solution)/shard_map/ppermute | solution.py:301
  22.8 2.3 %shard_map.88 = (f32[288,128]{1,0:T(8,128)S(1)}, f32[288,128]{1,0:T(8,128)S(1)}, bf16[576,128]{1,0:T(8,128)(2,1)S(1)}, f32[576,128]{1,0:T(8,128)S(1)}, bf16[576,...) custom-call(bf16[624,128]{1,0:T(8,128)(2,1)S(1)} %collective-permute-done.6.refs_0_, ...), custom_call_target="tpu_custom_call" | custom-call | flops 5662310400 | bytes 1179648 | tf_op jit(solution)/shard_map/pallas_call | solution.py:228
  25.1 0.2 collective-permute-start.12
  25.3 1.2 %collective-permute-start.10 = (bf16[288,128]{1,0:T(8,128)(2,1)S(1)}, bf16[288,128]{1,0:T(8,128)(2,1)S(1)}, u32[]{:S(2)}, u32[]{:S(2)}) collective-permute-start(bf16[288,128]{1,0:T(8,128)(2,1)S(1)} %get-tuple-element.37), channel_id=1, source_target_pairs={{0,2},{1,3},{2,0},{3,1},{4,6},{5,7},{6,4},{7,5},{8,10},{9,11},{10,... | collective-permute-start | bytes 221192 | tf_op jit(solution)/shard_map/ppermute | solution.py:301
  26.5 1.5 %collective-permute-start.15 = (bf16[576,128]{1,0:T(8,128)(2,1)S(1)}, bf16[576,128]{1,0:T(8,128)(2,1)S(1)}, u32[]{:S(2)}, u32[]{:S(2)}) collective-permute-start(bf16[576,128]{1,0:T(8,128)(2,1)S(1)} %get-tuple-element.48), channel_id=1, source_target_pairs={{0,4},{4,0},{8,12},{12,8},{16,20},{20,16},{24,28},{28,24},{1,5},{5... | collective-permute-start | bytes 442376 | tf_op jit(solution)/shard_map/ppermute | solution.py:303
  28.0 1.6 %collective-permute-start.16 = (bf16[576,128]{1,0:T(8,128)(2,1)S(1)}, bf16[576,128]{1,0:T(8,128)(2,1)S(1)}, u32[]{:S(2)}, u32[]{:S(2)}) collective-permute-start(bf16[576,128]{1,0:T(8,128)(2,1)S(1)} %get-tuple-element.49), channel_id=1, source_target_pairs={{0,8},{4,12},{8,0},{12,4},{16,24},{20,28},{24,16},{28,20},{1,9},{5... | collective-permute-start | bytes 442376 | tf_op jit(solution)/shard_map/ppermute | solution.py:303
  29.6 0.4 %collective-permute-start.17 = (bf16[576,128]{1,0:T(8,128)(2,1)S(1)}, bf16[576,128]{1,0:T(8,128)(2,1)S(1)}, u32[]{:S(2)}, u32[]{:S(2)}) collective-permute-start(bf16[576,128]{1,0:T(8,128)(2,1)S(1)} %get-tuple-element.50), channel_id=1, source_target_pairs={{0,12},{4,8},{8,4},{12,0},{16,28},{20,24},{24,20},{28,16},{1,13},{... | collective-permute-start | bytes 442376 | tf_op jit(solution)/shard_map/ppermute | solution.py:303
  30.1 2.7 %collective-permute-start.13 = (bf16[288,128]{1,0:T(8,128)(2,1)S(1)}, bf16[288,128]{1,0:T(8,128)(2,1)S(1)}, u32[]{:S(2)}, u32[]{:S(2)}) collective-permute-start(bf16[288,128]{1,0:T(8,128)(2,1)S(1)} %get-tuple-element.45), channel_id=1, source_target_pairs={{0,16},{4,20},{8,24},{12,28},{16,0},{20,4},{24,8},{28,12},{1,17},{... | collective-permute-start | bytes 221192 | tf_op jit(solution)/shard_map/ppermute | solution.py:303
  32.7 0.7 %collective-permute-start.14 = (bf16[288,128]{1,0:T(8,128)(2,1)S(1)}, bf16[288,128]{1,0:T(8,128)(2,1)S(1)}, u32[]{:S(2)}, u32[]{:S(2)}) collective-permute-start(bf16[288,128]{1,0:T(8,128)(2,1)S(1)} %get-tuple-element.46), channel_id=1, source_target_pairs={{0,18},{1,19},{2,16},{3,17},{4,22},{5,23},{6,20},{7,21},{8,26},{9,... | collective-permute-start | bytes 221192 | tf_op jit(solution)/shard_map/ppermute | solution.py:309
  33.4 3.8 %collective-permute-done.16.refs_6_ = bf16[576,128]{1,0:T(8,128)(2,1)S(1)} collective-permute-done((bf16[576,128]{1,0:T(8,128)(2,1)S(1)}, bf16[576,128]{1,0:T(8,128)(2,1)S(1)}, u32[]{:S(2)}, u32[]{:S(2)}) %collective-permute-start.16) | collective-permute-done | bytes 147488 | tf_op jit(solution)/shard_map/ppermute | solution.py:303
  37.2 2.7 %collective-permute-done.17.refs_7_ = bf16[576,128]{1,0:T(8,128)(2,1)S(1)} collective-permute-done((bf16[576,128]{1,0:T(8,128)(2,1)S(1)}, bf16[576,128]{1,0:T(8,128)(2,1)S(1)}, u32[]{:S(2)}, u32[]{:S(2)}) %collective-permute-start.17) | collective-permute-done | bytes 147488 | tf_op jit(solution)/shard_map/ppermute | solution.py:303
  39.9 0.8 %shard_map.90 = (bf16[48,768]{1,0:T(8,128)(2,1)}, bf16[48,768]{1,0:T(8,128)(2,1)}, bf16[48,768]{1,0:T(8,128)(2,1)}) custom-call(f32[288,128]{1,0:T(8,128)S(1)} %get-tuple-element.36.refs_0_, bf16[288,128]{1,0:T(8,128)(2,1)S(1)} %collective-permute-done.10.refs_1_, bf16[288,128]{1,0:T(8,128)(2,1)S(1)} %collective-permute-done.13.refs_2_, ...), custom_call_target="tpu_custom_call" | custom-call | tf_op jit(solution)/shard_map/pallas_call | solution.py:286
  (10 shorter events, 0.1 us)
Async XLA Ops:
  1.9 7.2 %collective-permute-start.1 = (bf16[624,128]{1,0:T(8,128)(2,1)S(1)}, bf16[624,128]{1,0:T(8,128)(2,1)S(1)}, u32[]{:S(2)}, u32[]{:S(2)}) collective-permute-start(bf16[624,128]{1,0:T(8,128)(2,1)S(1)} %get-tuple-element.27.refs_0_), channel_id=1, source_target_pairs={{0,2},{1,3},{2,0},{3,1},{4,6},{5,7},{6,4},{7,5},{8,10},{9,11},{10,... | collective-permute-start | bytes 479240 | tf_op jit(solution)/shard_map/ppermute | solution.py:301
  4.9 7.7 %collective-permute-start.4 = (bf16[576,128]{1,0:T(8,128)(2,1)S(1)}, bf16[576,128]{1,0:T(8,128)(2,1)S(1)}, u32[]{:S(2)}, u32[]{:S(2)}) collective-permute-start(bf16[576,128]{1,0:T(8,128)(2,1)S(1)} %get-tuple-element.28.refs_4_), channel_id=1, source_target_pairs={{0,8},{4,12},{8,0},{12,4},{16,24},{20,28},{24,16},{28,20},{1,9},{5... | collective-permute-start | bytes 442376 | tf_op jit(solution)/shard_map/ppermute | solution.py:303
  6.5 9.7 %collective-permute-start.6 = (bf16[624,128]{1,0:T(8,128)(2,1)S(1)}, bf16[624,128]{1,0:T(8,128)(2,1)S(1)}, u32[]{:S(2)}, u32[]{:S(2)}) collective-permute-start(bf16[624,128]{1,0:T(8,128)(2,1)S(1)} %get-tuple-element.27.refs_0_), channel_id=1, source_target_pairs={{0,16},{4,20},{8,24},{12,28},{16,0},{20,4},{24,8},{28,12},{1,17},{... | collective-permute-start | bytes 479240 | tf_op jit(solution)/shard_map/ppermute | solution.py:303
  9.1 7.6 %collective-permute-start = (bf16[624,128]{1,0:T(8,128)(2,1)S(1)}, bf16[624,128]{1,0:T(8,128)(2,1)S(1)}, u32[]{:S(2)}, u32[]{:S(2)}) collective-permute-start(bf16[624,128]{1,0:T(8,128)(2,1)S(1)} %get-tuple-element.27.refs_0_), channel_id=1, source_target_pairs={{0,1},{1,0},{2,3},{3,2},{4,5},{5,4},{6,7},{7,6},{8,9},{9,8},{10,11... | collective-permute-start | bytes 479240 | tf_op jit(solution)/shard_map/ppermute | solution.py:301
  9.1 9.4 %collective-permute-start.2 = (bf16[624,128]{1,0:T(8,128)(2,1)S(1)}, bf16[624,128]{1,0:T(8,128)(2,1)S(1)}, u32[]{:S(2)}, u32[]{:S(2)}) collective-permute-start(bf16[624,128]{1,0:T(8,128)(2,1)S(1)} %collective-permute-done.1.refs_2_), channel_id=1, source_target_pairs={{0,1},{1,0},{2,3},{3,2},{4,5},{5,4},{6,7},{7,6},{8,9},{9,8},{10,11... | collective-permute-start | bytes 479240 | tf_op jit(solution)/shard_map/ppermute | solution.py:301
  9.6 7.1 %collective-permute-start.3 = (bf16[576,128]{1,0:T(8,128)(2,1)S(1)}, bf16[576,128]{1,0:T(8,128)(2,1)S(1)}, u32[]{:S(2)}, u32[]{:S(2)}) collective-permute-start(bf16[576,128]{1,0:T(8,128)(2,1)S(1)} %get-tuple-element.28.refs_4_), channel_id=1, source_target_pairs={{0,4},{4,0},{8,12},{12,8},{16,20},{20,16},{24,28},{28,24},{1,5},{5... | collective-permute-start | bytes 442376 | tf_op jit(solution)/shard_map/ppermute | solution.py:303
  12.6 5.9 %collective-permute-start.5 = (bf16[576,128]{1,0:T(8,128)(2,1)S(1)}, bf16[576,128]{1,0:T(8,128)(2,1)S(1)}, u32[]{:S(2)}, u32[]{:S(2)}) collective-permute-start(bf16[576,128]{1,0:T(8,128)(2,1)S(1)} %collective-permute-done.4.refs_6_), channel_id=1, source_target_pairs={{0,4},{4,0},{8,12},{12,8},{16,20},{20,16},{24,28},{28,24},{1,5},{5... | collective-permute-start | bytes 442376 | tf_op jit(solution)/shard_map/ppermute | solution.py:303
  16.1 5.3 %collective-permute-start.8 = (bf16[624,128]{1,0:T(8,128)(2,1)S(1)}, bf16[624,128]{1,0:T(8,128)(2,1)S(1)}, u32[]{:S(2)}, u32[]{:S(2)}) collective-permute-start(bf16[624,128]{1,0:T(8,128)(2,1)S(1)} %collective-permute-done.6.refs_0_), channel_id=1, source_target_pairs={{0,2},{1,3},{2,0},{3,1},{4,6},{5,7},{6,4},{7,5},{8,10},{9,11},{10,... | collective-permute-start | bytes 479240 | tf_op jit(solution)/shard_map/ppermute | solution.py:301
  16.6 4.8 %collective-permute-start.7 = (bf16[624,128]{1,0:T(8,128)(2,1)S(1)}, bf16[624,128]{1,0:T(8,128)(2,1)S(1)}, u32[]{:S(2)}, u32[]{:S(2)}) collective-permute-start(bf16[624,128]{1,0:T(8,128)(2,1)S(1)} %collective-permute-done.6.refs_0_), channel_id=1, source_target_pairs={{0,1},{1,0},{2,3},{3,2},{4,5},{5,4},{6,7},{7,6},{8,9},{9,8},{10,11... | collective-permute-start | bytes 479240 | tf_op jit(solution)/shard_map/ppermute | solution.py:301
  21.4 1.4 %collective-permute-start.11 = (bf16[624,128]{1,0:T(8,128)(2,1)S(1)}, bf16[624,128]{1,0:T(8,128)(2,1)S(1)}, u32[]{:S(2)}, u32[]{:S(2)}) collective-permute-start(bf16[624,128]{1,0:T(8,128)(2,1)S(1)} %collective-permute-done.8.refs_2_), channel_id=1, source_target_pairs={{0,1},{1,0},{2,3},{3,2},{4,5},{5,4},{6,7},{7,6},{8,9},{9,8},{10,11... | collective-permute-start | bytes 479240 | tf_op jit(solution)/shard_map/ppermute | solution.py:301
  21.4 3.9 %collective-permute-start.9 = (bf16[576,128]{1,0:T(8,128)(2,1)S(1)}, bf16[576,128]{1,0:T(8,128)(2,1)S(1)}, u32[]{:S(2)}, u32[]{:S(2)}) collective-permute-start(bf16[576,128]{1,0:T(8,128)(2,1)S(1)} %get-tuple-element.35), channel_id=1, source_target_pairs={{0,1},{1,0},{2,3},{3,2},{4,5},{5,4},{6,7},{7,6},{8,9},{9,8},{10,11... | collective-permute-start | bytes 442376 | tf_op jit(solution)/shard_map/ppermute | solution.py:301
  25.1 5.0 %collective-permute-start.12 = (bf16[576,128]{1,0:T(8,128)(2,1)S(1)}, bf16[576,128]{1,0:T(8,128)(2,1)S(1)}, u32[]{:S(2)}, u32[]{:S(2)}) collective-permute-start(bf16[576,128]{1,0:T(8,128)(2,1)S(1)} %get-tuple-element.44), channel_id=1, source_target_pairs={{0,1},{1,0},{2,3},{3,2},{4,5},{5,4},{6,7},{7,6},{8,9},{9,8},{10,11... | collective-permute-start | bytes 442376 | tf_op jit(solution)/shard_map/ppermute | solution.py:301
  25.3 7.4 %collective-permute-start.10 = (bf16[288,128]{1,0:T(8,128)(2,1)S(1)}, bf16[288,128]{1,0:T(8,128)(2,1)S(1)}, u32[]{:S(2)}, u32[]{:S(2)}) collective-permute-start(bf16[288,128]{1,0:T(8,128)(2,1)S(1)} %get-tuple-element.37), channel_id=1, source_target_pairs={{0,2},{1,3},{2,0},{3,1},{4,6},{5,7},{6,4},{7,5},{8,10},{9,11},{10,... | collective-permute-start | bytes 221192 | tf_op jit(solution)/shard_map/ppermute | solution.py:301
  26.5 6.8 %collective-permute-start.15 = (bf16[576,128]{1,0:T(8,128)(2,1)S(1)}, bf16[576,128]{1,0:T(8,128)(2,1)S(1)}, u32[]{:S(2)}, u32[]{:S(2)}) collective-permute-start(bf16[576,128]{1,0:T(8,128)(2,1)S(1)} %get-tuple-element.48), channel_id=1, source_target_pairs={{0,4},{4,0},{8,12},{12,8},{16,20},{20,16},{24,28},{28,24},{1,5},{5... | collective-permute-start | bytes 442376 | tf_op jit(solution)/shard_map/ppermute | solution.py:303
  28.0 9.1 %collective-permute-start.16 = (bf16[576,128]{1,0:T(8,128)(2,1)S(1)}, bf16[576,128]{1,0:T(8,128)(2,1)S(1)}, u32[]{:S(2)}, u32[]{:S(2)}) collective-permute-start(bf16[576,128]{1,0:T(8,128)(2,1)S(1)} %get-tuple-element.49), channel_id=1, source_target_pairs={{0,8},{4,12},{8,0},{12,4},{16,24},{20,28},{24,16},{28,20},{1,9},{5... | collective-permute-start | bytes 442376 | tf_op jit(solution)/shard_map/ppermute | solution.py:303
  29.6 10.3 %collective-permute-start.17 = (bf16[576,128]{1,0:T(8,128)(2,1)S(1)}, bf16[576,128]{1,0:T(8,128)(2,1)S(1)}, u32[]{:S(2)}, u32[]{:S(2)}) collective-permute-start(bf16[576,128]{1,0:T(8,128)(2,1)S(1)} %get-tuple-element.50), channel_id=1, source_target_pairs={{0,12},{4,8},{8,4},{12,0},{16,28},{20,24},{24,20},{28,16},{1,13},{... | collective-permute-start | bytes 442376 | tf_op jit(solution)/shard_map/ppermute | solution.py:303
  30.1 9.8 %collective-permute-start.13 = (bf16[288,128]{1,0:T(8,128)(2,1)S(1)}, bf16[288,128]{1,0:T(8,128)(2,1)S(1)}, u32[]{:S(2)}, u32[]{:S(2)}) collective-permute-start(bf16[288,128]{1,0:T(8,128)(2,1)S(1)} %get-tuple-element.45), channel_id=1, source_target_pairs={{0,16},{4,20},{8,24},{12,28},{16,0},{20,4},{24,8},{28,12},{1,17},{... | collective-permute-start | bytes 221192 | tf_op jit(solution)/shard_map/ppermute | solution.py:303
  32.7 7.1 %collective-permute-start.14 = (bf16[288,128]{1,0:T(8,128)(2,1)S(1)}, bf16[288,128]{1,0:T(8,128)(2,1)S(1)}, u32[]{:S(2)}, u32[]{:S(2)}) collective-permute-start(bf16[288,128]{1,0:T(8,128)(2,1)S(1)} %get-tuple-element.46), channel_id=1, source_target_pairs={{0,18},{1,19},{2,16},{3,17},{4,22},{5,23},{6,20},{7,21},{8,26},{9,... | collective-permute-start | bytes 221192 | tf_op jit(solution)/shard_map/ppermute | solution.py:309

commit v3 on v2

--- a/solution.py
+++ b/solution.py
@@ -221,8 +221,10 @@
     if first:
         out.append(jax.ShapeDtypeStruct((blocks * 2 * s.part, LANES), F32))
     else:
-        out.append(jax.ShapeDtypeStruct((2 * s.part, LANES), F32))
-        out += [jax.ShapeDtypeStruct((2 * s.part, LANES), BF16)] * (blocks - 1)
+        out += [
+            jax.ShapeDtypeStruct((2 * s.part, LANES), BF16 if i % 2 else F32)
+            for i in range(blocks)
+        ]
     operands = list(qg) + list(kv) + ([] if first else [old])
     pairs = s.heads * s.span * blocks * s.rows
     result = pl.pallas_call(
@@ -239,7 +241,7 @@
         ],
         compiler_params=pltpu.CompilerParams(vmem_limit_bytes=s.grant(blocks)),
         cost_estimate=pl.CostEstimate(
-            flops=200 * pairs * s.dim, bytes_accessed=4 * s.part * LANES * 8, transcendentals=pairs
+            flops=20 * pairs * s.dim, bytes_accessed=4 * s.part * LANES * 8, transcendentals=pairs
         ),
     )(*operands)
     count = s.group // 2
@@ -269,11 +271,40 @@
     )(*keep, recv)
 
 
-def final_kernel(s, n_dq, n_kv, *refs):
-    dq, kv = refs[:n_dq], refs[n_dq : n_dq + n_kv]
-    outs = refs[n_dq + n_kv :]
+def sum_kernel(*refs):
+    total = refs[0][...].astype(F32)
+    for ref in refs[1:-1]:
+        total = total + ref[...].astype(F32)
+    refs[-1][...] = total.astype(refs[-1].dtype)
+
+
+def sum_low(arrays):
+    if len(arrays) == 1:
+        return arrays[0] if arrays[0].dtype == BF16 else arrays[0].astype(BF16)
+    return pl.pallas_call(
+        sum_kernel,
+        out_shape=jax.ShapeDtypeStruct(arrays[0].shape, BF16),
+        in_specs=[VMEM] * len(arrays),
+        out_specs=VMEM,
+        compiler_params=pltpu.CompilerParams(vmem_limit_bytes=2**20),
+    )(*arrays)
+
+
+def sum_all(s, arrays):
+    return pl.pallas_call(
+        sum_kernel,
+        out_shape=jax.ShapeDtypeStruct(arrays[0].shape, F32),
+        in_specs=[VMEM] * len(arrays),
+        out_specs=VMEM,
+        compiler_params=pltpu.CompilerParams(vmem_limit_bytes=2**20),
+        cost_estimate=pl.CostEstimate(flops=10**10, bytes_accessed=0, transcendentals=0),
+    )(*arrays)
+
+
+def final_kernel(s, count, *refs):
+    dq, kv, outs = refs[0], refs[1 : count + 1], refs[count + 1 :]
     r = s.rows
-    for out, sources, base in ((outs[0], dq, 0), (outs[1], kv, 0), (outs[2], kv, s.part)):
+    for out, sources, base in ((outs[0], [dq], 0), (outs[1], kv, 0), (outs[2], kv, s.part)):
         for t in range(s.tiles):
             rows = slice(base + t * r, base + (t + 1) * r)
             total = sources[0][rows, :].astype(F32)
@@ -284,12 +315,12 @@
 
 def finish(s, dq, kv):
     return pl.pallas_call(
-        functools.partial(final_kernel, s, len(dq), len(kv)),
+        functools.partial(final_kernel, s, len(kv)),
         out_shape=[jax.ShapeDtypeStruct((s.rows, s.width), BF16)] * 3,
-        in_specs=[VMEM] * (len(dq) + len(kv)),
+        in_specs=[VMEM] * (len(kv) + 1),
         out_specs=[VMEM] * 3,
         compiler_params=pltpu.CompilerParams(vmem_limit_bytes=2**20),
-    )(*dq, *kv)
+    )(dq, *kv)
 
 
 def local(queries, keys, values, attended, grad_out, logsumexp):
@@ -330,12 +361,21 @@
     keep0, send0, sums0, far = tie((keep0, send0, sums0, far))
     far[group // 2 + 1] = move(far[group // 2], 0, 1)
     keep1, send1, sums1 = attend(s, [far[i] for i in range(group)], kv, sums0[0])
+    dq = core_add(s, keep1, move(send1, 0, 1), False)
+    total_q = [move(dq[i], s.high, 2 * i) for i in range(group // 2)]
     dq = core_add(s, keep0, move(send0, 0, 1), True)
-    total_q = [dq[0]] + [move(dq[i], 0, 2 * i) for i in range(1, group // 2)]
-    dq = core_add(s, keep1, move(send1, 0, 1), False)
-    total_q += [move(dq[i], s.high, 2 * i) for i in range(group // 2)]
-    total_kv = [sums1[0]] + [move(sums1[off], off, 0) for off in range(1, s.high)]
-    return tuple(finish(s, total_q, total_kv))
+    total_q += [dq[0]] + [move(dq[i], 0, 2 * i) for i in range(1, group // 2)]
+    parts = {off: [sums1[off]] for off in range(s.high)}
+    for bit in reversed(bits):
+        others = [off for off in range(s.high) if off & (2 * bit - 1) == bit and off != bit]
+        for off in others:
+            parts[off - bit].append(move(sum_low(parts[off]), bit, 0))
+        last = sum_low(parts[bit])
+        if others:
+            last, parts[others[0] - bit] = tie((last, parts[others[0] - bit]))
+        parts[0].append(move(last, bit, 0))
+    total_q = sum_all(s, total_q)
+    return tuple(finish(s, total_q, parts[0]))
 
 
 def solution(mesh):

time: 40.9 us -> 39.4 us (0.963)
  waiting for transfers between devices: 13.4 us -> 12.3 us
    ppermute x8, waiting for transfers between devices: 11.9 us -> 6.03 us  [move(): return lax.ppermute(x, 'ctx', [(i, i ^ ctx_off) for i in range(ctx)])]
    ppermute x1, waiting for transfers between devices: 0.01 us -> 3.96 us  [move(): return lax.ppermute(x, ('ctx', 'head'), pairs)]
    ppermute x1, starting transfers between devices: 0.66 us -> 3.51 us  [move(): return lax.ppermute(x, ('ctx', 'head'), pairs)]
    ppermute x8, starting transfers between devices: 13.3 us -> 10.8 us  [move(): return lax.ppermute(x, 'ctx', [(i, i ^ ctx_off) for i in range(ctx)])]
    ppermute x9, waiting for transfers between devices: 1.54 us -> 2.3 us  [move(): return lax.ppermute(x, 'head', [(i, i ^ head_off) for i in range(group)])]
    ppermute x9, starting transfers between devices: 6 us -> 5.39 us  [move(): return lax.ppermute(x, 'head', [(i, i ^ head_off) for i in range(group)])]
  transfers between devices with their start and end apart: 18 -> 18, of which waited for: 7 -> 8; matrix products, arithmetic and copies ran while one was open for 0% -> 0% of each run, Pallas kernels for 11% -> 12%
where the time goes in v3:
time: 39.4 us; the launch traced here: 39.2 us
  starting transfers between devices  19.7 us (50%)
  waiting for transfers between devices  12.3 us (31%)
  Pallas kernels  6.58 us (17%)
  between operations  0.69 us (2%)
    ppermute x8, starting transfers between devices, move(): return lax.ppermute(x, 'ctx', [(i, i ^ ctx_off) for i in range(ctx)])  10.8 us
    ppermute x8, waiting for transfers between devices, move(): return lax.ppermute(x, 'ctx', [(i, i ^ ctx_off) for i in range(ctx)])  6.03 us
    ppermute x9, starting transfers between devices, move(): return lax.ppermute(x, 'head', [(i, i ^ head_off) for i in range(group)])  5.39 us
    pallas_call x2, Pallas kernels, attend(): pl.pallas_call(functools.partial(attend_kernel, s, blocks, first), out_sh...  4.52 us
    ppermute x1, waiting for transfers between devices, move(): return lax.ppermute(x, ('ctx', 'head'), pairs)  3.96 us
    ppermute x1, starting transfers between devices, move(): return lax.ppermute(x, ('ctx', 'head'), pairs)  3.51 us
    ppermute x9, waiting for transfers between devices, move(): return lax.ppermute(x, 'head', [(i, i ^ head_off) for i in range(group)])  2.3 us
    pallas_call x1, Pallas kernels, pack(): pl.pallas_call(functools.partial(pack_kernel, s), out_shape=(jax.ShapeDty...  1.21 us
  transfers between devices with their start and end apart: 18, of which 8 were waited for; matrix products, arithmetic and copies ran while one was open for 0% of the time, Pallas kernels for 12%

profile of v3, /device:TPU:0, one launch (start us, length us, event | category | flops | bytes accessed | tf_op | source)
XLA Modules:
  0.0 39.2 jit_solution(5900877217097364105)
XLA Ops:
  0.6 1.2 %shard_map.85 = (bf16[624,128]{1,0:T(8,128)(2,1)S(1)}, bf16[576,128]{1,0:T(8,128)(2,1)S(1)}) custom-call(bf16[48,768]{1,0:T(8,128)(2,1)} %q_in.1, bf16[48,768]{1,0:T(8,128)(2,1)} %k_in.1, bf16[48,768]{1,0:T(8,128)(2,1)} %v_in.1, bf16[48,768]{1,0:T(8,128)(2,1)} %o_in.1, bf16[48,768]{1,0:T(8,128)(2,1)} %g_in.1, f32[3,192]{1,0:T(4,128)} %bitcast.1), custom_call_target="tpu_custom_call" | custom-call | tf_op jit(solution)/shard_map/pallas_call | solution.py:111
  1.9 3.0 %collective-permute-start.1 = (bf16[624,128]{1,0:T(8,128)(2,1)S(1)}, bf16[624,128]{1,0:T(8,128)(2,1)S(1)}, u32[]{:S(2)}, u32[]{:S(2)}) collective-permute-start(bf16[624,128]{1,0:T(8,128)(2,1)S(1)} %get-tuple-element.30.refs_0_), channel_id=1, source_target_pairs={{0,2},{1,3},{2,0},{3,1},{4,6},{5,7},{6,4},{7,5},{8,10},{9,11},{10,... | collective-permute-start | bytes 479240 | tf_op jit(solution)/shard_map/ppermute | solution.py:332
  4.9 1.6 %collective-permute-start.4 = (bf16[576,128]{1,0:T(8,128)(2,1)S(1)}, bf16[576,128]{1,0:T(8,128)(2,1)S(1)}, u32[]{:S(2)}, u32[]{:S(2)}) collective-permute-start(bf16[576,128]{1,0:T(8,128)(2,1)S(1)} %get-tuple-element.31.refs_4_), channel_id=1, source_target_pairs={{0,8},{4,12},{8,0},{12,4},{16,24},{20,28},{24,16},{28,20},{1,9},{5... | collective-permute-start | bytes 442376 | tf_op jit(solution)/shard_map/ppermute | solution.py:334
  6.5 2.6 %collective-permute-start.6 = (bf16[624,128]{1,0:T(8,128)(2,1)S(1)}, bf16[624,128]{1,0:T(8,128)(2,1)S(1)}, u32[]{:S(2)}, u32[]{:S(2)}) collective-permute-start(bf16[624,128]{1,0:T(8,128)(2,1)S(1)} %get-tuple-element.30.refs_0_), channel_id=1, source_target_pairs={{0,16},{4,20},{8,24},{12,28},{16,0},{20,4},{24,8},{28,12},{1,17},{... | collective-permute-start | bytes 479240 | tf_op jit(solution)/shard_map/ppermute | solution.py:334
  9.1 1.5 %collective-permute-start.3 = (bf16[576,128]{1,0:T(8,128)(2,1)S(1)}, bf16[576,128]{1,0:T(8,128)(2,1)S(1)}, u32[]{:S(2)}, u32[]{:S(2)}) collective-permute-start(bf16[576,128]{1,0:T(8,128)(2,1)S(1)} %get-tuple-element.31.refs_4_), channel_id=1, source_target_pairs={{0,4},{4,0},{8,12},{12,8},{16,20},{20,16},{24,28},{28,24},{1,5},{5... | collective-permute-start | bytes 442376 | tf_op jit(solution)/shard_map/ppermute | solution.py:334
  10.5 0.5 %collective-permute-start.2 = (bf16[624,128]{1,0:T(8,128)(2,1)S(1)}, bf16[624,128]{1,0:T(8,128)(2,1)S(1)}, u32[]{:S(2)}, u32[]{:S(2)}) collective-permute-start(bf16[624,128]{1,0:T(8,128)(2,1)S(1)} %collective-permute-done.1.refs_2_), channel_id=1, source_target_pairs={{0,1},{1,0},{2,3},{3,2},{4,5},{5,4},{6,7},{7,6},{8,9},{9,8},{10,11... | collective-permute-start | bytes 479240 | tf_op jit(solution)/shard_map/ppermute | solution.py:332
  11.1 1.5 %collective-permute-done.4.refs_6_ = bf16[576,128]{1,0:T(8,128)(2,1)S(1)} collective-permute-done((bf16[576,128]{1,0:T(8,128)(2,1)S(1)}, bf16[576,128]{1,0:T(8,128)(2,1)S(1)}, u32[]{:S(2)}, u32[]{:S(2)}) %collective-permute-start.4) | collective-permute-done | bytes 147488 | tf_op jit(solution)/shard_map/ppermute | solution.py:334
  12.6 1.5 %collective-permute-start.5 = (bf16[576,128]{1,0:T(8,128)(2,1)S(1)}, bf16[576,128]{1,0:T(8,128)(2,1)S(1)}, u32[]{:S(2)}, u32[]{:S(2)}) collective-permute-start(bf16[576,128]{1,0:T(8,128)(2,1)S(1)} %collective-permute-done.4.refs_6_), channel_id=1, source_target_pairs={{0,4},{4,0},{8,12},{12,8},{16,20},{20,16},{24,28},{28,24},{1,5},{5... | collective-permute-start | bytes 442376 | tf_op jit(solution)/shard_map/ppermute | solution.py:334
  14.1 2.0 %collective-permute-done.6.refs_0_ = bf16[624,128]{1,0:T(8,128)(2,1)S(1)} collective-permute-done((bf16[624,128]{1,0:T(8,128)(2,1)S(1)}, bf16[624,128]{1,0:T(8,128)(2,1)S(1)}, u32[]{:S(2)}, u32[]{:S(2)}) %collective-permute-start.6) | collective-permute-done | bytes 159776 | tf_op jit(solution)/shard_map/ppermute | solution.py:334
  16.1 0.5 %collective-permute-start.8 = (bf16[624,128]{1,0:T(8,128)(2,1)S(1)}, bf16[624,128]{1,0:T(8,128)(2,1)S(1)}, u32[]{:S(2)}, u32[]{:S(2)}) collective-permute-start(bf16[624,128]{1,0:T(8,128)(2,1)S(1)} %collective-permute-done.6.refs_0_), channel_id=1, source_target_pairs={{0,2},{1,3},{2,0},{3,1},{4,6},{5,7},{6,4},{7,5},{8,10},{9,11},{10,... | collective-permute-start | bytes 479240 | tf_op jit(solution)/shard_map/ppermute | solution.py:332
  16.6 0.0 collective-permute-done.3.refs_5_
  16.6 0.0 collective-permute-start.7
  16.6 1.1 %collective-permute-done.5.refs_7_ = bf16[576,128]{1,0:T(8,128)(2,1)S(1)} collective-permute-done((bf16[576,128]{1,0:T(8,128)(2,1)S(1)}, bf16[576,128]{1,0:T(8,128)(2,1)S(1)}, u32[]{:S(2)}, u32[]{:S(2)}) %collective-permute-start.5) | collective-permute-done | bytes 147488 | tf_op jit(solution)/shard_map/ppermute | solution.py:334
  17.7 0.0 collective-permute-done.2.refs_3_
  17.7 2.3 %shard_map.86 = (f32[288,128]{1,0:T(8,128)S(1)}, f32[288,128]{1,0:T(8,128)S(1)}, bf16[576,128]{1,0:T(8,128)(2,1)S(1)}, f32[2304,128]{1,0:T(8,128)S(1)}) custom-call(bf16[624,128]{1,0:T(8,128)(2,1)S(1)} %get-tuple-element.30.refs_0_, bf16[624,128]{1,0:T(8,128)(2,1)S(1)} %collective-permute-done.refs_1_, bf16[624,128]{1,0:T(8,128)(2,1)S(1)} %collective-permute-done.1.refs_2_, ...), custom_call_target="tpu_custom_call" | custom-call | flops 566231040 | bytes 1179648 | tf_op jit(solution)/shard_map/pallas_call | solution.py:230
  20.0 1.4 %collective-permute-done.8.refs_2_ = bf16[624,128]{1,0:T(8,128)(2,1)S(1)} collective-permute-done((bf16[624,128]{1,0:T(8,128)(2,1)S(1)}, bf16[624,128]{1,0:T(8,128)(2,1)S(1)}, u32[]{:S(2)}, u32[]{:S(2)}) %collective-permute-start.8) | collective-permute-done | bytes 159776 | tf_op jit(solution)/shard_map/ppermute | solution.py:332
  21.4 0.0 collective-permute-done.7.refs_1_
  21.4 0.5 %collective-permute-start.13 = (bf16[576,128]{1,0:T(8,128)(2,1)S(1)}, bf16[576,128]{1,0:T(8,128)(2,1)S(1)}, u32[]{:S(2)}, u32[]{:S(2)}) collective-permute-start(bf16[576,128]{1,0:T(8,128)(2,1)S(1)} %get-tuple-element.47), channel_id=1, source_target_pairs={{0,1},{1,0},{2,3},{3,2},{4,5},{5,4},{6,7},{7,6},{8,9},{9,8},{10,11... | collective-permute-start | bytes 442376 | tf_op jit(solution)/shard_map/ppermute | solution.py:332
  21.9 0.9 %collective-permute-done.9.refs_3_ = bf16[624,128]{1,0:T(8,128)(2,1)S(1)} collective-permute-done((bf16[624,128]{1,0:T(8,128)(2,1)S(1)}, bf16[624,128]{1,0:T(8,128)(2,1)S(1)}, u32[]{:S(2)}, u32[]{:S(2)}) %collective-permute-start.9) | collective-permute-done | bytes 159776 | tf_op jit(solution)/shard_map/ppermute | solution.py:332
  22.8 2.3 %shard_map.87 = (f32[288,128]{1,0:T(8,128)S(1)}, f32[288,128]{1,0:T(8,128)S(1)}, bf16[576,128]{1,0:T(8,128)(2,1)S(1)}, f32[576,128]{1,0:T(8,128)S(1)}, bf16[576,...) custom-call(bf16[624,128]{1,0:T(8,128)(2,1)S(1)} %collective-permute-done.6.refs_0_, ...), custom_call_target="tpu_custom_call" | custom-call | flops 566231040 | bytes 1179648 | tf_op jit(solution)/shard_map/pallas_call | solution.py:230
  25.1 0.2 collective-permute-start.10
  25.3 1.5 %collective-permute-start.15 = (bf16[576,128]{1,0:T(8,128)(2,1)S(1)}, bf16[576,128]{1,0:T(8,128)(2,1)S(1)}, u32[]{:S(2)}, u32[]{:S(2)}) collective-permute-start(bf16[576,128]{1,0:T(8,128)(2,1)S(1)} %get-tuple-element.53), channel_id=1, source_target_pairs={{0,4},{4,0},{8,12},{12,8},{16,20},{20,16},{24,28},{28,24},{1,5},{5... | collective-permute-start | bytes 442376 | tf_op jit(solution)/shard_map/ppermute | solution.py:334
  26.8 0.6 %collective-permute-start.14 = (bf16[288,128]{1,0:T(8,128)(2,1)S(1)}, bf16[288,128]{1,0:T(8,128)(2,1)S(1)}, u32[]{:S(2)}, u32[]{:S(2)}) collective-permute-start(bf16[288,128]{1,0:T(8,128)(2,1)S(1)} %get-tuple-element.49), channel_id=1, source_target_pairs={{0,2},{1,3},{2,0},{3,1},{4,6},{5,7},{6,4},{7,5},{8,10},{9,11},{10,... | collective-permute-start | bytes 221192 | tf_op jit(solution)/shard_map/ppermute | solution.py:332
  27.5 0.4 %collective-permute-start.11 = (bf16[288,128]{1,0:T(8,128)(2,1)S(1)}, bf16[288,128]{1,0:T(8,128)(2,1)S(1)}, u32[]{:S(2)}, u32[]{:S(2)}) collective-permute-start(bf16[288,128]{1,0:T(8,128)(2,1)S(1)} %get-tuple-element.43), channel_id=1, source_target_pairs={{0,16},{4,20},{8,24},{12,28},{16,0},{20,4},{24,8},{28,12},{1,17},{... | collective-permute-start | bytes 221192 | tf_op jit(solution)/shard_map/ppermute | solution.py:334
  27.9 3.5 %collective-permute-start.12 = (bf16[288,128]{1,0:T(8,128)(2,1)S(1)}, bf16[288,128]{1,0:T(8,128)(2,1)S(1)}, u32[]{:S(2)}, u32[]{:S(2)}) collective-permute-start(bf16[288,128]{1,0:T(8,128)(2,1)S(1)} %get-tuple-element.44), channel_id=1, source_target_pairs={{0,18},{1,19},{2,16},{3,17},{4,22},{5,23},{6,20},{7,21},{8,26},{9,... | collective-permute-start | bytes 221192 | tf_op jit(solution)/shard_map/ppermute | solution.py:340
  31.4 0.0 collective-permute-done.15.refs_1_
  31.4 0.3 collective-permute-start.17
  31.7 1.5 %collective-permute-start.16 = (bf16[576,128]{1,0:T(8,128)(2,1)S(1)}, bf16[576,128]{1,0:T(8,128)(2,1)S(1)}, u32[]{:S(2)}, u32[]{:S(2)}) collective-permute-start(bf16[576,128]{1,0:T(8,128)(2,1)S(1)} %get-tuple-element.54), channel_id=1, source_target_pairs={{0,4},{4,0},{8,12},{12,8},{16,20},{20,16},{24,28},{28,24},{1,5},{5... | collective-permute-start | bytes 442376 | tf_op jit(solution)/shard_map/ppermute | solution.py:334
  33.2 0.8 %collective-permute-done.11.refs_0_ = bf16[288,128]{1,0:T(8,128)(2,1)S(1)} collective-permute-done((bf16[288,128]{1,0:T(8,128)(2,1)S(1)}, bf16[288,128]{1,0:T(8,128)(2,1)S(1)}, u32[]{:S(2)}, u32[]{:S(2)}) %collective-permute-start.11) | collective-permute-done | bytes 73760 | tf_op jit(solution)/shard_map/ppermute | solution.py:334
  34.0 4.0 %collective-permute-done.12.refs_1_ = bf16[288,128]{1,0:T(8,128)(2,1)S(1)} collective-permute-done((bf16[288,128]{1,0:T(8,128)(2,1)S(1)}, bf16[288,128]{1,0:T(8,128)(2,1)S(1)}, u32[]{:S(2)}, u32[]{:S(2)}) %collective-permute-start.12) | collective-permute-done | bytes 73760 | tf_op jit(solution)/shard_map/ppermute | solution.py:340
  38.0 0.5 %collective-permute-done.17.refs_3_ = bf16[576,128]{1,0:T(8,128)(2,1)S(1)} collective-permute-done((bf16[576,128]{1,0:T(8,128)(2,1)S(1)}, bf16[576,128]{1,0:T(8,128)(2,1)S(1)}, u32[]{:S(2)}, u32[]{:S(2)}) %collective-permute-start.17) | collective-permute-done | bytes 147488 | tf_op jit(solution)/shard_map/ppermute | solution.py:334
  38.5 0.7 %shard_map.92 = (bf16[48,768]{1,0:T(8,128)(2,1)}, bf16[48,768]{1,0:T(8,128)(2,1)}, bf16[48,768]{1,0:T(8,128)(2,1)}) custom-call(f32[288,128]{1,0:T(8,128)S(1)} %shard_map.90.refs_0_, f32[576,128]{1,0:T(8,128)S(1)} %get-tuple-element.50.refs_1_, bf16[576,128]{1,0:T(8,128)(2,1)S(1)} %collective-permute-done.16.refs_2_, ...), custom_call_target="tpu_custom_call" | custom-call | tf_op jit(solution)/shard_map/pallas_call | solution.py:317
  (12 shorter events, 0.2 us)
Async XLA Ops:
  1.9 8.7 %collective-permute-start.1 = (bf16[624,128]{1,0:T(8,128)(2,1)S(1)}, bf16[624,128]{1,0:T(8,128)(2,1)S(1)}, u32[]{:S(2)}, u32[]{:S(2)}) collective-permute-start(bf16[624,128]{1,0:T(8,128)(2,1)S(1)} %get-tuple-element.30.refs_0_), channel_id=1, source_target_pairs={{0,2},{1,3},{2,0},{3,1},{4,6},{5,7},{6,4},{7,5},{8,10},{9,11},{10,... | collective-permute-start | bytes 479240 | tf_op jit(solution)/shard_map/ppermute | solution.py:332
  4.9 7.7 %collective-permute-start.4 = (bf16[576,128]{1,0:T(8,128)(2,1)S(1)}, bf16[576,128]{1,0:T(8,128)(2,1)S(1)}, u32[]{:S(2)}, u32[]{:S(2)}) collective-permute-start(bf16[576,128]{1,0:T(8,128)(2,1)S(1)} %get-tuple-element.31.refs_4_), channel_id=1, source_target_pairs={{0,8},{4,12},{8,0},{12,4},{16,24},{20,28},{24,16},{28,20},{1,9},{5... | collective-permute-start | bytes 442376 | tf_op jit(solution)/shard_map/ppermute | solution.py:334
  6.5 9.7 %collective-permute-start.6 = (bf16[624,128]{1,0:T(8,128)(2,1)S(1)}, bf16[624,128]{1,0:T(8,128)(2,1)S(1)}, u32[]{:S(2)}, u32[]{:S(2)}) collective-permute-start(bf16[624,128]{1,0:T(8,128)(2,1)S(1)} %get-tuple-element.30.refs_0_), channel_id=1, source_target_pairs={{0,16},{4,20},{8,24},{12,28},{16,0},{20,4},{24,8},{28,12},{1,17},{... | collective-permute-start | bytes 479240 | tf_op jit(solution)/shard_map/ppermute | solution.py:334
  9.1 7.6 %collective-permute-start.3 = (bf16[576,128]{1,0:T(8,128)(2,1)S(1)}, bf16[576,128]{1,0:T(8,128)(2,1)S(1)}, u32[]{:S(2)}, u32[]{:S(2)}) collective-permute-start(bf16[576,128]{1,0:T(8,128)(2,1)S(1)} %get-tuple-element.31.refs_4_), channel_id=1, source_target_pairs={{0,4},{4,0},{8,12},{12,8},{16,20},{20,16},{24,28},{28,24},{1,5},{5... | collective-permute-start | bytes 442376 | tf_op jit(solution)/shard_map/ppermute | solution.py:334
  10.5 6.1 %collective-permute-start = (bf16[624,128]{1,0:T(8,128)(2,1)S(1)}, bf16[624,128]{1,0:T(8,128)(2,1)S(1)}, u32[]{:S(2)}, u32[]{:S(2)}) collective-permute-start(bf16[624,128]{1,0:T(8,128)(2,1)S(1)} %get-tuple-element.30.refs_0_), channel_id=1, source_target_pairs={{0,1},{1,0},{2,3},{3,2},{4,5},{5,4},{6,7},{7,6},{8,9},{9,8},{10,11... | collective-permute-start | bytes 479240 | tf_op jit(solution)/shard_map/ppermute | solution.py:332
  10.5 7.2 %collective-permute-start.2 = (bf16[624,128]{1,0:T(8,128)(2,1)S(1)}, bf16[624,128]{1,0:T(8,128)(2,1)S(1)}, u32[]{:S(2)}, u32[]{:S(2)}) collective-permute-start(bf16[624,128]{1,0:T(8,128)(2,1)S(1)} %collective-permute-done.1.refs_2_), channel_id=1, source_target_pairs={{0,1},{1,0},{2,3},{3,2},{4,5},{5,4},{6,7},{7,6},{8,9},{9,8},{10,11... | collective-permute-start | bytes 479240 | tf_op jit(solution)/shard_map/ppermute | solution.py:332
  12.6 5.1 %collective-permute-start.5 = (bf16[576,128]{1,0:T(8,128)(2,1)S(1)}, bf16[576,128]{1,0:T(8,128)(2,1)S(1)}, u32[]{:S(2)}, u32[]{:S(2)}) collective-permute-start(bf16[576,128]{1,0:T(8,128)(2,1)S(1)} %collective-permute-done.4.refs_6_), channel_id=1, source_target_pairs={{0,4},{4,0},{8,12},{12,8},{16,20},{20,16},{24,28},{28,24},{1,5},{5... | collective-permute-start | bytes 442376 | tf_op jit(solution)/shard_map/ppermute | solution.py:334
  16.1 5.3 %collective-permute-start.8 = (bf16[624,128]{1,0:T(8,128)(2,1)S(1)}, bf16[624,128]{1,0:T(8,128)(2,1)S(1)}, u32[]{:S(2)}, u32[]{:S(2)}) collective-permute-start(bf16[624,128]{1,0:T(8,128)(2,1)S(1)} %collective-permute-done.6.refs_0_), channel_id=1, source_target_pairs={{0,2},{1,3},{2,0},{3,1},{4,6},{5,7},{6,4},{7,5},{8,10},{9,11},{10,... | collective-permute-start | bytes 479240 | tf_op jit(solution)/shard_map/ppermute | solution.py:332
  16.6 4.8 %collective-permute-start.7 = (bf16[624,128]{1,0:T(8,128)(2,1)S(1)}, bf16[624,128]{1,0:T(8,128)(2,1)S(1)}, u32[]{:S(2)}, u32[]{:S(2)}) collective-permute-start(bf16[624,128]{1,0:T(8,128)(2,1)S(1)} %collective-permute-done.6.refs_0_), channel_id=1, source_target_pairs={{0,1},{1,0},{2,3},{3,2},{4,5},{5,4},{6,7},{7,6},{8,9},{9,8},{10,11... | collective-permute-start | bytes 479240 | tf_op jit(solution)/shard_map/ppermute | solution.py:332
  21.4 1.4 %collective-permute-start.9 = (bf16[624,128]{1,0:T(8,128)(2,1)S(1)}, bf16[624,128]{1,0:T(8,128)(2,1)S(1)}, u32[]{:S(2)}, u32[]{:S(2)}) collective-permute-start(bf16[624,128]{1,0:T(8,128)(2,1)S(1)} %collective-permute-done.8.refs_2_), channel_id=1, source_target_pairs={{0,1},{1,0},{2,3},{3,2},{4,5},{5,4},{6,7},{7,6},{8,9},{9,8},{10,11... | collective-permute-start | bytes 479240 | tf_op jit(solution)/shard_map/ppermute | solution.py:332
  21.4 5.4 %collective-permute-start.13 = (bf16[576,128]{1,0:T(8,128)(2,1)S(1)}, bf16[576,128]{1,0:T(8,128)(2,1)S(1)}, u32[]{:S(2)}, u32[]{:S(2)}) collective-permute-start(bf16[576,128]{1,0:T(8,128)(2,1)S(1)} %get-tuple-element.47), channel_id=1, source_target_pairs={{0,1},{1,0},{2,3},{3,2},{4,5},{5,4},{6,7},{7,6},{8,9},{9,8},{10,11... | collective-permute-start | bytes 442376 | tf_op jit(solution)/shard_map/ppermute | solution.py:332
  25.1 2.4 %collective-permute-start.10 = (bf16[576,128]{1,0:T(8,128)(2,1)S(1)}, bf16[576,128]{1,0:T(8,128)(2,1)S(1)}, u32[]{:S(2)}, u32[]{:S(2)}) collective-permute-start(bf16[576,128]{1,0:T(8,128)(2,1)S(1)} %get-tuple-element.42), channel_id=1, source_target_pairs={{0,1},{1,0},{2,3},{3,2},{4,5},{5,4},{6,7},{7,6},{8,9},{9,8},{10,11... | collective-permute-start | bytes 442376 | tf_op jit(solution)/shard_map/ppermute | solution.py:332
  25.3 6.1 %collective-permute-start.15 = (bf16[576,128]{1,0:T(8,128)(2,1)S(1)}, bf16[576,128]{1,0:T(8,128)(2,1)S(1)}, u32[]{:S(2)}, u32[]{:S(2)}) collective-permute-start(bf16[576,128]{1,0:T(8,128)(2,1)S(1)} %get-tuple-element.53), channel_id=1, source_target_pairs={{0,4},{4,0},{8,12},{12,8},{16,20},{20,16},{24,28},{28,24},{1,5},{5... | collective-permute-start | bytes 442376 | tf_op jit(solution)/shard_map/ppermute | solution.py:334
  26.8 6.3 %collective-permute-start.14 = (bf16[288,128]{1,0:T(8,128)(2,1)S(1)}, bf16[288,128]{1,0:T(8,128)(2,1)S(1)}, u32[]{:S(2)}, u32[]{:S(2)}) collective-permute-start(bf16[288,128]{1,0:T(8,128)(2,1)S(1)} %get-tuple-element.49), channel_id=1, source_target_pairs={{0,2},{1,3},{2,0},{3,1},{4,6},{5,7},{6,4},{7,5},{8,10},{9,11},{10,... | collective-permute-start | bytes 221192 | tf_op jit(solution)/shard_map/ppermute | solution.py:332
  27.5 6.5 %collective-permute-start.11 = (bf16[288,128]{1,0:T(8,128)(2,1)S(1)}, bf16[288,128]{1,0:T(8,128)(2,1)S(1)}, u32[]{:S(2)}, u32[]{:S(2)}) collective-permute-start(bf16[288,128]{1,0:T(8,128)(2,1)S(1)} %get-tuple-element.43), channel_id=1, source_target_pairs={{0,16},{4,20},{8,24},{12,28},{16,0},{20,4},{24,8},{28,12},{1,17},{... | collective-permute-start | bytes 221192 | tf_op jit(solution)/shard_map/ppermute | solution.py:334
  27.9 10.1 %collective-permute-start.12 = (bf16[288,128]{1,0:T(8,128)(2,1)S(1)}, bf16[288,128]{1,0:T(8,128)(2,1)S(1)}, u32[]{:S(2)}, u32[]{:S(2)}) collective-permute-start(bf16[288,128]{1,0:T(8,128)(2,1)S(1)} %get-tuple-element.44), channel_id=1, source_target_pairs={{0,18},{1,19},{2,16},{3,17},{4,22},{5,23},{6,20},{7,21},{8,26},{9,... | collective-permute-start | bytes 221192 | tf_op jit(solution)/shard_map/ppermute | solution.py:340
  31.4 7.1 %collective-permute-start.17 = (bf16[576,128]{1,0:T(8,128)(2,1)S(1)}, bf16[576,128]{1,0:T(8,128)(2,1)S(1)}, u32[]{:S(2)}, u32[]{:S(2)}) collective-permute-start(bf16[576,128]{1,0:T(8,128)(2,1)S(1)} %shard_map.91), channel_id=1, source_target_pairs={{0,8},{4,12},{8,0},{12,4},{16,24},{20,28},{24,16},{28,20},{1,9},{5... | collective-permute-start | bytes 442376 | tf_op jit(solution)/shard_map/ppermute | solution.py:334
  31.7 6.8 %collective-permute-start.16 = (bf16[576,128]{1,0:T(8,128)(2,1)S(1)}, bf16[576,128]{1,0:T(8,128)(2,1)S(1)}, u32[]{:S(2)}, u32[]{:S(2)}) collective-permute-start(bf16[576,128]{1,0:T(8,128)(2,1)S(1)} %get-tuple-element.54), channel_id=1, source_target_pairs={{0,4},{4,0},{8,12},{12,8},{16,20},{20,16},{24,28},{28,24},{1,5},{5... | collective-permute-start | bytes 442376 | tf_op jit(solution)/shard_map/ppermute | solution.py:334

commit v4 on v3

--- a/solution.py
+++ b/solution.py
@@ -34,8 +34,8 @@
         self.span = rows * group
         self.span_tiles = -(-self.span // LANES)
         self.part = self.tiles * rows
-        self.lse_rows = 3 * heads_group * self.span_tiles
-        self.extra = round_up(self.lse_rows + 2 * self.heads, 16)
+        self.lse_rows = 2 * heads_group * self.span_tiles
+        self.extra = round_up(self.lse_rows + self.heads, 16)
         self.high = ctx // 2
 
     def grant(self, blocks):
@@ -44,15 +44,13 @@
         return 2 * scratch + 32 * pairs + 2**20
 
 
-def split3(x):
+def split2(x):
     hi = x.astype(BF16).astype(F32)
-    rest = x - hi
-    mid = rest.astype(BF16).astype(F32)
-    return hi, mid, rest - mid
+    return hi, x - hi
 
 
 def pack_kernel(s, q_in, k_in, v_in, o_in, g_in, lse_in, qg_ref, kv_ref, *scratch):
-    q_ref, k_ref, v_ref, o_ref, g_ref, lse_ref, small, sems = scratch
+    q_ref, k_ref, v_ref, o_ref, g_ref, lse_ref, small, side, sems = scratch
     copies = [
         pltpu.make_async_copy(source, target, sems.at[i])
         for i, (source, target) in enumerate(
@@ -78,18 +76,22 @@
     pick = lax.broadcasted_iota(jnp.int32, shape, 1) // s.dim
     pick = (pick == lax.broadcasted_iota(jnp.int32, shape, 0)).astype(F32).astype(BF16)
     delta = dot(pick, hi, NT) + dot(pick, lo, NT)
-    d_hi, d_mid, _ = split3(delta)
+    d_hi, d_low = split2(delta)
     small[...] = jnp.zeros(small.shape, F32)
+    side[...] = jnp.zeros(side.shape, F32)
+    side[:, :r] = d_low
+    d_low = pltpu.roll(side[...], LANES // 2, 1)
+    side[:, :r] = d_hi
+    deltas = side[...] + d_low
     copies[2].wait()
     h = s.heads_group
     at = 0
     for t in range(s.span_tiles):
         lanes = min(LANES, s.span - t * LANES)
-        for piece in split3(lse_ref[:, t * LANES : t * LANES + lanes]):
+        for piece in split2(lse_ref[:, t * LANES : t * LANES + lanes]):
             small[at : at + h, :lanes] = piece
             at += h
-    small[at : at + s.heads, :r] = d_hi[: s.heads]
-    small[at + s.heads : at + 2 * s.heads, :r] = d_mid[: s.heads]
+    small[at : at + s.heads, :] = deltas[: s.heads]
     qg_ref[2 * s.part :, :] = small[...].astype(BF16)
     for copy in copies[3:]:
         copy.wait()
@@ -120,6 +122,7 @@
         + [
             pltpu.VMEM((s.heads_group, s.span), F32),
             pltpu.VMEM((s.extra, LANES), F32),
+            pltpu.VMEM((round_up(s.heads, 16), LANES), F32),
             pltpu.SemaphoreType.DMA((6,)),
         ],
         compiler_params=pltpu.CompilerParams(vmem_limit_bytes=2 * 2**20),
@@ -140,6 +143,7 @@
     wide = s.span_tiles * LANES
     h = s.heads_group
     total = jnp.zeros((s.heads, wide), F32)
+    used = lax.broadcasted_iota(jnp.int32, (s.heads, LANES), 1) < r
     for off in range(n):
         who = lax.bitwise_xor(me, off)
         at = pl.multiple_of(who * r, 16)
@@ -150,11 +154,12 @@
         small = qg[off][2 * s.part :, :].astype(F32)
         pieces = []
         for t in range(s.span_tiles):
-            b = 3 * h * t
-            pieces.append(small[b : b + h] + small[b + h : b + 2 * h] + small[b + 2 * h : b + 3 * h])
+            b = 2 * h * t
+            pieces.append(small[b : b + h] + small[b + h : b + 2 * h])
         norms[who, :h, :] = jnp.concatenate(pieces, axis=1)
         b = s.lse_rows
-        delta = small[b : b + s.heads] + small[b + s.heads : b + 2 * s.heads]
+        delta = small[b : b + s.heads]
+        delta = jnp.where(used, delta + pltpu.roll(delta, LANES // 2, 1), 0.0)
         if wide > LANES:
             delta = jnp.concatenate([delta, jnp.zeros((s.heads, wide - LANES), F32)], axis=1)
         total = total + pltpu.roll(delta, who * r, 1)
@@ -169,14 +174,14 @@
     def pair(block):
         return jnp.where(own_lanes, jnp.concatenate([block, block], axis=0), zero)
 
-    for t in range(s.tiles):
+    def front(t):
         rows = slice(t * r, (t + 1) * r)
         more = slice(s.part + t * r, s.part + (t + 1) * r)
         k = pair(jnp.concatenate([ref[rows, :] for ref in kv], axis=0))
         v = pair(jnp.concatenate([ref[more, :] for ref in kv], axis=0))
-        q, g = qs[t], gs[t]
-        scores = dot(k, q, NT)
-        dweights = dot(v, g, NT)
+        return k, dot(k, qs[t], NT), dot(v, gs[t], NT)
+
+    def middle(t, scores, dweights):
         low, dscores = [], []
         for e in range(2):
             head = 2 * t + e
@@ -186,13 +191,15 @@
             low.append(weights.astype(BF16))
             gap = dweights[mine] - deltas[head : head + 1, : s.span]
             dscores.append((weights * gap).astype(BF16))
-        low = jnp.concatenate(low, axis=0)
-        dscores = jnp.concatenate(dscores, axis=0)
-        dv = dot(low, g, NN)
-        dk = dot(dscores, q, NN)
+        return jnp.concatenate(low, axis=0), jnp.concatenate(dscores, axis=0)
+
+    def back(t, k, low, dscores):
+        rows = slice(t * r, (t + 1) * r)
+        more = slice(s.part + t * r, s.part + (t + 1) * r)
+        dv = dot(low, gs[t], NN)
+        dk = dot(dscores, qs[t], NN)
         dv, dk = [dv[:size], dv[size:]], [dk[:size], dk[size:]]
-        dq = dot(dscores, k, TN)
-        dqs[t] = dq * scale
+        dqs[t] = dot(k, dscores, TN).T * scale
         for where, parts in ((rows, dk), (more, dv)):
             both = jnp.where(half, parts[0], parts[1])
             for i in range(blocks):
@@ -202,6 +209,13 @@
                 else:
                     piece = piece + old[2 * s.part * i + where.start : 2 * s.part * i + where.stop, :]
                     sums[i][where, :] = piece.astype(sums[i].dtype)
+
+    ahead = front(0)
+    for t in range(s.tiles):
+        k, scores, dweights = ahead
+        if t + 1 < s.tiles:
+            ahead = front(t + 1)
+        back(t, k, *middle(t, scores, dweights))
     for off in range(n):
         at = pl.multiple_of(lax.bitwise_xor(me, off) * r, 16)
         for t in range(s.tiles):
@@ -241,7 +255,7 @@
         ],
         compiler_params=pltpu.CompilerParams(vmem_limit_bytes=s.grant(blocks)),
         cost_estimate=pl.CostEstimate(
-            flops=20 * pairs * s.dim, bytes_accessed=4 * s.part * LANES * 8, transcendentals=pairs
+            flops=(20 if first else 200) * pairs * s.dim, bytes_accessed=4 * s.part * LANES * 8, transcendentals=pairs
         ),
     )(*operands)
     count = s.group // 2
@@ -297,14 +311,14 @@
         in_specs=[VMEM] * len(arrays),
         out_specs=VMEM,
         compiler_params=pltpu.CompilerParams(vmem_limit_bytes=2**20),
-        cost_estimate=pl.CostEstimate(flops=10**10, bytes_accessed=0, transcendentals=0),
+        cost_estimate=pl.CostEstimate(flops=4000000000, bytes_accessed=0, transcendentals=0),
     )(*arrays)
 
 
-def final_kernel(s, count, *refs):
-    dq, kv, outs = refs[0], refs[1 : count + 1], refs[count + 1 :]
+def final_kernel(s, n_dq, n_kv, *refs):
+    dq, kv, outs = refs[:n_dq], refs[n_dq : n_dq + n_kv], refs[n_dq + n_kv :]
     r = s.rows
-    for out, sources, base in ((outs[0], [dq], 0), (outs[1], kv, 0), (outs[2], kv, s.part)):
+    for out, sources, base in ((outs[0], dq, 0), (outs[1], kv, 0), (outs[2], kv, s.part)):
         for t in range(s.tiles):
             rows = slice(base + t * r, base + (t + 1) * r)
             total = sources[0][rows, :].astype(F32)
@@ -315,12 +329,24 @@
 
 def finish(s, dq, kv):
     return pl.pallas_call(
-        functools.partial(final_kernel, s, len(kv)),
+        functools.partial(final_kernel, s, len(dq), len(kv)),
         out_shape=[jax.ShapeDtypeStruct((s.rows, s.width), BF16)] * 3,
-        in_specs=[VMEM] * (len(kv) + 1),
+        in_specs=[VMEM] * (len(dq) + len(kv)),
         out_specs=[VMEM] * 3,
         compiler_params=pltpu.CompilerParams(vmem_limit_bytes=2**20),
-    )(dq, *kv)
+    )(*dq, *kv)
+
+
+def hold(x, flops):
+    return pl.pallas_call(
+        lambda ref, out: None,
+        out_shape=jax.ShapeDtypeStruct(x.shape, x.dtype),
+        in_specs=[VMEM],
+        out_specs=VMEM,
+        input_output_aliases={0: 0},
+        compiler_params=pltpu.CompilerParams(vmem_limit_bytes=2**20),
+        cost_estimate=pl.CostEstimate(flops=flops, bytes_accessed=0, transcendentals=0),
+    )(x)
 
 
 def local(queries, keys, values, attended, grad_out, logsumexp):
@@ -342,40 +368,46 @@
     tie = lax.optimization_barrier
     qg_own, kv_own = pack(s, queries, keys, values, attended, grad_out, logsumexp)
     bits = [1 << i for i in reversed(range(s.high.bit_length() - 1))]
-    far = {0: move(qg_own, s.high, 0)}
-    kv = {0: kv_own}
-    kv.update({bit: move(kv_own, bit, 0) for bit in bits})
-    near = {0: qg_own, group // 2: move(qg_own, 0, group // 2)}
+    side = group // 2
+    far, kv, near = {}, {0: kv_own}, {0: qg_own}
+    far[0] = move(qg_own, s.high, 0)
+    kv[bits[0]] = move(kv_own, bits[0], 0)
+    kv.update({bit: move(kv_own, bit, 0) for bit in bits[1:]})
+    near[side] = move(qg_own, 0, side)
+    kv[bits[0]] = hold(kv[bits[0]], 10000000000)
     for bit in bits:
         for off in sorted(off for off in kv if off % (2 * bit) == 0 and off):
             kv[off + bit] = move(kv[off], bit, 0)
-    bit = group // 2
+    far[side] = move(far[0], 0, side)
+    kv[s.high - 1] = hold(kv[s.high - 1], 3000000000)
+    bit = side
     while bit:
         for blocks in (far, near):
             for off in sorted(off for off in blocks if off % (2 * bit) == 0):
-                if off + bit not in blocks and not (blocks is far and bit == 1 and off == group // 2):
+                if off + bit not in blocks and not (blocks is far and bit == 1 and off == side):
                     blocks[off + bit] = move(blocks[off], 0, bit)
         bit //= 2
     kv = [kv[off] for off in range(s.high)]
     keep0, send0, sums0 = attend(s, [near[i] for i in range(group)], kv, None)
     keep0, send0, sums0, far = tie((keep0, send0, sums0, far))
-    far[group // 2 + 1] = move(far[group // 2], 0, 1)
+    far[side + 1] = move(far[side], 0, 1)
     keep1, send1, sums1 = attend(s, [far[i] for i in range(group)], kv, sums0[0])
+    sums1 = list(sums1)
     dq = core_add(s, keep1, move(send1, 0, 1), False)
-    total_q = [move(dq[i], s.high, 2 * i) for i in range(group // 2)]
+    total_q = [move(dq[i], s.high, 2 * i) for i in range(side)]
     dq = core_add(s, keep0, move(send0, 0, 1), True)
-    total_q += [dq[0]] + [move(dq[i], 0, 2 * i) for i in range(1, group // 2)]
+    late_q = [move(dq[i], 0, 2 * i) for i in range(1, side)]
+    late_q = total_q[1:] + late_q
+    total_q = total_q[:1]
+    total_q = [dq[0]] + total_q
     parts = {off: [sums1[off]] for off in range(s.high)}
     for bit in reversed(bits):
         others = [off for off in range(s.high) if off & (2 * bit - 1) == bit and off != bit]
         for off in others:
             parts[off - bit].append(move(sum_low(parts[off]), bit, 0))
-        last = sum_low(parts[bit])
-        if others:
-            last, parts[others[0] - bit] = tie((last, parts[others[0] - bit]))
-        parts[0].append(move(last, bit, 0))
+        parts[0].append(move(sum_low(parts[bit]), bit, 0))
     total_q = sum_all(s, total_q)
-    return tuple(finish(s, total_q, parts[0]))
+    return tuple(finish(s, [total_q] + late_q, parts[0]))
 
 
 def solution(mesh):

time: 39.4 us -> 38.2 us (0.970)
  waiting for transfers between devices: 12.3 us -> 11.2 us
  Pallas kernels: 6.58 us -> 5.74 us
  starting transfers between devices: 19.7 us -> 20.4 us
    ppermute x8, starting transfers between devices: 10.8 us -> 13.5 us  [move(): return lax.ppermute(x, 'ctx', [(i, i ^ ctx_off) for i in range(ctx)])]
    ppermute x1, starting transfers between devices: 3.51 us -> 1.31 us  [move(): return lax.ppermute(x, ('ctx', 'head'), pairs)]
    ppermute x1, waiting for transfers between devices: 3.96 us -> 1.97 us  [move(): return lax.ppermute(x, ('ctx', 'head'), pairs)]
    ppermute x8, waiting for transfers between devices: 6.03 us -> 7.83 us  [move(): return lax.ppermute(x, 'ctx', [(i, i ^ ctx_off) for i in range(ctx)])]
    ppermute x9, waiting for transfers between devices: 2.3 us -> 1.39 us  [move(): return lax.ppermute(x, 'head', [(i, i ^ head_off) for i in range(group)])]
    pallas_call x2, Pallas kernels: 4.52 us -> 3.64 us  [attend(): pl.pallas_call(functools.partial(attend_kernel, s, blocks, first), out_sh...]
  transfers between devices with their start and end apart: 18 -> 18, of which waited for: 8 -> 8; matrix products, arithmetic and copies ran while one was open for 0% -> 0% of each run, Pallas kernels for 12% -> 5%
where the time goes in v4:
time: 38.2 us; the launch traced here: 38.1 us
  starting transfers between devices  20.4 us (53%)
  waiting for transfers between devices  11.2 us (29%)
  Pallas kernels  5.74 us (15%)
  between operations  0.72 us (2%)
    ppermute x8, starting transfers between devices, move(): return lax.ppermute(x, 'ctx', [(i, i ^ ctx_off) for i in range(ctx)])  13.5 us
    ppermute x8, waiting for transfers between devices, move(): return lax.ppermute(x, 'ctx', [(i, i ^ ctx_off) for i in range(ctx)])  7.83 us
    ppermute x9, starting transfers between devices, move(): return lax.ppermute(x, 'head', [(i, i ^ head_off) for i in range(group)])  5.56 us
    pallas_call x2, Pallas kernels, attend(): pl.pallas_call(functools.partial(attend_kernel, s, blocks, first), out_sh...  3.64 us
    ppermute x1, waiting for transfers between devices, move(): return lax.ppermute(x, ('ctx', 'head'), pairs)  1.97 us
    ppermute x9, waiting for transfers between devices, move(): return lax.ppermute(x, 'head', [(i, i ^ head_off) for i in range(group)])  1.39 us
    ppermute x1, starting transfers between devices, move(): return lax.ppermute(x, ('ctx', 'head'), pairs)  1.31 us
    pallas_call x1, Pallas kernels, pack(): pl.pallas_call(functools.partial(pack_kernel, s), out_shape=(jax.ShapeDty...  1.28 us
  transfers between devices with their start and end apart: 18, of which 8 were waited for; matrix products, arithmetic and copies ran while one was open for 0% of the time, Pallas kernels for 5%

profile of v4, /device:TPU:0, one launch (start us, length us, event | category | flops | bytes accessed | tf_op | source)
XLA Modules:
  0.0 38.1 jit_solution(2267136534849505205)
XLA Ops:
  0.6 1.3 %shard_map.85 = (bf16[608,128]{1,0:T(8,128)(2,1)S(1)}, bf16[576,128]{1,0:T(8,128)(2,1)S(1)}) custom-call(bf16[48,768]{1,0:T(8,128)(2,1)} %q_in.1, bf16[48,768]{1,0:T(8,128)(2,1)} %k_in.1, bf16[48,768]{1,0:T(8,128)(2,1)} %v_in.1, bf16[48,768]{1,0:T(8,128)(2,1)} %o_in.1, bf16[48,768]{1,0:T(8,128)(2,1)} %g_in.1, f32[3,192]{1,0:T(4,128)} %bitcast.1), custom_call_target="tpu_custom_call" | custom-call | tf_op jit(solution)/shard_map/pallas_call | solution.py:113
  1.9 3.1 %collective-permute-start.4 = (bf16[576,128]{1,0:T(8,128)(2,1)S(1)}, bf16[576,128]{1,0:T(8,128)(2,1)S(1)}, u32[]{:S(2)}, u32[]{:S(2)}) collective-permute-start(bf16[576,128]{1,0:T(8,128)(2,1)S(1)} %get-tuple-element.28.refs_4_), channel_id=1, source_target_pairs={{0,8},{4,12},{8,0},{12,4},{16,24},{20,28},{24,16},{28,20},{1,9},{5... | collective-permute-start | bytes 442376 | tf_op jit(solution)/shard_map/ppermute | solution.py:360
  5.0 2.6 %collective-permute-start.6 = (bf16[608,128]{1,0:T(8,128)(2,1)S(1)}, bf16[608,128]{1,0:T(8,128)(2,1)S(1)}, u32[]{:S(2)}, u32[]{:S(2)}) collective-permute-start(bf16[608,128]{1,0:T(8,128)(2,1)S(1)} %get-tuple-element.27.refs_0_), channel_id=1, source_target_pairs={{0,16},{4,20},{8,24},{12,28},{16,0},{20,4},{24,8},{28,12},{1,17},{... | collective-permute-start | bytes 466952 | tf_op jit(solution)/shard_map/ppermute | solution.py:360
  7.6 1.5 %collective-permute-start.1 = (bf16[608,128]{1,0:T(8,128)(2,1)S(1)}, bf16[608,128]{1,0:T(8,128)(2,1)S(1)}, u32[]{:S(2)}, u32[]{:S(2)}) collective-permute-start(bf16[608,128]{1,0:T(8,128)(2,1)S(1)} %get-tuple-element.27.refs_0_), channel_id=1, source_target_pairs={{0,2},{1,3},{2,0},{3,1},{4,6},{5,7},{6,4},{7,5},{8,10},{9,11},{10,... | collective-permute-start | bytes 466952 | tf_op jit(solution)/shard_map/ppermute | solution.py:358
  9.1 2.3 %collective-permute-done.4.ref = bf16[576,128]{1,0:T(8,128)(2,1)S(1)} collective-permute-done((bf16[576,128]{1,0:T(8,128)(2,1)S(1)}, bf16[576,128]{1,0:T(8,128)(2,1)S(1)}, u32[]{:S(2)}, u32[]{:S(2)}) %collective-permute-start.4) | collective-permute-done | bytes 147488 | tf_op jit(solution)/shard_map/ppermute | solution.py:360
  11.4 1.8 %collective-permute-start.5 = (bf16[576,128]{1,0:T(8,128)(2,1)S(1)}, bf16[576,128]{1,0:T(8,128)(2,1)S(1)}, u32[]{:S(2)}, u32[]{:S(2)}) collective-permute-start(bf16[576,128]{1,0:T(8,128)(2,1)S(1)} %shard_map.86.refs_6_), channel_id=1, source_target_pairs={{0,4},{4,0},{8,12},{12,8},{16,20},{20,16},{24,28},{28,24},{1,5},{5... | collective-permute-start | bytes 442376 | tf_op jit(solution)/shard_map/ppermute | solution.py:360
  13.2 0.2 collective-permute-start.3
  13.4 0.0 collective-permute-start
  13.4 1.3 %collective-permute-done.6.refs_0_ = bf16[608,128]{1,0:T(8,128)(2,1)S(1)} collective-permute-done((bf16[608,128]{1,0:T(8,128)(2,1)S(1)}, bf16[608,128]{1,0:T(8,128)(2,1)S(1)}, u32[]{:S(2)}, u32[]{:S(2)}) %collective-permute-start.6) | collective-permute-done | bytes 155680 | tf_op jit(solution)/shard_map/ppermute | solution.py:360
  14.8 1.5 %collective-permute-start.8 = (bf16[608,128]{1,0:T(8,128)(2,1)S(1)}, bf16[608,128]{1,0:T(8,128)(2,1)S(1)}, u32[]{:S(2)}, u32[]{:S(2)}) collective-permute-start(bf16[608,128]{1,0:T(8,128)(2,1)S(1)} %collective-permute-done.6.refs_0_), channel_id=1, source_target_pairs={{0,2},{1,3},{2,0},{3,1},{4,6},{5,7},{6,4},{7,5},{8,10},{9,11},{10,... | collective-permute-start | bytes 466952 | tf_op jit(solution)/shard_map/ppermute | solution.py:358
  16.3 0.0 collective-permute-start.7
  16.3 0.2 collective-permute-done.5.ref
  16.6 0.3 collective-permute-start.2
  16.8 1.6 %collective-permute-done.3.refs_5_ = bf16[576,128]{1,0:T(8,128)(2,1)S(1)} collective-permute-done((bf16[576,128]{1,0:T(8,128)(2,1)S(1)}, bf16[576,128]{1,0:T(8,128)(2,1)S(1)}, u32[]{:S(2)}, u32[]{:S(2)}) %collective-permute-start.3) | collective-permute-done | bytes 147488 | tf_op jit(solution)/shard_map/ppermute | solution.py:360
  18.4 0.0 collective-permute-done.refs_1_
  18.4 0.0 collective-permute-done.2.refs_3_
  18.4 1.8 %shard_map.88 = (f32[288,128]{1,0:T(8,128)S(1)}, f32[288,128]{1,0:T(8,128)S(1)}, bf16[576,128]{1,0:T(8,128)(2,1)S(1)}, f32[2304,128]{1,0:T(8,128)S(1)}) custom-call(bf16[608,128]{1,0:T(8,128)(2,1)S(1)} %get-tuple-element.27.refs_0_, bf16[608,128]{1,0:T(8,128)(2,1)S(1)} %collective-permute-done.refs_1_, bf16[608,128]{1,0:T(8,128)(2,1)S(1)} %collective-permute-done.1.refs_2_, ...), custom_call_target="tpu_custom_call" | custom-call | flops 566231040 | bytes 1179648 | tf_op jit(solution)/shard_map/pallas_call | solution.py:244
  20.2 0.1 collective-permute-start.10
  20.3 1.4 %collective-permute-done.10.refs_3_ = bf16[608,128]{1,0:T(8,128)(2,1)S(1)} collective-permute-done((bf16[608,128]{1,0:T(8,128)(2,1)S(1)}, bf16[608,128]{1,0:T(8,128)(2,1)S(1)}, u32[]{:S(2)}, u32[]{:S(2)}) %collective-permute-start.10) | collective-permute-done | bytes 155680 | tf_op jit(solution)/shard_map/ppermute | solution.py:358
  21.7 1.8 %shard_map.90 = (f32[288,128]{1,0:T(8,128)S(1)}, f32[288,128]{1,0:T(8,128)S(1)}, bf16[576,128]{1,0:T(8,128)(2,1)S(1)}, f32[576,128]{1,0:T(8,128)S(1)}, bf16[576,...) custom-call(bf16[608,128]{1,0:T(8,128)(2,1)S(1)} %collective-permute-done.6.refs_0_, ...), custom_call_target="tpu_custom_call" | custom-call | flops 5662310400 | bytes 1179648 | tf_op jit(solution)/shard_map/pallas_call | solution.py:244
  23.5 0.2 collective-permute-start.11
  23.7 0.4 collective-permute-start.9
  24.1 1.6 %collective-permute-start.16 = (bf16[576,128]{1,0:T(8,128)(2,1)S(1)}, bf16[576,128]{1,0:T(8,128)(2,1)S(1)}, u32[]{:S(2)}, u32[]{:S(2)}) collective-permute-start(bf16[576,128]{1,0:T(8,128)(2,1)S(1)} %get-tuple-element.50), channel_id=1, source_target_pairs={{0,4},{4,0},{8,12},{12,8},{16,20},{20,16},{24,28},{28,24},{1,5},{5... | collective-permute-start | bytes 442376 | tf_op jit(solution)/shard_map/ppermute | solution.py:360
  25.7 1.6 %collective-permute-start.12 = (bf16[288,128]{1,0:T(8,128)(2,1)S(1)}, bf16[288,128]{1,0:T(8,128)(2,1)S(1)}, u32[]{:S(2)}, u32[]{:S(2)}) collective-permute-start(bf16[288,128]{1,0:T(8,128)(2,1)S(1)} %get-tuple-element.44), channel_id=1, source_target_pairs={{0,16},{4,20},{8,24},{12,28},{16,0},{20,4},{24,8},{28,12},{1,17},{... | collective-permute-start | bytes 221192 | tf_op jit(solution)/shard_map/ppermute | solution.py:360
  27.3 1.6 %collective-permute-start.14 = (bf16[288,128]{1,0:T(8,128)(2,1)S(1)}, bf16[288,128]{1,0:T(8,128)(2,1)S(1)}, u32[]{:S(2)}, u32[]{:S(2)}) collective-permute-start(bf16[288,128]{1,0:T(8,128)(2,1)S(1)} %get-tuple-element.46), channel_id=1, source_target_pairs={{0,2},{1,3},{2,0},{3,1},{4,6},{5,7},{6,4},{7,5},{8,10},{9,11},{10,... | collective-permute-start | bytes 221192 | tf_op jit(solution)/shard_map/ppermute | solution.py:358
  28.9 0.9 %collective-permute-start.15 = (bf16[576,128]{1,0:T(8,128)(2,1)S(1)}, bf16[576,128]{1,0:T(8,128)(2,1)S(1)}, u32[]{:S(2)}, u32[]{:S(2)}) collective-permute-start(bf16[576,128]{1,0:T(8,128)(2,1)S(1)} %get-tuple-element.48), channel_id=1, source_target_pairs={{0,4},{4,0},{8,12},{12,8},{16,20},{20,16},{24,28},{28,24},{1,5},{5... | collective-permute-start | bytes 442376 | tf_op jit(solution)/shard_map/ppermute | solution.py:360
  29.8 1.3 %collective-permute-start.13 = (bf16[288,128]{1,0:T(8,128)(2,1)S(1)}, bf16[288,128]{1,0:T(8,128)(2,1)S(1)}, u32[]{:S(2)}, u32[]{:S(2)}) collective-permute-start(bf16[288,128]{1,0:T(8,128)(2,1)S(1)} %get-tuple-element.45), channel_id=1, source_target_pairs={{0,18},{1,19},{2,16},{3,17},{4,22},{5,23},{6,20},{7,21},{8,26},{9,... | collective-permute-start | bytes 221192 | tf_op jit(solution)/shard_map/ppermute | solution.py:366
  31.1 1.8 %collective-permute-start.17 = (bf16[576,128]{1,0:T(8,128)(2,1)S(1)}, bf16[576,128]{1,0:T(8,128)(2,1)S(1)}, u32[]{:S(2)}, u32[]{:S(2)}) collective-permute-start(bf16[576,128]{1,0:T(8,128)(2,1)S(1)} %shard_map.93), channel_id=1, source_target_pairs={{0,8},{4,12},{8,0},{12,4},{16,24},{20,28},{24,16},{28,20},{1,9},{5... | collective-permute-start | bytes 442376 | tf_op jit(solution)/shard_map/ppermute | solution.py:360
  33.0 1.1 %collective-permute-done.15.refs_4_ = bf16[576,128]{1,0:T(8,128)(2,1)S(1)} collective-permute-done((bf16[576,128]{1,0:T(8,128)(2,1)S(1)}, bf16[576,128]{1,0:T(8,128)(2,1)S(1)}, u32[]{:S(2)}, u32[]{:S(2)}) %collective-permute-start.15) | collective-permute-done | bytes 147488 | tf_op jit(solution)/shard_map/ppermute | solution.py:360
  34.1 2.0 %collective-permute-done.13.refs_1_ = bf16[288,128]{1,0:T(8,128)(2,1)S(1)} collective-permute-done((bf16[288,128]{1,0:T(8,128)(2,1)S(1)}, bf16[288,128]{1,0:T(8,128)(2,1)S(1)}, u32[]{:S(2)}, u32[]{:S(2)}) %collective-permute-start.13) | collective-permute-done | bytes 73760 | tf_op jit(solution)/shard_map/ppermute | solution.py:366
  36.1 1.3 %collective-permute-done.17.refs_5_ = bf16[576,128]{1,0:T(8,128)(2,1)S(1)} collective-permute-done((bf16[576,128]{1,0:T(8,128)(2,1)S(1)}, bf16[576,128]{1,0:T(8,128)(2,1)S(1)}, u32[]{:S(2)}, u32[]{:S(2)}) %collective-permute-start.17) | collective-permute-done | bytes 147488 | tf_op jit(solution)/shard_map/ppermute | solution.py:360
  37.3 0.7 %shard_map.94 = (bf16[48,768]{1,0:T(8,128)(2,1)}, bf16[48,768]{1,0:T(8,128)(2,1)}, bf16[48,768]{1,0:T(8,128)(2,1)}) custom-call(f32[288,128]{1,0:T(8,128)S(1)} %shard_map.92.refs_0_, bf16[288,128]{1,0:T(8,128)(2,1)S(1)} %collective-permute-done.13.refs_1_, bf16[288,128]{1,0:T(8,128)(2,1)S(1)} %collective-permute-done.14.refs_2_, ...), custom_call_target="tpu_custom_call" | custom-call | tf_op jit(solution)/shard_map/pallas_call | solution.py:331
  (14 shorter events, 0.1 us)
Async XLA Ops:
  1.9 9.5 %collective-permute-start.4 = (bf16[576,128]{1,0:T(8,128)(2,1)S(1)}, bf16[576,128]{1,0:T(8,128)(2,1)S(1)}, u32[]{:S(2)}, u32[]{:S(2)}) collective-permute-start(bf16[576,128]{1,0:T(8,128)(2,1)S(1)} %get-tuple-element.28.refs_4_), channel_id=1, source_target_pairs={{0,8},{4,12},{8,0},{12,4},{16,24},{20,28},{24,16},{28,20},{1,9},{5... | collective-permute-start | bytes 442376 | tf_op jit(solution)/shard_map/ppermute | solution.py:360
  5.0 9.8 %collective-permute-start.6 = (bf16[608,128]{1,0:T(8,128)(2,1)S(1)}, bf16[608,128]{1,0:T(8,128)(2,1)S(1)}, u32[]{:S(2)}, u32[]{:S(2)}) collective-permute-start(bf16[608,128]{1,0:T(8,128)(2,1)S(1)} %get-tuple-element.27.refs_0_), channel_id=1, source_target_pairs={{0,16},{4,20},{8,24},{12,28},{16,0},{20,4},{24,8},{28,12},{1,17},{... | collective-permute-start | bytes 466952 | tf_op jit(solution)/shard_map/ppermute | solution.py:360
  7.6 8.7 %collective-permute-start.1 = (bf16[608,128]{1,0:T(8,128)(2,1)S(1)}, bf16[608,128]{1,0:T(8,128)(2,1)S(1)}, u32[]{:S(2)}, u32[]{:S(2)}) collective-permute-start(bf16[608,128]{1,0:T(8,128)(2,1)S(1)} %get-tuple-element.27.refs_0_), channel_id=1, source_target_pairs={{0,2},{1,3},{2,0},{3,1},{4,6},{5,7},{6,4},{7,5},{8,10},{9,11},{10,... | collective-permute-start | bytes 466952 | tf_op jit(solution)/shard_map/ppermute | solution.py:358
  11.4 5.1 %collective-permute-start.5 = (bf16[576,128]{1,0:T(8,128)(2,1)S(1)}, bf16[576,128]{1,0:T(8,128)(2,1)S(1)}, u32[]{:S(2)}, u32[]{:S(2)}) collective-permute-start(bf16[576,128]{1,0:T(8,128)(2,1)S(1)} %shard_map.86.refs_6_), channel_id=1, source_target_pairs={{0,4},{4,0},{8,12},{12,8},{16,20},{20,16},{24,28},{28,24},{1,5},{5... | collective-permute-start | bytes 442376 | tf_op jit(solution)/shard_map/ppermute | solution.py:360
  13.2 5.1 %collective-permute-start.3 = (bf16[576,128]{1,0:T(8,128)(2,1)S(1)}, bf16[576,128]{1,0:T(8,128)(2,1)S(1)}, u32[]{:S(2)}, u32[]{:S(2)}) collective-permute-start(bf16[576,128]{1,0:T(8,128)(2,1)S(1)} %get-tuple-element.28.refs_4_), channel_id=1, source_target_pairs={{0,4},{4,0},{8,12},{12,8},{16,20},{20,16},{24,28},{28,24},{1,5},{5... | collective-permute-start | bytes 442376 | tf_op jit(solution)/shard_map/ppermute | solution.py:360
  13.4 4.9 %collective-permute-start = (bf16[608,128]{1,0:T(8,128)(2,1)S(1)}, bf16[608,128]{1,0:T(8,128)(2,1)S(1)}, u32[]{:S(2)}, u32[]{:S(2)}) collective-permute-start(bf16[608,128]{1,0:T(8,128)(2,1)S(1)} %get-tuple-element.27.refs_0_), channel_id=1, source_target_pairs={{0,1},{1,0},{2,3},{3,2},{4,5},{5,4},{6,7},{7,6},{8,9},{9,8},{10,11... | collective-permute-start | bytes 466952 | tf_op jit(solution)/shard_map/ppermute | solution.py:358
  14.8 5.4 %collective-permute-start.8 = (bf16[608,128]{1,0:T(8,128)(2,1)S(1)}, bf16[608,128]{1,0:T(8,128)(2,1)S(1)}, u32[]{:S(2)}, u32[]{:S(2)}) collective-permute-start(bf16[608,128]{1,0:T(8,128)(2,1)S(1)} %collective-permute-done.6.refs_0_), channel_id=1, source_target_pairs={{0,2},{1,3},{2,0},{3,1},{4,6},{5,7},{6,4},{7,5},{8,10},{9,11},{10,... | collective-permute-start | bytes 466952 | tf_op jit(solution)/shard_map/ppermute | solution.py:358
  16.3 3.9 %collective-permute-start.7 = (bf16[608,128]{1,0:T(8,128)(2,1)S(1)}, bf16[608,128]{1,0:T(8,128)(2,1)S(1)}, u32[]{:S(2)}, u32[]{:S(2)}) collective-permute-start(bf16[608,128]{1,0:T(8,128)(2,1)S(1)} %collective-permute-done.6.refs_0_), channel_id=1, source_target_pairs={{0,1},{1,0},{2,3},{3,2},{4,5},{5,4},{6,7},{7,6},{8,9},{9,8},{10,11... | collective-permute-start | bytes 466952 | tf_op jit(solution)/shard_map/ppermute | solution.py:358
  16.6 1.8 %collective-permute-start.2 = (bf16[608,128]{1,0:T(8,128)(2,1)S(1)}, bf16[608,128]{1,0:T(8,128)(2,1)S(1)}, u32[]{:S(2)}, u32[]{:S(2)}) collective-permute-start(bf16[608,128]{1,0:T(8,128)(2,1)S(1)} %collective-permute-done.1.refs_2_), channel_id=1, source_target_pairs={{0,1},{1,0},{2,3},{3,2},{4,5},{5,4},{6,7},{7,6},{8,9},{9,8},{10,11... | collective-permute-start | bytes 466952 | tf_op jit(solution)/shard_map/ppermute | solution.py:358
  20.2 1.4 %collective-permute-start.10 = (bf16[608,128]{1,0:T(8,128)(2,1)S(1)}, bf16[608,128]{1,0:T(8,128)(2,1)S(1)}, u32[]{:S(2)}, u32[]{:S(2)}) collective-permute-start(bf16[608,128]{1,0:T(8,128)(2,1)S(1)} %collective-permute-done.8.refs_2_), channel_id=1, source_target_pairs={{0,1},{1,0},{2,3},{3,2},{4,5},{5,4},{6,7},{7,6},{8,9},{9,8},{10,11... | collective-permute-start | bytes 466952 | tf_op jit(solution)/shard_map/ppermute | solution.py:358
  23.5 2.2 %collective-permute-start.11 = (bf16[576,128]{1,0:T(8,128)(2,1)S(1)}, bf16[576,128]{1,0:T(8,128)(2,1)S(1)}, u32[]{:S(2)}, u32[]{:S(2)}) collective-permute-start(bf16[576,128]{1,0:T(8,128)(2,1)S(1)} %get-tuple-element.43), channel_id=1, source_target_pairs={{0,1},{1,0},{2,3},{3,2},{4,5},{5,4},{6,7},{7,6},{8,9},{9,8},{10,11... | collective-permute-start | bytes 442376 | tf_op jit(solution)/shard_map/ppermute | solution.py:358
  23.7 3.6 %collective-permute-start.9 = (bf16[576,128]{1,0:T(8,128)(2,1)S(1)}, bf16[576,128]{1,0:T(8,128)(2,1)S(1)}, u32[]{:S(2)}, u32[]{:S(2)}) collective-permute-start(bf16[576,128]{1,0:T(8,128)(2,1)S(1)} %get-tuple-element.35), channel_id=1, source_target_pairs={{0,1},{1,0},{2,3},{3,2},{4,5},{5,4},{6,7},{7,6},{8,9},{9,8},{10,11... | collective-permute-start | bytes 442376 | tf_op jit(solution)/shard_map/ppermute | solution.py:358
  24.1 7.0 %collective-permute-start.16 = (bf16[576,128]{1,0:T(8,128)(2,1)S(1)}, bf16[576,128]{1,0:T(8,128)(2,1)S(1)}, u32[]{:S(2)}, u32[]{:S(2)}) collective-permute-start(bf16[576,128]{1,0:T(8,128)(2,1)S(1)} %get-tuple-element.50), channel_id=1, source_target_pairs={{0,4},{4,0},{8,12},{12,8},{16,20},{20,16},{24,28},{28,24},{1,5},{5... | collective-permute-start | bytes 442376 | tf_op jit(solution)/shard_map/ppermute | solution.py:360
  25.7 7.2 %collective-permute-start.12 = (bf16[288,128]{1,0:T(8,128)(2,1)S(1)}, bf16[288,128]{1,0:T(8,128)(2,1)S(1)}, u32[]{:S(2)}, u32[]{:S(2)}) collective-permute-start(bf16[288,128]{1,0:T(8,128)(2,1)S(1)} %get-tuple-element.44), channel_id=1, source_target_pairs={{0,16},{4,20},{8,24},{12,28},{16,0},{20,4},{24,8},{28,12},{1,17},{... | collective-permute-start | bytes 221192 | tf_op jit(solution)/shard_map/ppermute | solution.py:360
  27.3 5.6 %collective-permute-start.14 = (bf16[288,128]{1,0:T(8,128)(2,1)S(1)}, bf16[288,128]{1,0:T(8,128)(2,1)S(1)}, u32[]{:S(2)}, u32[]{:S(2)}) collective-permute-start(bf16[288,128]{1,0:T(8,128)(2,1)S(1)} %get-tuple-element.46), channel_id=1, source_target_pairs={{0,2},{1,3},{2,0},{3,1},{4,6},{5,7},{6,4},{7,5},{8,10},{9,11},{10,... | collective-permute-start | bytes 221192 | tf_op jit(solution)/shard_map/ppermute | solution.py:358
  28.9 5.1 %collective-permute-start.15 = (bf16[576,128]{1,0:T(8,128)(2,1)S(1)}, bf16[576,128]{1,0:T(8,128)(2,1)S(1)}, u32[]{:S(2)}, u32[]{:S(2)}) collective-permute-start(bf16[576,128]{1,0:T(8,128)(2,1)S(1)} %get-tuple-element.48), channel_id=1, source_target_pairs={{0,4},{4,0},{8,12},{12,8},{16,20},{20,16},{24,28},{28,24},{1,5},{5... | collective-permute-start | bytes 442376 | tf_op jit(solution)/shard_map/ppermute | solution.py:360
  29.8 6.3 %collective-permute-start.13 = (bf16[288,128]{1,0:T(8,128)(2,1)S(1)}, bf16[288,128]{1,0:T(8,128)(2,1)S(1)}, u32[]{:S(2)}, u32[]{:S(2)}) collective-permute-start(bf16[288,128]{1,0:T(8,128)(2,1)S(1)} %get-tuple-element.45), channel_id=1, source_target_pairs={{0,18},{1,19},{2,16},{3,17},{4,22},{5,23},{6,20},{7,21},{8,26},{9,... | collective-permute-start | bytes 221192 | tf_op jit(solution)/shard_map/ppermute | solution.py:366
  31.1 6.2 %collective-permute-start.17 = (bf16[576,128]{1,0:T(8,128)(2,1)S(1)}, bf16[576,128]{1,0:T(8,128)(2,1)S(1)}, u32[]{:S(2)}, u32[]{:S(2)}) collective-permute-start(bf16[576,128]{1,0:T(8,128)(2,1)S(1)} %shard_map.93), channel_id=1, source_target_pairs={{0,8},{4,12},{8,0},{12,4},{16,24},{20,28},{24,16},{28,20},{1,9},{5... | collective-permute-start | bytes 442376 | tf_op jit(solution)/shard_map/ppermute | solution.py:360

commit v5 on v4

--- a/solution.py
+++ b/solution.py
@@ -41,7 +41,7 @@
     def grant(self, blocks):
         scratch = 8 * self.tiles * self.span * LANES
         pairs = blocks * self.rows * round_up(self.span, LANES)
-        return 2 * scratch + 32 * pairs + 2**20
+        return 2 * scratch + 48 * pairs + 2**20
 
 
 def split2(x):
@@ -99,7 +99,7 @@
         lanes = slice(t * LANES, (t + 1) * LANES)
         rows = slice(t * r, (t + 1) * r)
         more = slice(s.part + t * r, s.part + (t + 1) * r)
-        qg_ref[rows, :] = q_ref[:, lanes]
+        qg_ref[rows, :] = (q_ref[:, lanes].astype(F32) * s.dim**-0.5).astype(BF16)
         qg_ref[more, :] = g_ref[:, lanes]
         kv_ref[rows, :] = k_ref[:, lanes]
         kv_ref[more, :] = v_ref[:, lanes]
@@ -148,8 +148,7 @@
         who = lax.bitwise_xor(me, off)
         at = pl.multiple_of(who * r, 16)
         for t in range(s.tiles):
-            q = qg[off][t * r : (t + 1) * r, :]
-            qs[t, pl.ds(at, r), :] = (q.astype(F32) * scale).astype(BF16)
+            qs[t, pl.ds(at, r), :] = qg[off][t * r : (t + 1) * r, :]
             gs[t, pl.ds(at, r), :] = qg[off][s.part + t * r : s.part + (t + 1) * r, :]
         small = qg[off][2 * s.part :, :].astype(F32)
         pieces = []
@@ -210,11 +209,11 @@
                     piece = piece + old[2 * s.part * i + where.start : 2 * s.part * i + where.stop, :]
                     sums[i][where, :] = piece.astype(sums[i].dtype)
 
-    ahead = front(0)
+    ahead = [front(t) for t in range(min(2, s.tiles))]
     for t in range(s.tiles):
-        k, scores, dweights = ahead
-        if t + 1 < s.tiles:
-            ahead = front(t + 1)
+        k, scores, dweights = ahead.pop(0)
+        if t + 2 < s.tiles:
+            ahead.append(front(t + 2))
         back(t, k, *middle(t, scores, dweights))
     for off in range(n):
         at = pl.multiple_of(lax.bitwise_xor(me, off) * r, 16)
@@ -375,11 +374,11 @@
     kv.update({bit: move(kv_own, bit, 0) for bit in bits[1:]})
     near[side] = move(qg_own, 0, side)
     kv[bits[0]] = hold(kv[bits[0]], 10000000000)
+    kv[bits[-1]] = hold(kv[bits[-1]], 10000000000)
     for bit in bits:
         for off in sorted(off for off in kv if off % (2 * bit) == 0 and off):
             kv[off + bit] = move(kv[off], bit, 0)
     far[side] = move(far[0], 0, side)
-    kv[s.high - 1] = hold(kv[s.high - 1], 3000000000)
     bit = side
     while bit:
         for blocks in (far, near):

time: 38.2 us -> 38.2 us (level)
  starting transfers between devices: 20.4 us -> 19.9 us
  waiting for transfers between devices: 11.2 us -> 11.7 us
    ppermute x8, starting transfers between devices: 13.5 us -> 11.3 us  [move(): return lax.ppermute(x, 'ctx', [(i, i ^ ctx_off) for i in range(ctx)])]
    ppermute x9, waiting for transfers between devices: 1.39 us -> 3.09 us  [move(): return lax.ppermute(x, 'head', [(i, i ^ head_off) for i in range(group)])]
    ppermute x1, starting transfers between devices: 1.31 us -> 2.83 us  [move(): return lax.ppermute(x, ('ctx', 'head'), pairs)]
    ppermute x8, waiting for transfers between devices: 7.83 us -> 6.61 us  [move(): return lax.ppermute(x, 'ctx', [(i, i ^ ctx_off) for i in range(ctx)])]
  transfers between devices with their start and end apart: 18 -> 18, of which waited for: 8 -> 10; matrix products, arithmetic and copies ran while one was open for 0% -> 0% of each run, Pallas kernels for 5% -> 5%
where the time goes in v5:
time: 38.2 us; the launch traced here: 38.1 us
  starting transfers between devices  19.9 us (52%)
  waiting for transfers between devices  11.7 us (31%)
  Pallas kernels  5.7 us (15%)
  between operations  0.71 us (2%)
    ppermute x8, starting transfers between devices, move(): return lax.ppermute(x, 'ctx', [(i, i ^ ctx_off) for i in range(ctx)])  11.3 us
    ppermute x8, waiting for transfers between devices, move(): return lax.ppermute(x, 'ctx', [(i, i ^ ctx_off) for i in range(ctx)])  6.61 us
    ppermute x9, starting transfers between devices, move(): return lax.ppermute(x, 'head', [(i, i ^ head_off) for i in range(group)])  5.79 us
    pallas_call x2, Pallas kernels, attend(): pl.pallas_call(functools.partial(attend_kernel, s, blocks, first), out_sh...  3.6 us
    ppermute x9, waiting for transfers between devices, move(): return lax.ppermute(x, 'head', [(i, i ^ head_off) for i in range(group)])  3.09 us
    ppermute x1, starting transfers between devices, move(): return lax.ppermute(x, ('ctx', 'head'), pairs)  2.83 us
    ppermute x1, waiting for transfers between devices, move(): return lax.ppermute(x, ('ctx', 'head'), pairs)  2.02 us
    pallas_call x1, Pallas kernels, pack(): pl.pallas_call(functools.partial(pack_kernel, s), out_shape=(jax.ShapeDty...  1.28 us
  transfers between devices with their start and end apart: 18, of which 10 were waited for; matrix products, arithmetic and copies ran while one was open for 0% of the time, Pallas kernels for 5%

profile of v5, /device:TPU:0, one launch (start us, length us, event | category | flops | bytes accessed | tf_op | source)
XLA Modules:
  0.0 38.1 jit_solution(6912969091756837742)
XLA Ops:
  0.6 1.3 %shard_map.85 = (bf16[608,128]{1,0:T(8,128)(2,1)S(1)}, bf16[576,128]{1,0:T(8,128)(2,1)S(1)}) custom-call(bf16[48,768]{1,0:T(8,128)(2,1)} %q_in.1, bf16[48,768]{1,0:T(8,128)(2,1)} %k_in.1, bf16[48,768]{1,0:T(8,128)(2,1)} %v_in.1, bf16[48,768]{1,0:T(8,128)(2,1)} %o_in.1, bf16[48,768]{1,0:T(8,128)(2,1)} %g_in.1, f32[3,192]{1,0:T(4,128)} %bitcast.1), custom_call_target="tpu_custom_call" | custom-call | tf_op jit(solution)/shard_map/pallas_call | solution.py:113
  1.9 3.1 %collective-permute-start.4 = (bf16[576,128]{1,0:T(8,128)(2,1)S(1)}, bf16[576,128]{1,0:T(8,128)(2,1)S(1)}, u32[]{:S(2)}, u32[]{:S(2)}) collective-permute-start(bf16[576,128]{1,0:T(8,128)(2,1)S(1)} %get-tuple-element.28.refs_4_), channel_id=1, source_target_pairs={{0,8},{4,12},{8,0},{12,4},{16,24},{20,28},{24,16},{28,20},{1,9},{5... | collective-permute-start | bytes 442376 | tf_op jit(solution)/shard_map/ppermute | solution.py:359
  5.0 1.5 %collective-permute-start.3 = (bf16[576,128]{1,0:T(8,128)(2,1)S(1)}, bf16[576,128]{1,0:T(8,128)(2,1)S(1)}, u32[]{:S(2)}, u32[]{:S(2)}) collective-permute-start(bf16[576,128]{1,0:T(8,128)(2,1)S(1)} %get-tuple-element.28.refs_4_), channel_id=1, source_target_pairs={{0,4},{4,0},{8,12},{12,8},{16,20},{20,16},{24,28},{28,24},{1,5},{5... | collective-permute-start | bytes 442376 | tf_op jit(solution)/shard_map/ppermute | solution.py:359
  6.5 2.6 %collective-permute-start.6 = (bf16[608,128]{1,0:T(8,128)(2,1)S(1)}, bf16[608,128]{1,0:T(8,128)(2,1)S(1)}, u32[]{:S(2)}, u32[]{:S(2)}) collective-permute-start(bf16[608,128]{1,0:T(8,128)(2,1)S(1)} %get-tuple-element.27.refs_0_), channel_id=1, source_target_pairs={{0,16},{4,20},{8,24},{12,28},{16,0},{20,4},{24,8},{28,12},{1,17},{... | collective-permute-start | bytes 466952 | tf_op jit(solution)/shard_map/ppermute | solution.py:359
  9.1 1.5 %collective-permute-start.1 = (bf16[608,128]{1,0:T(8,128)(2,1)S(1)}, bf16[608,128]{1,0:T(8,128)(2,1)S(1)}, u32[]{:S(2)}, u32[]{:S(2)}) collective-permute-start(bf16[608,128]{1,0:T(8,128)(2,1)S(1)} %get-tuple-element.27.refs_0_), channel_id=1, source_target_pairs={{0,2},{1,3},{2,0},{3,1},{4,6},{5,7},{6,4},{7,5},{8,10},{9,11},{10,... | collective-permute-start | bytes 466952 | tf_op jit(solution)/shard_map/ppermute | solution.py:357
  10.6 0.0 collective-permute-start
  10.6 0.0 collective-permute-done.4.ref
  10.6 2.1 %collective-permute-start.5 = (bf16[576,128]{1,0:T(8,128)(2,1)S(1)}, bf16[576,128]{1,0:T(8,128)(2,1)S(1)}, u32[]{:S(2)}, u32[]{:S(2)}) collective-permute-start(bf16[576,128]{1,0:T(8,128)(2,1)S(1)} %shard_map.87.refs_6_), channel_id=1, source_target_pairs={{0,4},{4,0},{8,12},{12,8},{16,20},{20,16},{24,28},{28,24},{1,5},{5... | collective-permute-start | bytes 442376 | tf_op jit(solution)/shard_map/ppermute | solution.py:359
  12.7 3.2 %collective-permute-done.6.refs_0_ = bf16[608,128]{1,0:T(8,128)(2,1)S(1)} collective-permute-done((bf16[608,128]{1,0:T(8,128)(2,1)S(1)}, bf16[608,128]{1,0:T(8,128)(2,1)S(1)}, u32[]{:S(2)}, u32[]{:S(2)}) %collective-permute-start.6) | collective-permute-done | bytes 155680 | tf_op jit(solution)/shard_map/ppermute | solution.py:359
  15.9 1.5 %collective-permute-start.8 = (bf16[608,128]{1,0:T(8,128)(2,1)S(1)}, bf16[608,128]{1,0:T(8,128)(2,1)S(1)}, u32[]{:S(2)}, u32[]{:S(2)}) collective-permute-start(bf16[608,128]{1,0:T(8,128)(2,1)S(1)} %collective-permute-done.6.refs_0_), channel_id=1, source_target_pairs={{0,2},{1,3},{2,0},{3,1},{4,6},{5,7},{6,4},{7,5},{8,10},{9,11},{10,... | collective-permute-start | bytes 466952 | tf_op jit(solution)/shard_map/ppermute | solution.py:357
  17.5 0.5 %collective-permute-start.2 = (bf16[608,128]{1,0:T(8,128)(2,1)S(1)}, bf16[608,128]{1,0:T(8,128)(2,1)S(1)}, u32[]{:S(2)}, u32[]{:S(2)}) collective-permute-start(bf16[608,128]{1,0:T(8,128)(2,1)S(1)} %collective-permute-done.1.refs_2_), channel_id=1, source_target_pairs={{0,1},{1,0},{2,3},{3,2},{4,5},{5,4},{6,7},{7,6},{8,9},{9,8},{10,11... | collective-permute-start | bytes 466952 | tf_op jit(solution)/shard_map/ppermute | solution.py:357
  18.0 1.1 %collective-permute-done.2.refs_3_ = bf16[608,128]{1,0:T(8,128)(2,1)S(1)} collective-permute-done((bf16[608,128]{1,0:T(8,128)(2,1)S(1)}, bf16[608,128]{1,0:T(8,128)(2,1)S(1)}, u32[]{:S(2)}, u32[]{:S(2)}) %collective-permute-start.2) | collective-permute-done | bytes 155680 | tf_op jit(solution)/shard_map/ppermute | solution.py:357
  19.1 1.8 %shard_map.88 = (f32[288,128]{1,0:T(8,128)S(1)}, f32[288,128]{1,0:T(8,128)S(1)}, bf16[576,128]{1,0:T(8,128)(2,1)S(1)}, f32[2304,128]{1,0:T(8,128)S(1)}) custom-call(bf16[608,128]{1,0:T(8,128)(2,1)S(1)} %get-tuple-element.27.refs_0_, bf16[608,128]{1,0:T(8,128)(2,1)S(1)} %collective-permute-done.refs_1_, bf16[608,128]{1,0:T(8,128)(2,1)S(1)} %collective-permute-done.1.refs_2_, ...), custom_call_target="tpu_custom_call" | custom-call | flops 566231040 | bytes 1179648 | tf_op jit(solution)/shard_map/pallas_call | solution.py:243
  20.9 0.3 collective-permute-done.8.refs_2_
  21.2 0.1 collective-permute-start.10
  21.2 1.3 %collective-permute-done.10.refs_3_ = bf16[608,128]{1,0:T(8,128)(2,1)S(1)} collective-permute-done((bf16[608,128]{1,0:T(8,128)(2,1)S(1)}, bf16[608,128]{1,0:T(8,128)(2,1)S(1)}, u32[]{:S(2)}, u32[]{:S(2)}) %collective-permute-start.10) | collective-permute-done | bytes 155680 | tf_op jit(solution)/shard_map/ppermute | solution.py:357
  22.6 1.8 %shard_map.90 = (f32[288,128]{1,0:T(8,128)S(1)}, f32[288,128]{1,0:T(8,128)S(1)}, bf16[576,128]{1,0:T(8,128)(2,1)S(1)}, f32[576,128]{1,0:T(8,128)S(1)}, bf16[576,...) custom-call(bf16[608,128]{1,0:T(8,128)(2,1)S(1)} %collective-permute-done.6.refs_0_, ...), custom_call_target="tpu_custom_call" | custom-call | flops 5662310400 | bytes 1179648 | tf_op jit(solution)/shard_map/pallas_call | solution.py:243
  24.4 0.2 collective-permute-start.11
  24.6 0.4 collective-permute-start.9
  25.0 0.6 %collective-permute-start.16 = (bf16[576,128]{1,0:T(8,128)(2,1)S(1)}, bf16[576,128]{1,0:T(8,128)(2,1)S(1)}, u32[]{:S(2)}, u32[]{:S(2)}) collective-permute-start(bf16[576,128]{1,0:T(8,128)(2,1)S(1)} %get-tuple-element.50), channel_id=1, source_target_pairs={{0,4},{4,0},{8,12},{12,8},{16,20},{20,16},{24,28},{28,24},{1,5},{5... | collective-permute-start | bytes 442376 | tf_op jit(solution)/shard_map/ppermute | solution.py:359
  25.5 0.3 collective-permute-done.11.refs_2_
  25.8 0.1 collective-permute-start.12
  25.9 0.1 collective-permute-done.9.refs_2_
  26.1 1.6 %collective-permute-start.14 = (bf16[288,128]{1,0:T(8,128)(2,1)S(1)}, bf16[288,128]{1,0:T(8,128)(2,1)S(1)}, u32[]{:S(2)}, u32[]{:S(2)}) collective-permute-start(bf16[288,128]{1,0:T(8,128)(2,1)S(1)} %get-tuple-element.46), channel_id=1, source_target_pairs={{0,2},{1,3},{2,0},{3,1},{4,6},{5,7},{6,4},{7,5},{8,10},{9,11},{10,... | collective-permute-start | bytes 221192 | tf_op jit(solution)/shard_map/ppermute | solution.py:357
  27.6 1.1 %collective-permute-start.15 = (bf16[576,128]{1,0:T(8,128)(2,1)S(1)}, bf16[576,128]{1,0:T(8,128)(2,1)S(1)}, u32[]{:S(2)}, u32[]{:S(2)}) collective-permute-start(bf16[576,128]{1,0:T(8,128)(2,1)S(1)} %get-tuple-element.48), channel_id=1, source_target_pairs={{0,4},{4,0},{8,12},{12,8},{16,20},{20,16},{24,28},{28,24},{1,5},{5... | collective-permute-start | bytes 442376 | tf_op jit(solution)/shard_map/ppermute | solution.py:359
  28.7 2.8 %collective-permute-start.13 = (bf16[288,128]{1,0:T(8,128)(2,1)S(1)}, bf16[288,128]{1,0:T(8,128)(2,1)S(1)}, u32[]{:S(2)}, u32[]{:S(2)}) collective-permute-start(bf16[288,128]{1,0:T(8,128)(2,1)S(1)} %get-tuple-element.45), channel_id=1, source_target_pairs={{0,18},{1,19},{2,16},{3,17},{4,22},{5,23},{6,20},{7,21},{8,26},{9,... | collective-permute-start | bytes 221192 | tf_op jit(solution)/shard_map/ppermute | solution.py:365
  31.6 0.3 collective-permute-start.17
  31.9 0.8 %collective-permute-done.12.refs_1_ = bf16[288,128]{1,0:T(8,128)(2,1)S(1)} collective-permute-done((bf16[288,128]{1,0:T(8,128)(2,1)S(1)}, bf16[288,128]{1,0:T(8,128)(2,1)S(1)}, u32[]{:S(2)}, u32[]{:S(2)}) %collective-permute-start.12) | collective-permute-done | bytes 73760 | tf_op jit(solution)/shard_map/ppermute | solution.py:359
  32.7 1.3 %collective-permute-done.15.refs_4_ = bf16[576,128]{1,0:T(8,128)(2,1)S(1)} collective-permute-done((bf16[576,128]{1,0:T(8,128)(2,1)S(1)}, bf16[576,128]{1,0:T(8,128)(2,1)S(1)}, u32[]{:S(2)}, u32[]{:S(2)}) %collective-permute-start.15) | collective-permute-done | bytes 147488 | tf_op jit(solution)/shard_map/ppermute | solution.py:359
  34.0 2.0 %collective-permute-done.13.refs_1_ = bf16[288,128]{1,0:T(8,128)(2,1)S(1)} collective-permute-done((bf16[288,128]{1,0:T(8,128)(2,1)S(1)}, bf16[288,128]{1,0:T(8,128)(2,1)S(1)}, u32[]{:S(2)}, u32[]{:S(2)}) %collective-permute-start.13) | collective-permute-done | bytes 73760 | tf_op jit(solution)/shard_map/ppermute | solution.py:365
  36.0 1.3 %collective-permute-done.17.refs_5_ = bf16[576,128]{1,0:T(8,128)(2,1)S(1)} collective-permute-done((bf16[576,128]{1,0:T(8,128)(2,1)S(1)}, bf16[576,128]{1,0:T(8,128)(2,1)S(1)}, u32[]{:S(2)}, u32[]{:S(2)}) %collective-permute-start.17) | collective-permute-done | bytes 147488 | tf_op jit(solution)/shard_map/ppermute | solution.py:359
  37.3 0.7 %shard_map.94 = (bf16[48,768]{1,0:T(8,128)(2,1)}, bf16[48,768]{1,0:T(8,128)(2,1)}, bf16[48,768]{1,0:T(8,128)(2,1)}) custom-call(f32[288,128]{1,0:T(8,128)S(1)} %shard_map.92.refs_0_, bf16[288,128]{1,0:T(8,128)(2,1)S(1)} %collective-permute-done.13.refs_1_, bf16[288,128]{1,0:T(8,128)(2,1)S(1)} %collective-permute-done.14.refs_2_, ...), custom_call_target="tpu_custom_call" | custom-call | tf_op jit(solution)/shard_map/pallas_call | solution.py:330
  (14 shorter events, 0.1 us)
Async XLA Ops:
  1.9 8.7 %collective-permute-start.4 = (bf16[576,128]{1,0:T(8,128)(2,1)S(1)}, bf16[576,128]{1,0:T(8,128)(2,1)S(1)}, u32[]{:S(2)}, u32[]{:S(2)}) collective-permute-start(bf16[576,128]{1,0:T(8,128)(2,1)S(1)} %get-tuple-element.28.refs_4_), channel_id=1, source_target_pairs={{0,8},{4,12},{8,0},{12,4},{16,24},{20,28},{24,16},{28,20},{1,9},{5... | collective-permute-start | bytes 442376 | tf_op jit(solution)/shard_map/ppermute | solution.py:359
  5.0 12.5 %collective-permute-start.3 = (bf16[576,128]{1,0:T(8,128)(2,1)S(1)}, bf16[576,128]{1,0:T(8,128)(2,1)S(1)}, u32[]{:S(2)}, u32[]{:S(2)}) collective-permute-start(bf16[576,128]{1,0:T(8,128)(2,1)S(1)} %get-tuple-element.28.refs_4_), channel_id=1, source_target_pairs={{0,4},{4,0},{8,12},{12,8},{16,20},{20,16},{24,28},{28,24},{1,5},{5... | collective-permute-start | bytes 442376 | tf_op jit(solution)/shard_map/ppermute | solution.py:359
  6.5 9.4 %collective-permute-start.6 = (bf16[608,128]{1,0:T(8,128)(2,1)S(1)}, bf16[608,128]{1,0:T(8,128)(2,1)S(1)}, u32[]{:S(2)}, u32[]{:S(2)}) collective-permute-start(bf16[608,128]{1,0:T(8,128)(2,1)S(1)} %get-tuple-element.27.refs_0_), channel_id=1, source_target_pairs={{0,16},{4,20},{8,24},{12,28},{16,0},{20,4},{24,8},{28,12},{1,17},{... | collective-permute-start | bytes 466952 | tf_op jit(solution)/shard_map/ppermute | solution.py:359
  9.1 8.4 %collective-permute-start.1 = (bf16[608,128]{1,0:T(8,128)(2,1)S(1)}, bf16[608,128]{1,0:T(8,128)(2,1)S(1)}, u32[]{:S(2)}, u32[]{:S(2)}) collective-permute-start(bf16[608,128]{1,0:T(8,128)(2,1)S(1)} %get-tuple-element.27.refs_0_), channel_id=1, source_target_pairs={{0,2},{1,3},{2,0},{3,1},{4,6},{5,7},{6,4},{7,5},{8,10},{9,11},{10,... | collective-permute-start | bytes 466952 | tf_op jit(solution)/shard_map/ppermute | solution.py:357
  10.6 7.4 %collective-permute-start = (bf16[608,128]{1,0:T(8,128)(2,1)S(1)}, bf16[608,128]{1,0:T(8,128)(2,1)S(1)}, u32[]{:S(2)}, u32[]{:S(2)}) collective-permute-start(bf16[608,128]{1,0:T(8,128)(2,1)S(1)} %get-tuple-element.27.refs_0_), channel_id=1, source_target_pairs={{0,1},{1,0},{2,3},{3,2},{4,5},{5,4},{6,7},{7,6},{8,9},{9,8},{10,11... | collective-permute-start | bytes 466952 | tf_op jit(solution)/shard_map/ppermute | solution.py:357
  10.6 7.4 %collective-permute-start.5 = (bf16[576,128]{1,0:T(8,128)(2,1)S(1)}, bf16[576,128]{1,0:T(8,128)(2,1)S(1)}, u32[]{:S(2)}, u32[]{:S(2)}) collective-permute-start(bf16[576,128]{1,0:T(8,128)(2,1)S(1)} %shard_map.87.refs_6_), channel_id=1, source_target_pairs={{0,4},{4,0},{8,12},{12,8},{16,20},{20,16},{24,28},{28,24},{1,5},{5... | collective-permute-start | bytes 442376 | tf_op jit(solution)/shard_map/ppermute | solution.py:359
  15.9 5.2 %collective-permute-start.8 = (bf16[608,128]{1,0:T(8,128)(2,1)S(1)}, bf16[608,128]{1,0:T(8,128)(2,1)S(1)}, u32[]{:S(2)}, u32[]{:S(2)}) collective-permute-start(bf16[608,128]{1,0:T(8,128)(2,1)S(1)} %collective-permute-done.6.refs_0_), channel_id=1, source_target_pairs={{0,2},{1,3},{2,0},{3,1},{4,6},{5,7},{6,4},{7,5},{8,10},{9,11},{10,... | collective-permute-start | bytes 466952 | tf_op jit(solution)/shard_map/ppermute | solution.py:357
  17.5 3.7 %collective-permute-start.7 = (bf16[608,128]{1,0:T(8,128)(2,1)S(1)}, bf16[608,128]{1,0:T(8,128)(2,1)S(1)}, u32[]{:S(2)}, u32[]{:S(2)}) collective-permute-start(bf16[608,128]{1,0:T(8,128)(2,1)S(1)} %collective-permute-done.6.refs_0_), channel_id=1, source_target_pairs={{0,1},{1,0},{2,3},{3,2},{4,5},{5,4},{6,7},{7,6},{8,9},{9,8},{10,11... | collective-permute-start | bytes 466952 | tf_op jit(solution)/shard_map/ppermute | solution.py:357
  17.5 1.6 %collective-permute-start.2 = (bf16[608,128]{1,0:T(8,128)(2,1)S(1)}, bf16[608,128]{1,0:T(8,128)(2,1)S(1)}, u32[]{:S(2)}, u32[]{:S(2)}) collective-permute-start(bf16[608,128]{1,0:T(8,128)(2,1)S(1)} %collective-permute-done.1.refs_2_), channel_id=1, source_target_pairs={{0,1},{1,0},{2,3},{3,2},{4,5},{5,4},{6,7},{7,6},{8,9},{9,8},{10,11... | collective-permute-start | bytes 466952 | tf_op jit(solution)/shard_map/ppermute | solution.py:357
  21.2 1.4 %collective-permute-start.10 = (bf16[608,128]{1,0:T(8,128)(2,1)S(1)}, bf16[608,128]{1,0:T(8,128)(2,1)S(1)}, u32[]{:S(2)}, u32[]{:S(2)}) collective-permute-start(bf16[608,128]{1,0:T(8,128)(2,1)S(1)} %collective-permute-done.8.refs_2_), channel_id=1, source_target_pairs={{0,1},{1,0},{2,3},{3,2},{4,5},{5,4},{6,7},{7,6},{8,9},{9,8},{10,11... | collective-permute-start | bytes 466952 | tf_op jit(solution)/shard_map/ppermute | solution.py:357
  24.4 1.4 %collective-permute-start.11 = (bf16[576,128]{1,0:T(8,128)(2,1)S(1)}, bf16[576,128]{1,0:T(8,128)(2,1)S(1)}, u32[]{:S(2)}, u32[]{:S(2)}) collective-permute-start(bf16[576,128]{1,0:T(8,128)(2,1)S(1)} %get-tuple-element.43), channel_id=1, source_target_pairs={{0,1},{1,0},{2,3},{3,2},{4,5},{5,4},{6,7},{7,6},{8,9},{9,8},{10,11... | collective-permute-start | bytes 442376 | tf_op jit(solution)/shard_map/ppermute | solution.py:357
  24.6 1.4 %collective-permute-start.9 = (bf16[576,128]{1,0:T(8,128)(2,1)S(1)}, bf16[576,128]{1,0:T(8,128)(2,1)S(1)}, u32[]{:S(2)}, u32[]{:S(2)}) collective-permute-start(bf16[576,128]{1,0:T(8,128)(2,1)S(1)} %get-tuple-element.35), channel_id=1, source_target_pairs={{0,1},{1,0},{2,3},{3,2},{4,5},{5,4},{6,7},{7,6},{8,9},{9,8},{10,11... | collective-permute-start | bytes 442376 | tf_op jit(solution)/shard_map/ppermute | solution.py:357
  25.0 6.6 %collective-permute-start.16 = (bf16[576,128]{1,0:T(8,128)(2,1)S(1)}, bf16[576,128]{1,0:T(8,128)(2,1)S(1)}, u32[]{:S(2)}, u32[]{:S(2)}) collective-permute-start(bf16[576,128]{1,0:T(8,128)(2,1)S(1)} %get-tuple-element.50), channel_id=1, source_target_pairs={{0,4},{4,0},{8,12},{12,8},{16,20},{20,16},{24,28},{28,24},{1,5},{5... | collective-permute-start | bytes 442376 | tf_op jit(solution)/shard_map/ppermute | solution.py:359
  25.8 6.8 %collective-permute-start.12 = (bf16[288,128]{1,0:T(8,128)(2,1)S(1)}, bf16[288,128]{1,0:T(8,128)(2,1)S(1)}, u32[]{:S(2)}, u32[]{:S(2)}) collective-permute-start(bf16[288,128]{1,0:T(8,128)(2,1)S(1)} %get-tuple-element.44), channel_id=1, source_target_pairs={{0,16},{4,20},{8,24},{12,28},{16,0},{20,4},{24,8},{28,12},{1,17},{... | collective-permute-start | bytes 221192 | tf_op jit(solution)/shard_map/ppermute | solution.py:359
  26.1 6.6 %collective-permute-start.14 = (bf16[288,128]{1,0:T(8,128)(2,1)S(1)}, bf16[288,128]{1,0:T(8,128)(2,1)S(1)}, u32[]{:S(2)}, u32[]{:S(2)}) collective-permute-start(bf16[288,128]{1,0:T(8,128)(2,1)S(1)} %get-tuple-element.46), channel_id=1, source_target_pairs={{0,2},{1,3},{2,0},{3,1},{4,6},{5,7},{6,4},{7,5},{8,10},{9,11},{10,... | collective-permute-start | bytes 221192 | tf_op jit(solution)/shard_map/ppermute | solution.py:357
  27.6 6.4 %collective-permute-start.15 = (bf16[576,128]{1,0:T(8,128)(2,1)S(1)}, bf16[576,128]{1,0:T(8,128)(2,1)S(1)}, u32[]{:S(2)}, u32[]{:S(2)}) collective-permute-start(bf16[576,128]{1,0:T(8,128)(2,1)S(1)} %get-tuple-element.48), channel_id=1, source_target_pairs={{0,4},{4,0},{8,12},{12,8},{16,20},{20,16},{24,28},{28,24},{1,5},{5... | collective-permute-start | bytes 442376 | tf_op jit(solution)/shard_map/ppermute | solution.py:359
  28.7 7.3 %collective-permute-start.13 = (bf16[288,128]{1,0:T(8,128)(2,1)S(1)}, bf16[288,128]{1,0:T(8,128)(2,1)S(1)}, u32[]{:S(2)}, u32[]{:S(2)}) collective-permute-start(bf16[288,128]{1,0:T(8,128)(2,1)S(1)} %get-tuple-element.45), channel_id=1, source_target_pairs={{0,18},{1,19},{2,16},{3,17},{4,22},{5,23},{6,20},{7,21},{8,26},{9,... | collective-permute-start | bytes 221192 | tf_op jit(solution)/shard_map/ppermute | solution.py:365
  31.6 5.7 %collective-permute-start.17 = (bf16[576,128]{1,0:T(8,128)(2,1)S(1)}, bf16[576,128]{1,0:T(8,128)(2,1)S(1)}, u32[]{:S(2)}, u32[]{:S(2)}) collective-permute-start(bf16[576,128]{1,0:T(8,128)(2,1)S(1)} %shard_map.93), channel_id=1, source_target_pairs={{0,8},{4,12},{8,0},{12,4},{16,24},{20,28},{24,16},{28,20},{1,9},{5... | collective-permute-start | bytes 442376 | tf_op jit(solution)/shard_map/ppermute | solution.py:359

commit v6 on v5

--- a/solution.py
+++ b/solution.py
@@ -399,6 +399,9 @@
     late_q = total_q[1:] + late_q
     total_q = total_q[:1]
     total_q = [dq[0]] + total_q
+    sums1 = list(sums1)
+    sums1[-1], near_dq = tie((sums1[-1], late_q[-1]))
+    late_q[-1] = near_dq
     parts = {off: [sums1[off]] for off in range(s.high)}
     for bit in reversed(bits):
         others = [off for off in range(s.high) if off & (2 * bit - 1) == bit and off != bit]

time: 38.2 us -> 40.2 us (1.052)
  starting transfers between devices: 19.9 us -> 21 us
  waiting for transfers between devices: 11.7 us -> 12.7 us
    ppermute x8, waiting for transfers between devices: 6.61 us -> 7.71 us  [move(): return lax.ppermute(x, 'ctx', [(i, i ^ ctx_off) for i in range(ctx)])]
    ppermute x1, starting transfers between devices: 2.83 us -> 3.8 us  [move(): return lax.ppermute(x, ('ctx', 'head'), pairs)]
    ppermute x1, waiting for transfers between devices: 2.02 us -> 1.41 us  [move(): return lax.ppermute(x, ('ctx', 'head'), pairs)]
    ppermute x9, waiting for transfers between devices: 3.09 us -> 3.54 us  [move(): return lax.ppermute(x, 'head', [(i, i ^ head_off) for i in range(group)])]
  transfers between devices with their start and end apart: 18 -> 18, of which waited for: 10 -> 10; matrix products, arithmetic and copies ran while one was open for 0% -> 0% of each run, Pallas kernels for 5% -> 9%
where the time goes in v6:
time: 40.2 us; the launch traced here: 40.1 us
  starting transfers between devices  21 us (52%)
  waiting for transfers between devices  12.7 us (32%)
  Pallas kernels  5.68 us (14%)
  between operations  0.71 us (2%)
    ppermute x8, starting transfers between devices, move(): return lax.ppermute(x, 'ctx', [(i, i ^ ctx_off) for i in range(ctx)])  11.5 us
    ppermute x8, waiting for transfers between devices, move(): return lax.ppermute(x, 'ctx', [(i, i ^ ctx_off) for i in range(ctx)])  7.71 us
    ppermute x9, starting transfers between devices, move(): return lax.ppermute(x, 'head', [(i, i ^ head_off) for i in range(group)])  5.72 us
    ppermute x1, starting transfers between devices, move(): return lax.ppermute(x, ('ctx', 'head'), pairs)  3.8 us
    pallas_call x2, Pallas kernels, attend(): pl.pallas_call(functools.partial(attend_kernel, s, blocks, first), out_sh...  3.58 us
    ppermute x9, waiting for transfers between devices, move(): return lax.ppermute(x, 'head', [(i, i ^ head_off) for i in range(group)])  3.54 us
    ppermute x1, waiting for transfers between devices, move(): return lax.ppermute(x, ('ctx', 'head'), pairs)  1.41 us
    pallas_call x1, Pallas kernels, pack(): pl.pallas_call(functools.partial(pack_kernel, s), out_shape=(jax.ShapeDty...  1.28 us
  transfers between devices with their start and end apart: 18, of which 10 were waited for; matrix products, arithmetic and copies ran while one was open for 0% of the time, Pallas kernels for 9%

profile of v6, /device:TPU:0, one launch (start us, length us, event | category | flops | bytes accessed | tf_op | source)
XLA Modules:
  0.0 40.1 jit_solution(14589463275691754323)
XLA Ops:
  0.6 1.3 %shard_map.85 = (bf16[608,128]{1,0:T(8,128)(2,1)S(1)}, bf16[576,128]{1,0:T(8,128)(2,1)S(1)}) custom-call(bf16[48,768]{1,0:T(8,128)(2,1)} %q_in.1, bf16[48,768]{1,0:T(8,128)(2,1)} %k_in.1, bf16[48,768]{1,0:T(8,128)(2,1)} %v_in.1, bf16[48,768]{1,0:T(8,128)(2,1)} %o_in.1, bf16[48,768]{1,0:T(8,128)(2,1)} %g_in.1, f32[3,192]{1,0:T(4,128)} %bitcast.1), custom_call_target="tpu_custom_call" | custom-call | tf_op jit(solution)/shard_map/pallas_call | solution.py:113
  1.9 3.1 %collective-permute-start.4 = (bf16[576,128]{1,0:T(8,128)(2,1)S(1)}, bf16[576,128]{1,0:T(8,128)(2,1)S(1)}, u32[]{:S(2)}, u32[]{:S(2)}) collective-permute-start(bf16[576,128]{1,0:T(8,128)(2,1)S(1)} %get-tuple-element.30.refs_4_), channel_id=1, source_target_pairs={{0,8},{4,12},{8,0},{12,4},{16,24},{20,28},{24,16},{28,20},{1,9},{5... | collective-permute-start | bytes 442376 | tf_op jit(solution)/shard_map/ppermute | solution.py:359
  5.0 1.5 %collective-permute-start.3 = (bf16[576,128]{1,0:T(8,128)(2,1)S(1)}, bf16[576,128]{1,0:T(8,128)(2,1)S(1)}, u32[]{:S(2)}, u32[]{:S(2)}) collective-permute-start(bf16[576,128]{1,0:T(8,128)(2,1)S(1)} %get-tuple-element.30.refs_4_), channel_id=1, source_target_pairs={{0,4},{4,0},{8,12},{12,8},{16,20},{20,16},{24,28},{28,24},{1,5},{5... | collective-permute-start | bytes 442376 | tf_op jit(solution)/shard_map/ppermute | solution.py:359
  6.5 2.6 %collective-permute-start.6 = (bf16[608,128]{1,0:T(8,128)(2,1)S(1)}, bf16[608,128]{1,0:T(8,128)(2,1)S(1)}, u32[]{:S(2)}, u32[]{:S(2)}) collective-permute-start(bf16[608,128]{1,0:T(8,128)(2,1)S(1)} %get-tuple-element.29.refs_0_), channel_id=1, source_target_pairs={{0,16},{4,20},{8,24},{12,28},{16,0},{20,4},{24,8},{28,12},{1,17},{... | collective-permute-start | bytes 466952 | tf_op jit(solution)/shard_map/ppermute | solution.py:359
  9.1 1.5 %collective-permute-start.1 = (bf16[608,128]{1,0:T(8,128)(2,1)S(1)}, bf16[608,128]{1,0:T(8,128)(2,1)S(1)}, u32[]{:S(2)}, u32[]{:S(2)}) collective-permute-start(bf16[608,128]{1,0:T(8,128)(2,1)S(1)} %get-tuple-element.29.refs_0_), channel_id=1, source_target_pairs={{0,2},{1,3},{2,0},{3,1},{4,6},{5,7},{6,4},{7,5},{8,10},{9,11},{10,... | collective-permute-start | bytes 466952 | tf_op jit(solution)/shard_map/ppermute | solution.py:357
  10.6 2.1 %collective-permute-start.5 = (bf16[576,128]{1,0:T(8,128)(2,1)S(1)}, bf16[576,128]{1,0:T(8,128)(2,1)S(1)}, u32[]{:S(2)}, u32[]{:S(2)}) collective-permute-start(bf16[576,128]{1,0:T(8,128)(2,1)S(1)} %shard_map.87.refs_6_), channel_id=1, source_target_pairs={{0,4},{4,0},{8,12},{12,8},{16,20},{20,16},{24,28},{28,24},{1,5},{5... | collective-permute-start | bytes 442376 | tf_op jit(solution)/shard_map/ppermute | solution.py:359
  12.7 3.2 %collective-permute-done.6.refs_0_ = bf16[608,128]{1,0:T(8,128)(2,1)S(1)} collective-permute-done((bf16[608,128]{1,0:T(8,128)(2,1)S(1)}, bf16[608,128]{1,0:T(8,128)(2,1)S(1)}, u32[]{:S(2)}, u32[]{:S(2)}) %collective-permute-start.6) | collective-permute-done | bytes 155680 | tf_op jit(solution)/shard_map/ppermute | solution.py:359
  15.9 1.5 %collective-permute-start.8 = (bf16[608,128]{1,0:T(8,128)(2,1)S(1)}, bf16[608,128]{1,0:T(8,128)(2,1)S(1)}, u32[]{:S(2)}, u32[]{:S(2)}) collective-permute-start(bf16[608,128]{1,0:T(8,128)(2,1)S(1)} %collective-permute-done.6.refs_0_), channel_id=1, source_target_pairs={{0,2},{1,3},{2,0},{3,1},{4,6},{5,7},{6,4},{7,5},{8,10},{9,11},{10,... | collective-permute-start | bytes 466952 | tf_op jit(solution)/shard_map/ppermute | solution.py:357
  17.5 0.0 collective-permute-done.3.ref
  17.5 0.0 collective-permute-start.7
  17.5 0.5 %collective-permute-start.2 = (bf16[608,128]{1,0:T(8,128)(2,1)S(1)}, bf16[608,128]{1,0:T(8,128)(2,1)S(1)}, u32[]{:S(2)}, u32[]{:S(2)}) collective-permute-start(bf16[608,128]{1,0:T(8,128)(2,1)S(1)} %collective-permute-done.1.refs_2_), channel_id=1, source_target_pairs={{0,1},{1,0},{2,3},{3,2},{4,5},{5,4},{6,7},{7,6},{8,9},{9,8},{10,11... | collective-permute-start | bytes 466952 | tf_op jit(solution)/shard_map/ppermute | solution.py:357
  18.0 1.1 %collective-permute-done.2.refs_3_ = bf16[608,128]{1,0:T(8,128)(2,1)S(1)} collective-permute-done((bf16[608,128]{1,0:T(8,128)(2,1)S(1)}, bf16[608,128]{1,0:T(8,128)(2,1)S(1)}, u32[]{:S(2)}, u32[]{:S(2)}) %collective-permute-start.2) | collective-permute-done | bytes 155680 | tf_op jit(solution)/shard_map/ppermute | solution.py:357
  19.1 1.8 %shard_map.88 = (f32[288,128]{1,0:T(8,128)S(1)}, f32[288,128]{1,0:T(8,128)S(1)}, bf16[576,128]{1,0:T(8,128)(2,1)S(1)}, f32[2304,128]{1,0:T(8,128)S(1)}) custom-call(bf16[608,128]{1,0:T(8,128)(2,1)S(1)} %get-tuple-element.29.refs_0_, bf16[608,128]{1,0:T(8,128)(2,1)S(1)} %collective-permute-done.refs_1_, bf16[608,128]{1,0:T(8,128)(2,1)S(1)} %collective-permute-done.1.refs_2_, ...), custom_call_target="tpu_custom_call" | custom-call | flops 566231040 | bytes 1179648 | tf_op jit(solution)/shard_map/pallas_call | solution.py:243
  20.9 0.3 collective-permute-done.8.refs_2_
  21.2 0.1 collective-permute-start.10
  21.2 0.4 %collective-permute-start.9 = (bf16[576,128]{1,0:T(8,128)(2,1)S(1)}, bf16[576,128]{1,0:T(8,128)(2,1)S(1)}, u32[]{:S(2)}, u32[]{:S(2)}) collective-permute-start(bf16[576,128]{1,0:T(8,128)(2,1)S(1)} %get-tuple-element.37), channel_id=1, source_target_pairs={{0,1},{1,0},{2,3},{3,2},{4,5},{5,4},{6,7},{7,6},{8,9},{9,8},{10,11... | collective-permute-start | bytes 442376 | tf_op jit(solution)/shard_map/ppermute | solution.py:357
  21.7 1.1 %collective-permute-done.9.refs_2_ = bf16[576,128]{1,0:T(8,128)(2,1)S(1)} collective-permute-done((bf16[576,128]{1,0:T(8,128)(2,1)S(1)}, bf16[576,128]{1,0:T(8,128)(2,1)S(1)}, u32[]{:S(2)}, u32[]{:S(2)}) %collective-permute-start.9) | collective-permute-done | bytes 147488 | tf_op jit(solution)/shard_map/ppermute | solution.py:357
  22.8 1.6 %collective-permute-start.14 = (bf16[288,128]{1,0:T(8,128)(2,1)S(1)}, bf16[288,128]{1,0:T(8,128)(2,1)S(1)}, u32[]{:S(2)}, u32[]{:S(2)}) collective-permute-start(bf16[288,128]{1,0:T(8,128)(2,1)S(1)} %get-tuple-element.49), channel_id=1, source_target_pairs={{0,2},{1,3},{2,0},{3,1},{4,6},{5,7},{6,4},{7,5},{8,10},{9,11},{10,... | collective-permute-start | bytes 221192 | tf_op jit(solution)/shard_map/ppermute | solution.py:357
  24.4 1.8 %shard_map.90 = (f32[288,128]{1,0:T(8,128)S(1)}, f32[288,128]{1,0:T(8,128)S(1)}, bf16[576,128]{1,0:T(8,128)(2,1)S(1)}, f32[576,128]{1,0:T(8,128)S(1)}, bf16[576,...) custom-call(bf16[608,128]{1,0:T(8,128)(2,1)S(1)} %collective-permute-done.6.refs_0_, ...), custom_call_target="tpu_custom_call" | custom-call | flops 5662310400 | bytes 1179648 | tf_op jit(solution)/shard_map/pallas_call | solution.py:243
  26.2 0.1 collective-permute-start.11
  26.3 1.1 %collective-permute-done.14.refs_2_ = bf16[288,128]{1,0:T(8,128)(2,1)S(1)} collective-permute-done((bf16[288,128]{1,0:T(8,128)(2,1)S(1)}, bf16[288,128]{1,0:T(8,128)(2,1)S(1)}, u32[]{:S(2)}, u32[]{:S(2)}) %collective-permute-start.14) | collective-permute-done | bytes 73760 | tf_op jit(solution)/shard_map/ppermute | solution.py:357
  27.3 0.6 %collective-permute-start.16 = (bf16[576,128]{1,0:T(8,128)(2,1)S(1)}, bf16[576,128]{1,0:T(8,128)(2,1)S(1)}, u32[]{:S(2)}, u32[]{:S(2)}) collective-permute-start(bf16[576,128]{1,0:T(8,128)(2,1)S(1)} %get-tuple-element.54), channel_id=1, source_target_pairs={{0,4},{4,0},{8,12},{12,8},{16,20},{20,16},{24,28},{28,24},{1,5},{5... | collective-permute-start | bytes 442376 | tf_op jit(solution)/shard_map/ppermute | solution.py:359
  27.9 0.1 collective-permute-start.12
  28.0 1.5 %collective-permute-start.15 = (bf16[576,128]{1,0:T(8,128)(2,1)S(1)}, bf16[576,128]{1,0:T(8,128)(2,1)S(1)}, u32[]{:S(2)}, u32[]{:S(2)}) collective-permute-start(bf16[576,128]{1,0:T(8,128)(2,1)S(1)} %get-tuple-element.52), channel_id=1, source_target_pairs={{0,4},{4,0},{8,12},{12,8},{16,20},{20,16},{24,28},{28,24},{1,5},{5... | collective-permute-start | bytes 442376 | tf_op jit(solution)/shard_map/ppermute | solution.py:359
  29.5 3.8 %collective-permute-start.13 = (bf16[288,128]{1,0:T(8,128)(2,1)S(1)}, bf16[288,128]{1,0:T(8,128)(2,1)S(1)}, u32[]{:S(2)}, u32[]{:S(2)}) collective-permute-start(bf16[288,128]{1,0:T(8,128)(2,1)S(1)} %get-tuple-element.47), channel_id=1, source_target_pairs={{0,18},{1,19},{2,16},{3,17},{4,22},{5,23},{6,20},{7,21},{8,26},{9,... | collective-permute-start | bytes 221192 | tf_op jit(solution)/shard_map/ppermute | solution.py:365
  33.3 0.8 %collective-permute-done.16.refs_1_ = bf16[576,128]{1,0:T(8,128)(2,1)S(1)} collective-permute-done((bf16[576,128]{1,0:T(8,128)(2,1)S(1)}, bf16[576,128]{1,0:T(8,128)(2,1)S(1)}, u32[]{:S(2)}, u32[]{:S(2)}) %collective-permute-start.16) | collective-permute-done | bytes 147488 | tf_op jit(solution)/shard_map/ppermute | solution.py:359
  34.1 0.1 collective-permute-start.17
  34.2 0.3 collective-permute-done.12.refs_1_
  34.5 1.2 %collective-permute-done.15.refs_4_ = bf16[576,128]{1,0:T(8,128)(2,1)S(1)} collective-permute-done((bf16[576,128]{1,0:T(8,128)(2,1)S(1)}, bf16[576,128]{1,0:T(8,128)(2,1)S(1)}, u32[]{:S(2)}, u32[]{:S(2)}) %collective-permute-start.15) | collective-permute-done | bytes 147488 | tf_op jit(solution)/shard_map/ppermute | solution.py:359
  35.7 1.4 %collective-permute-done.13.refs_1_ = bf16[288,128]{1,0:T(8,128)(2,1)S(1)} collective-permute-done((bf16[288,128]{1,0:T(8,128)(2,1)S(1)}, bf16[288,128]{1,0:T(8,128)(2,1)S(1)}, u32[]{:S(2)}, u32[]{:S(2)}) %collective-permute-start.13) | collective-permute-done | bytes 73760 | tf_op jit(solution)/shard_map/ppermute | solution.py:365
  37.1 2.2 %collective-permute-done.17.refs_5_ = bf16[576,128]{1,0:T(8,128)(2,1)S(1)} collective-permute-done((bf16[576,128]{1,0:T(8,128)(2,1)S(1)}, bf16[576,128]{1,0:T(8,128)(2,1)S(1)}, u32[]{:S(2)}, u32[]{:S(2)}) %collective-permute-start.17) | collective-permute-done | bytes 147488 | tf_op jit(solution)/shard_map/ppermute | solution.py:359
  39.4 0.7 %shard_map.94 = (bf16[48,768]{1,0:T(8,128)(2,1)}, bf16[48,768]{1,0:T(8,128)(2,1)}, bf16[48,768]{1,0:T(8,128)(2,1)}) custom-call(f32[288,128]{1,0:T(8,128)S(1)} %shard_map.92.refs_0_, bf16[288,128]{1,0:T(8,128)(2,1)S(1)} %collective-permute-done.13.refs_1_, bf16[288,128]{1,0:T(8,128)(2,1)S(1)} %collective-permute-done.14.refs_2_, ...), custom_call_target="tpu_custom_call" | custom-call | tf_op jit(solution)/shard_map/pallas_call | solution.py:330
  (14 shorter events, 0.1 us)
Async XLA Ops:
  1.9 8.7 %collective-permute-start.4 = (bf16[576,128]{1,0:T(8,128)(2,1)S(1)}, bf16[576,128]{1,0:T(8,128)(2,1)S(1)}, u32[]{:S(2)}, u32[]{:S(2)}) collective-permute-start(bf16[576,128]{1,0:T(8,128)(2,1)S(1)} %get-tuple-element.30.refs_4_), channel_id=1, source_target_pairs={{0,8},{4,12},{8,0},{12,4},{16,24},{20,28},{24,16},{28,20},{1,9},{5... | collective-permute-start | bytes 442376 | tf_op jit(solution)/shard_map/ppermute | solution.py:359
  5.0 12.5 %collective-permute-start.3 = (bf16[576,128]{1,0:T(8,128)(2,1)S(1)}, bf16[576,128]{1,0:T(8,128)(2,1)S(1)}, u32[]{:S(2)}, u32[]{:S(2)}) collective-permute-start(bf16[576,128]{1,0:T(8,128)(2,1)S(1)} %get-tuple-element.30.refs_4_), channel_id=1, source_target_pairs={{0,4},{4,0},{8,12},{12,8},{16,20},{20,16},{24,28},{28,24},{1,5},{5... | collective-permute-start | bytes 442376 | tf_op jit(solution)/shard_map/ppermute | solution.py:359
  6.5 9.4 %collective-permute-start.6 = (bf16[608,128]{1,0:T(8,128)(2,1)S(1)}, bf16[608,128]{1,0:T(8,128)(2,1)S(1)}, u32[]{:S(2)}, u32[]{:S(2)}) collective-permute-start(bf16[608,128]{1,0:T(8,128)(2,1)S(1)} %get-tuple-element.29.refs_0_), channel_id=1, source_target_pairs={{0,16},{4,20},{8,24},{12,28},{16,0},{20,4},{24,8},{28,12},{1,17},{... | collective-permute-start | bytes 466952 | tf_op jit(solution)/shard_map/ppermute | solution.py:359
  9.1 8.4 %collective-permute-start.1 = (bf16[608,128]{1,0:T(8,128)(2,1)S(1)}, bf16[608,128]{1,0:T(8,128)(2,1)S(1)}, u32[]{:S(2)}, u32[]{:S(2)}) collective-permute-start(bf16[608,128]{1,0:T(8,128)(2,1)S(1)} %get-tuple-element.29.refs_0_), channel_id=1, source_target_pairs={{0,2},{1,3},{2,0},{3,1},{4,6},{5,7},{6,4},{7,5},{8,10},{9,11},{10,... | collective-permute-start | bytes 466952 | tf_op jit(solution)/shard_map/ppermute | solution.py:357
  10.6 7.4 %collective-permute-start = (bf16[608,128]{1,0:T(8,128)(2,1)S(1)}, bf16[608,128]{1,0:T(8,128)(2,1)S(1)}, u32[]{:S(2)}, u32[]{:S(2)}) collective-permute-start(bf16[608,128]{1,0:T(8,128)(2,1)S(1)} %get-tuple-element.29.refs_0_), channel_id=1, source_target_pairs={{0,1},{1,0},{2,3},{3,2},{4,5},{5,4},{6,7},{7,6},{8,9},{9,8},{10,11... | collective-permute-start | bytes 466952 | tf_op jit(solution)/shard_map/ppermute | solution.py:357
  10.6 7.4 %collective-permute-start.5 = (bf16[576,128]{1,0:T(8,128)(2,1)S(1)}, bf16[576,128]{1,0:T(8,128)(2,1)S(1)}, u32[]{:S(2)}, u32[]{:S(2)}) collective-permute-start(bf16[576,128]{1,0:T(8,128)(2,1)S(1)} %shard_map.87.refs_6_), channel_id=1, source_target_pairs={{0,4},{4,0},{8,12},{12,8},{16,20},{20,16},{24,28},{28,24},{1,5},{5... | collective-permute-start | bytes 442376 | tf_op jit(solution)/shard_map/ppermute | solution.py:359
  15.9 5.2 %collective-permute-start.8 = (bf16[608,128]{1,0:T(8,128)(2,1)S(1)}, bf16[608,128]{1,0:T(8,128)(2,1)S(1)}, u32[]{:S(2)}, u32[]{:S(2)}) collective-permute-start(bf16[608,128]{1,0:T(8,128)(2,1)S(1)} %collective-permute-done.6.refs_0_), channel_id=1, source_target_pairs={{0,2},{1,3},{2,0},{3,1},{4,6},{5,7},{6,4},{7,5},{8,10},{9,11},{10,... | collective-permute-start | bytes 466952 | tf_op jit(solution)/shard_map/ppermute | solution.py:357
  17.5 3.7 %collective-permute-start.7 = (bf16[608,128]{1,0:T(8,128)(2,1)S(1)}, bf16[608,128]{1,0:T(8,128)(2,1)S(1)}, u32[]{:S(2)}, u32[]{:S(2)}) collective-permute-start(bf16[608,128]{1,0:T(8,128)(2,1)S(1)} %collective-permute-done.6.refs_0_), channel_id=1, source_target_pairs={{0,1},{1,0},{2,3},{3,2},{4,5},{5,4},{6,7},{7,6},{8,9},{9,8},{10,11... | collective-permute-start | bytes 466952 | tf_op jit(solution)/shard_map/ppermute | solution.py:357
  17.5 1.6 %collective-permute-start.2 = (bf16[608,128]{1,0:T(8,128)(2,1)S(1)}, bf16[608,128]{1,0:T(8,128)(2,1)S(1)}, u32[]{:S(2)}, u32[]{:S(2)}) collective-permute-start(bf16[608,128]{1,0:T(8,128)(2,1)S(1)} %collective-permute-done.1.refs_2_), channel_id=1, source_target_pairs={{0,1},{1,0},{2,3},{3,2},{4,5},{5,4},{6,7},{7,6},{8,9},{9,8},{10,11... | collective-permute-start | bytes 466952 | tf_op jit(solution)/shard_map/ppermute | solution.py:357
  21.2 3.2 %collective-permute-start.10 = (bf16[608,128]{1,0:T(8,128)(2,1)S(1)}, bf16[608,128]{1,0:T(8,128)(2,1)S(1)}, u32[]{:S(2)}, u32[]{:S(2)}) collective-permute-start(bf16[608,128]{1,0:T(8,128)(2,1)S(1)} %collective-permute-done.8.refs_2_), channel_id=1, source_target_pairs={{0,1},{1,0},{2,3},{3,2},{4,5},{5,4},{6,7},{7,6},{8,9},{9,8},{10,11... | collective-permute-start | bytes 466952 | tf_op jit(solution)/shard_map/ppermute | solution.py:357
  21.2 1.5 %collective-permute-start.9 = (bf16[576,128]{1,0:T(8,128)(2,1)S(1)}, bf16[576,128]{1,0:T(8,128)(2,1)S(1)}, u32[]{:S(2)}, u32[]{:S(2)}) collective-permute-start(bf16[576,128]{1,0:T(8,128)(2,1)S(1)} %get-tuple-element.37), channel_id=1, source_target_pairs={{0,1},{1,0},{2,3},{3,2},{4,5},{5,4},{6,7},{7,6},{8,9},{9,8},{10,11... | collective-permute-start | bytes 442376 | tf_op jit(solution)/shard_map/ppermute | solution.py:357
  22.8 4.5 %collective-permute-start.14 = (bf16[288,128]{1,0:T(8,128)(2,1)S(1)}, bf16[288,128]{1,0:T(8,128)(2,1)S(1)}, u32[]{:S(2)}, u32[]{:S(2)}) collective-permute-start(bf16[288,128]{1,0:T(8,128)(2,1)S(1)} %get-tuple-element.49), channel_id=1, source_target_pairs={{0,2},{1,3},{2,0},{3,1},{4,6},{5,7},{6,4},{7,5},{8,10},{9,11},{10,... | collective-permute-start | bytes 221192 | tf_op jit(solution)/shard_map/ppermute | solution.py:357
  26.2 1.7 %collective-permute-start.11 = (bf16[576,128]{1,0:T(8,128)(2,1)S(1)}, bf16[576,128]{1,0:T(8,128)(2,1)S(1)}, u32[]{:S(2)}, u32[]{:S(2)}) collective-permute-start(bf16[576,128]{1,0:T(8,128)(2,1)S(1)} %get-tuple-element.45), channel_id=1, source_target_pairs={{0,1},{1,0},{2,3},{3,2},{4,5},{5,4},{6,7},{7,6},{8,9},{9,8},{10,11... | collective-permute-start | bytes 442376 | tf_op jit(solution)/shard_map/ppermute | solution.py:357
  27.3 6.8 %collective-permute-start.16 = (bf16[576,128]{1,0:T(8,128)(2,1)S(1)}, bf16[576,128]{1,0:T(8,128)(2,1)S(1)}, u32[]{:S(2)}, u32[]{:S(2)}) collective-permute-start(bf16[576,128]{1,0:T(8,128)(2,1)S(1)} %get-tuple-element.54), channel_id=1, source_target_pairs={{0,4},{4,0},{8,12},{12,8},{16,20},{20,16},{24,28},{28,24},{1,5},{5... | collective-permute-start | bytes 442376 | tf_op jit(solution)/shard_map/ppermute | solution.py:359
  27.9 6.6 %collective-permute-start.12 = (bf16[288,128]{1,0:T(8,128)(2,1)S(1)}, bf16[288,128]{1,0:T(8,128)(2,1)S(1)}, u32[]{:S(2)}, u32[]{:S(2)}) collective-permute-start(bf16[288,128]{1,0:T(8,128)(2,1)S(1)} %get-tuple-element.46), channel_id=1, source_target_pairs={{0,16},{4,20},{8,24},{12,28},{16,0},{20,4},{24,8},{28,12},{1,17},{... | collective-permute-start | bytes 221192 | tf_op jit(solution)/shard_map/ppermute | solution.py:359
  28.0 7.7 %collective-permute-start.15 = (bf16[576,128]{1,0:T(8,128)(2,1)S(1)}, bf16[576,128]{1,0:T(8,128)(2,1)S(1)}, u32[]{:S(2)}, u32[]{:S(2)}) collective-permute-start(bf16[576,128]{1,0:T(8,128)(2,1)S(1)} %get-tuple-element.52), channel_id=1, source_target_pairs={{0,4},{4,0},{8,12},{12,8},{16,20},{20,16},{24,28},{28,24},{1,5},{5... | collective-permute-start | bytes 442376 | tf_op jit(solution)/shard_map/ppermute | solution.py:359
  29.5 7.6 %collective-permute-start.13 = (bf16[288,128]{1,0:T(8,128)(2,1)S(1)}, bf16[288,128]{1,0:T(8,128)(2,1)S(1)}, u32[]{:S(2)}, u32[]{:S(2)}) collective-permute-start(bf16[288,128]{1,0:T(8,128)(2,1)S(1)} %get-tuple-element.47), channel_id=1, source_target_pairs={{0,18},{1,19},{2,16},{3,17},{4,22},{5,23},{6,20},{7,21},{8,26},{9,... | collective-permute-start | bytes 221192 | tf_op jit(solution)/shard_map/ppermute | solution.py:365
  34.1 5.2 %collective-permute-start.17 = (bf16[576,128]{1,0:T(8,128)(2,1)S(1)}, bf16[576,128]{1,0:T(8,128)(2,1)S(1)}, u32[]{:S(2)}, u32[]{:S(2)}) collective-permute-start(bf16[576,128]{1,0:T(8,128)(2,1)S(1)} %shard_map.93), channel_id=1, source_target_pairs={{0,8},{4,12},{8,0},{12,4},{16,24},{20,28},{24,16},{28,20},{1,9},{5... | collective-permute-start | bytes 442376 | tf_op jit(solution)/shard_map/ppermute | solution.py:359
